TPU v7x, 32 devices: a whole 2x2x4 slice. The times are simulated.
32 devices in a mesh: ctx: 8 (over z, y), wt: 4 (over x, core).
Axes of the slice: x: 2, y: 2, z: 4, core: 2. Of those that a mesh axis runs over, the one named last changes fastest.
Arguments:
- tokens: bfloat16 [4, 1024, 1600], P('wt', 'ctx'), may hold values from -6 to 6
- slots: int32 [16], replicated, may hold values from 0 to 15, as said below
- norm_gains: bfloat16 [2, 1600], P(None, 'wt'), may hold values from 0.25 to 1.75
- norm_shifts: bfloat16 [2, 1600], P(None, 'wt'), may hold values from -2 to 2
- qkv_weight: bfloat16 [1600, 4800], P('wt'), may hold values from -0.21875 to 0.21875
- qv_bias: bfloat16 [2, 1600], P(None, 'wt'), may hold values from -3 to 3
- proj_weight: bfloat16 [1600, 1600], P('wt'), may hold values from -0.625 to 0.625
- proj_bias: bfloat16 [1600], P('wt'), may hold values from -2 to 2
- up_weight: bfloat16 [1600, 6400], P('wt'), may hold values from -0.15625 to 0.15625
- up_bias: bfloat16 [6400], P('wt'), may hold values from -2 to 2
- down_weight: bfloat16 [6400, 1600], P('wt'), may hold values from -0.15625 to 0.15625
- down_bias: bfloat16 [1600], P('wt'), may hold values from -2 to 2
- cotangent: bfloat16 [4, 1024, 1600], P('wt', 'ctx'), may hold values from -6 to 6
Outputs:
- output: bfloat16 [4, 1024, 1600], P('wt', 'ctx')
- d_tokens: bfloat16 [4, 1024, 1600], P('wt', 'ctx')
- d_norm_gains: float32 [2, 1600], P(None, 'wt')
- d_norm_shifts: float32 [2, 1600], P(None, 'wt')
- d_qkv_weight: float32 [1600, 4800], P('wt')
- d_qv_bias: float32 [2, 1600], P(None, 'wt')
- d_proj_weight: float32 [1600, 1600], P('wt')
- d_proj_bias: float32 [1600], P('wt')
- d_up_weight: float32 [1600, 6400], P('wt')
- d_up_bias: float32 [6400], P('wt')
- d_down_weight: float32 [6400, 1600], P('wt')
- d_down_bias: float32 [1600], P('wt')
Inputs may be any that keep to these rules, and one draw needn't show every extreme that they name: `slots`: a permutation of the blocks; row blocks 2c and 2c+1 hold blocks b and 15 - b for some b.
All inputs are finite; a program needn't handle non-finite values.
Results may differ from a plain program's by a relative error of at most 0.02.
Values may be sent and summed in bfloat16 or wider, within the bound.
No kernel may reach another device: no remote copies, remote signals or barrier semaphores. Data moves between devices by JAX's collectives and lax.ppermute only.
A program may use at most 384 MiB of HBM per device.

v0:
```python
import math

import jax
import jax.numpy as jnp
from jax import lax
from jax.sharding import PartitionSpec as P

HEADS = 25


def standardize(values):
    centred = values - jnp.mean(values, axis=-1, keepdims=True)
    scale = lax.rsqrt(jnp.mean(centred * centred, axis=-1, keepdims=True) + 1e-05)
    return (centred * scale, scale)


def finish_norm(scaled, normed, scale):
    inner = (
        scaled
        - jnp.mean(scaled, axis=-1, keepdims=True)
        - normed * jnp.mean(scaled * normed, axis=-1, keepdims=True)
    )
    return scale * inner


def gelu(values):
    return (
        0.5
        * values
        * (1.0 + jnp.tanh(0.7978845608028654 * (values + 0.044715 * values * values * values)))
    )


def over_rows(left, right):
    return lax.dot_general(
        left, right, (((0,), (0,)), ((), ())), preferred_element_type=jnp.float32
    )


def by_transpose(left, right):
    return lax.dot_general(
        left, right, (((1,), (1,)), ((), ())), preferred_element_type=jnp.float32
    )


def positions_of(slots, first, count, block):
    rows = first + jnp.arange(count, dtype=jnp.int32)
    owner = rows // block
    table = jnp.arange(slots.shape[0], dtype=jnp.int32)
    picked = jnp.sum(jnp.where(owner[:, None] == table[None, :], slots[None, :], 0), axis=1)
    return picked * block + rows % block


def attend_block(carry, keys, values, start, queries, query_pos, slots, block):
    most, total, acc = carry
    seqs, count = (keys.shape[0], keys.shape[1])
    heads, size = (queries.shape[2], queries.shape[3])
    kblock = keys.reshape(seqs, count, heads, size)
    vblock = values.reshape(seqs, count, heads, size)
    scores = (
        jnp.einsum("srhd,sphd->shrp", queries, kblock, preferred_element_type=jnp.float32) * 0.125
    )
    allowed = positions_of(slots, start, count, block)[None, :] <= query_pos[:, None]
    scores = jnp.where(allowed, scores, -1e30)
    newmost = jnp.maximum(most, jnp.max(scores, axis=-1))
    fade = jnp.exp(most - newmost)
    weights = jnp.where(allowed, jnp.exp(scores - newmost[..., None]), 0.0)
    total = total * fade + jnp.sum(weights, axis=-1)
    acc = acc * jnp.transpose(fade, (0, 2, 1))[..., None] + jnp.einsum(
        "shrp,sphd->srhd", weights.astype(jnp.bfloat16), vblock, preferred_element_type=jnp.float32
    )
    return (newmost, total, acc)


def query_side(q4, grad4, lse, delta, keys_all, values_all, query_pos, slots, block):
    seqs, rows, heads, size = q4.shape
    length = keys_all.shape[1]
    step = math.gcd(length, 512)

    def query_turn(index, carry):
        offset = index * step
        kblock = lax.dynamic_slice_in_dim(keys_all, offset, step, 1).reshape(
            seqs, step, heads, size
        )
        vblock = lax.dynamic_slice_in_dim(values_all, offset, step, 1).reshape(
            seqs, step, heads, size
        )
        scores = (
            jnp.einsum("srhd,sphd->shrp", q4, kblock, preferred_element_type=jnp.float32) * 0.125
        )
        allowed = positions_of(slots, offset, step, block)[None, :] <= query_pos[:, None]
        probs = jnp.where(allowed, jnp.exp(scores - lse[..., None]), 0.0)
        dprobs = jnp.einsum("srhd,sphd->shrp", grad4, vblock, preferred_element_type=jnp.float32)
        dscores = (probs * (dprobs - delta[..., None])).astype(jnp.bfloat16)
        dquery = carry[0] + jnp.einsum(
            "shrp,sphd->srhd", dscores, kblock, preferred_element_type=jnp.float32
        )
        vpiece = jnp.einsum(
            "shrp,srhd->sphd", probs.astype(jnp.bfloat16), grad4, preferred_element_type=jnp.float32
        )
        kpiece = (
            jnp.einsum("shrp,srhd->sphd", dscores, q4, preferred_element_type=jnp.float32) * 0.125
        )
        return (
            dquery,
            lax.dynamic_update_slice_in_dim(carry[1], kpiece, offset, 1),
            lax.dynamic_update_slice_in_dim(carry[2], vpiece, offset, 1),
        )

    start = (jnp.zeros((seqs, rows, heads, size), jnp.float32),)
    start = start + (
        jnp.zeros((seqs, length, heads, size), jnp.float32),
        jnp.zeros((seqs, length, heads, size), jnp.float32),
    )
    return lax.fori_loop(0, length // step, query_turn, start)


def on_device(
    tokens,
    slots,
    norm_gains,
    norm_shifts,
    qkv_weight,
    qv_bias,
    proj_weight,
    proj_bias,
    up_weight,
    up_bias,
    down_weight,
    down_bias,
    cotangent,
):
    seqs, rows, width = tokens.shape
    heads = HEADS
    size = width // heads
    block = rows // 2
    count = seqs * rows
    query_pos = positions_of(slots, lax.axis_index("ctx") * rows, rows, block)
    flat = tokens.reshape(count, width).astype(jnp.float32)
    normed1, scale1 = standardize(flat)
    gains, shifts, wqkv, qvb, wproj, bproj = (
        lax.all_gather(norm_gains, "wt", axis=1, tiled=True),
        lax.all_gather(norm_shifts, "wt", axis=1, tiled=True),
        lax.all_gather(qkv_weight, "wt", axis=0, tiled=True),
        lax.all_gather(qv_bias, "wt", axis=1, tiled=True),
        lax.all_gather(proj_weight, "wt", axis=0, tiled=True),
        lax.all_gather(proj_bias, "wt", axis=0, tiled=True),
    )
    gains32 = gains.astype(jnp.float32)
    shifts32 = shifts.astype(jnp.float32)
    qvb32 = qvb.astype(jnp.float32)
    a1 = (normed1 * gains32[0] + shifts32[0]).astype(jnp.bfloat16)
    qkv_full = jnp.dot(a1, wqkv, preferred_element_type=jnp.float32) + jnp.concatenate(
        [qvb32[0], jnp.zeros((width,), jnp.float32), qvb32[1]]
    )
    query = qkv_full[:, :width].astype(jnp.bfloat16).reshape(seqs, rows, width)
    keys = qkv_full[:, width : 2 * width].astype(jnp.bfloat16).reshape(seqs, rows, width)
    values = qkv_full[:, 2 * width :].astype(jnp.bfloat16).reshape(seqs, rows, width)
    q4 = query.reshape(seqs, rows, heads, size)
    init = (
        jnp.full((seqs, heads, rows), -1e30, jnp.float32),
        jnp.zeros((seqs, heads, rows), jnp.float32),
        jnp.zeros((seqs, rows, heads, size), jnp.float32),
    )
    pieces = (
        lax.all_gather(keys, "ctx", axis=1, tiled=True),
        lax.all_gather(values, "ctx", axis=1, tiled=True),
    )
    length = pieces[0].shape[1]
    step = math.gcd(length, 512)

    def fold_turn(index, inner):
        kpiece = lax.dynamic_slice_in_dim(pieces[0], index * step, step, 1)
        vpiece = lax.dynamic_slice_in_dim(pieces[1], index * step, step, 1)
        return attend_block(inner, kpiece, vpiece, index * step, q4, query_pos, slots, block)

    most, total, acc = lax.fori_loop(0, length // step, fold_turn, init)
    attn_full = acc / jnp.transpose(total, (0, 2, 1))[..., None]
    lse = most + jnp.log(total)
    attended = attn_full.reshape(count, width).astype(jnp.bfloat16)
    mid = (
        flat
        + jnp.dot(attended, wproj, preferred_element_type=jnp.float32)
        + bproj.astype(jnp.float32)
    )
    normed2, scale2 = standardize(mid)
    wup, bup, wdown, bdown = (
        lax.all_gather(up_weight, "wt", axis=0, tiled=True),
        lax.all_gather(up_bias, "wt", axis=0, tiled=True),
        lax.all_gather(down_weight, "wt", axis=0, tiled=True),
        lax.all_gather(down_bias, "wt", axis=0, tiled=True),
    )
    a2 = (normed2 * gains32[1] + shifts32[1]).astype(jnp.bfloat16)
    pre = jnp.dot(a2, wup, preferred_element_type=jnp.float32) + bup.astype(jnp.float32)
    activated, gelu_pull = jax.vjp(gelu, pre)
    hidden = activated.astype(jnp.bfloat16)
    branch_out = jnp.dot(hidden, wdown, preferred_element_type=jnp.float32) + bdown.astype(
        jnp.float32
    )
    output = mid + branch_out
    grad_out = cotangent.reshape(count, width)
    grad_out32 = grad_out.astype(jnp.float32)
    d_down_w = over_rows(hidden, grad_out)
    d_down_b = jnp.sum(grad_out32, axis=0)
    grad_pre = gelu_pull(by_transpose(grad_out, wdown))[0].astype(jnp.bfloat16)
    d_up_w = over_rows(a2, grad_pre)
    d_up_b = jnp.sum(grad_pre.astype(jnp.float32), axis=0)
    grad_a2 = by_transpose(grad_pre, wup)
    d_gain2 = jnp.sum(grad_a2 * normed2, axis=0)
    d_shift2 = jnp.sum(grad_a2, axis=0)
    grad_mid = grad_out32 + finish_norm(grad_a2 * gains32[1], normed2, scale2)
    d_up_weight, d_up_bias, d_down_weight, d_down_bias = (
        lax.psum_scatter(d_up_w.astype(jnp.bfloat16), "wt", scatter_dimension=0, tiled=True).astype(
            jnp.float32
        ),
        lax.psum_scatter(d_up_b.astype(jnp.bfloat16), "wt", scatter_dimension=0, tiled=True).astype(
            jnp.float32
        ),
        lax.psum_scatter(
            d_down_w.astype(jnp.bfloat16), "wt", scatter_dimension=0, tiled=True
        ).astype(jnp.float32),
        lax.psum_scatter(
            d_down_b.astype(jnp.bfloat16), "wt", scatter_dimension=0, tiled=True
        ).astype(jnp.float32),
    )
    grad_proj = grad_mid.astype(jnp.bfloat16)
    d_proj_w = over_rows(attended, grad_proj)
    d_proj_b = jnp.sum(grad_proj.astype(jnp.float32), axis=0)
    grad_attn = by_transpose(grad_proj, wproj).astype(jnp.bfloat16)
    grad4 = grad_attn.reshape(seqs, rows, heads, size)
    delta = jnp.einsum("srhd,srhd->shr", grad4.astype(jnp.float32), attn_full)
    keys_all, values_all = (
        lax.all_gather(keys, "ctx", axis=1, tiled=True),
        lax.all_gather(values, "ctx", axis=1, tiled=True),
    )
    dquery, dkeys_all, dvalues_all = query_side(
        q4, grad4, lse, delta, keys_all, values_all, query_pos, slots, block
    )
    dkeys, dvalues = (
        lax.psum_scatter(
            dkeys_all.reshape(seqs, -1, width).astype(jnp.bfloat16),
            "ctx",
            scatter_dimension=1,
            tiled=True,
        ).astype(jnp.float32),
        lax.psum_scatter(
            dvalues_all.reshape(seqs, -1, width).astype(jnp.bfloat16),
            "ctx",
            scatter_dimension=1,
            tiled=True,
        ).astype(jnp.float32),
    )
    grad_qkv = jnp.concatenate(
        [
            (dquery * 0.125).reshape(count, width),
            dkeys.reshape(count, width),
            dvalues.reshape(count, width),
        ],
        axis=1,
    ).astype(jnp.bfloat16)
    d_qkv_whole = over_rows(a1, grad_qkv)
    column_sums = jnp.sum(grad_qkv.astype(jnp.float32), axis=0)
    d_qv_whole = jnp.stack([column_sums[:width], column_sums[2 * width :]])
    grad_a1 = by_transpose(grad_qkv, wqkv)
    d_gain1 = jnp.sum(grad_a1 * normed1, axis=0)
    d_shift1 = jnp.sum(grad_a1, axis=0)
    grad_norm1 = finish_norm(grad_a1 * gains32[0], normed1, scale1)
    d_gains_part, d_shifts_part, d_qkv_w, d_qv_b, d_proj_w, d_proj_b = (
        lax.psum_scatter(
            jnp.stack([d_gain1, d_gain2]).astype(jnp.bfloat16),
            "wt",
            scatter_dimension=1,
            tiled=True,
        ).astype(jnp.float32),
        lax.psum_scatter(
            jnp.stack([d_shift1, d_shift2]).astype(jnp.bfloat16),
            "wt",
            scatter_dimension=1,
            tiled=True,
        ).astype(jnp.float32),
        lax.psum_scatter(
            d_qkv_whole.astype(jnp.bfloat16), "wt", scatter_dimension=0, tiled=True
        ).astype(jnp.float32),
        lax.psum_scatter(
            d_qv_whole.astype(jnp.bfloat16), "wt", scatter_dimension=1, tiled=True
        ).astype(jnp.float32),
        lax.psum_scatter(
            d_proj_w.astype(jnp.bfloat16), "wt", scatter_dimension=0, tiled=True
        ).astype(jnp.float32),
        lax.psum_scatter(
            d_proj_b.astype(jnp.bfloat16), "wt", scatter_dimension=0, tiled=True
        ).astype(jnp.float32),
    )
    d_tokens = (grad_mid + grad_norm1).astype(jnp.bfloat16).reshape(seqs, rows, width)
    (
        d_norm_gains,
        d_norm_shifts,
        d_qkv_weight,
        d_qv_bias,
        d_proj_weight,
        d_proj_bias,
        d_up_weight,
        d_up_bias,
        d_down_weight,
        d_down_bias,
    ) = (
        lax.psum(d_gains_part.astype(jnp.bfloat16), "ctx").astype(jnp.float32),
        lax.psum(d_shifts_part.astype(jnp.bfloat16), "ctx").astype(jnp.float32),
        lax.psum(d_qkv_w.astype(jnp.bfloat16), "ctx").astype(jnp.float32),
        lax.psum(d_qv_b.astype(jnp.bfloat16), "ctx").astype(jnp.float32),
        lax.psum(d_proj_w.astype(jnp.bfloat16), "ctx").astype(jnp.float32),
        lax.psum(d_proj_b.astype(jnp.bfloat16), "ctx").astype(jnp.float32),
        lax.psum(d_up_weight.astype(jnp.bfloat16), "ctx").astype(jnp.float32),
        lax.psum(d_up_bias.astype(jnp.bfloat16), "ctx").astype(jnp.float32),
        lax.psum(d_down_weight.astype(jnp.bfloat16), "ctx").astype(jnp.float32),
        lax.psum(d_down_bias.astype(jnp.bfloat16), "ctx").astype(jnp.float32),
    )
    return (
        output.astype(jnp.bfloat16).reshape(seqs, rows, width),
        d_tokens,
        d_norm_gains,
        d_norm_shifts,
        d_qkv_weight,
        d_qv_bias,
        d_proj_weight,
        d_proj_bias,
        d_up_weight,
        d_up_bias,
        d_down_weight,
        d_down_bias,
    )


def solution(mesh):
    placed = (
        P("wt", "ctx", None),
        P(),
        P(None, "wt"),
        P(None, "wt"),
        P("wt", None),
        P(None, "wt"),
        P("wt", None),
        P("wt"),
        P("wt", None),
        P("wt"),
        P("wt", None),
        P("wt"),
        P("wt", "ctx", None),
    )
    return jax.shard_map(
        on_device,
        mesh=mesh,
        in_specs=placed,
        out_specs=(
            P("wt", "ctx", None),
            P("wt", "ctx", None),
            P(None, "wt"),
            P(None, "wt"),
            P("wt", None),
            P(None, "wt"),
            P("wt", None),
            P("wt"),
            P("wt", None),
            P("wt"),
            P("wt", None),
            P("wt"),
        ),
        check_vma=False,
    )
```

profile of v0, /device:TPU:0, one launch (start us, length us, event | category | flops | bytes accessed | tf_op | source)
XLA Modules:
  0.0 1891.5 jit_solution(13507591511341450963)
XLA Ops:
  8.0 6.1 all-gather.4
  25.8 85.6 %all-gather.12.cloned.1.call-done = bf16[1600,4800]{1,0:T(8,128)(2,1)} async-done(((bf16[400,4800]{1,0:T(8,128)(2,1)}), bf16[1600,4800]{1,0:T(8,128)(2,1)}) %all-gather.12.cloned.1.call-update) | async-done | bytes 15360016 | tf_op jit(solution)/shard_map/all_gather | solution.py:144
  111.4 12.1 fusion.44
  129.7 11.1 all-reduce.9
  140.9 48.4 %all-gather.20.cloned.1.call-done = bf16[1024,1600]{0,1:T(8,128)(2,1)} async-done(((bf16[128,1600]{0,1:T(8,128)(2,1)}), bf16[1024,1600]{0,1:T(8,128)(2,1)}) %all-gather.20.cloned.1.call-update) | async-done | bytes 3276816 | tf_op jit(solution)/shard_map/all_gather | solution.py:166
  189.3 65.4 %all-gather.22.cloned.1.call-done = bf16[1024,1600]{0,1:T(8,128)(2,1)} async-done(((bf16[128,1600]{0,1:T(8,128)(2,1)}), bf16[1024,1600]{0,1:T(8,128)(2,1)}) %all-gather.22.cloned.1.call-update) | async-done | bytes 3276816 | tf_op jit(solution)/shard_map/all_gather | solution.py:167
  254.7 31.1 %while.40 = (s32[]{:T(128)}, f32[1,25,128]{2,1,0:T(8,128)S(1)}, f32[1,25,128]{2,1,0:T(8,128)S(1)}, f32[1,128,25,64]{1,3,2,0:T(8,128)}, s32[16]{0:T(128)S(1)}, /*...) while((s32[]{:T(128)}, f32[1,25,128]{2,1,0:T(8,128)S(1)}, ...), condition=%wide.region_7.8_spmd.clone, body=%wide.region_3.7_spmd.clone.sunk | while | flops 441468160 | bytes 58233636 | solution.py:177
  287.0 8.2 all-gather.14.cloned.1.call-done
  300.2 125.3 %all-gather.16.cloned.1.call-done = bf16[1600,6400]{1,0:T(8,128)(2,1)} async-done(((bf16[400,6400]{1,0:T(8,128)(2,1)}), bf16[1600,6400]{1,0:T(8,128)(2,1)}) %all-gather.16.cloned.1.call-update) | async-done | bytes 20480016 | tf_op jit(solution)/shard_map/all_gather | solution.py:188
  425.5 12.2 convolution_add_fusion
  437.8 122.6 %all-gather.18.cloned.1.call-done = bf16[6400,1600]{1,0:T(8,128)(2,1)} async-done(((bf16[1600,1600]{1,0:T(8,128)(2,1)}), bf16[6400,1600]{1,0:T(8,128)(2,1)}) %all-gather.18.cloned.1.call-update) | async-done | bytes 20480016 | tf_op jit(solution)/shard_map/all_gather | solution.py:190
  560.4 12.6 fusion.90
  573.0 12.1 multiply_reduce_fusion
  595.2 37.7 %while.41 = (s32[]{:T(128)}, f32[1,128,25,64]{1,3,2,0:T(8,128)}, bf16[1,1024,25,64]{1,3,2,0:T(8,128)(2,1)}, bf16[1,1024,25,64]{1,3,2,0:T(8,128)(2,1)}, bf16[1,10...) while((s32[]{:T(128)}, f32[1,128,25,64]{1,3,2,0:T(8,128)}, ...), condition=%wide.region_14.15_spmd.clone, body=%wide.region_12.14_spmd.clone.sunk | while | flops 1066293760 | bytes 146065904 | solution.py:115
  632.8 16.0 copy.70
  654.1 16.0 copy.68
  681.9 49.7 %reduce-scatter.30.cloned.1.call-done = bf16[128,1600]{1,0:T(8,128)(2,1)} async-done(((bf16[1024,1600]{1,0:T(8,128)(2,1)}), bf16[128,1600]{1,0:T(8,128)(2,1)}) %reduce-scatter.30.cloned.1.call-update) | async-done | bytes 409616
  736.7 76.3 %reduce-scatter.28.cloned.1.call-done = bf16[128,1600]{1,0:T(8,128)(2,1)} async-done(((bf16[1024,1600]{1,0:T(8,128)(2,1)}), bf16[128,1600]{1,0:T(8,128)(2,1)}) %reduce-scatter.28.cloned.1.call-update) | async-done | bytes 409616
  818.0 9.5 convolution_convert_fusion.2
  827.6 12.1 convolution_convert_fusion.1
  839.7 11.7 convolution_convert_fusion
  851.8 10.7 fusion.69
  867.5 121.5 %reduce-scatter.20.cloned.1.call-done = bf16[400,4800]{1,0:T(8,128)(2,1)} async-done(((bf16[1600,4800]{1,0:T(8,128)(2,1)}), bf16[400,4800]{1,0:T(8,128)(2,1)}) %reduce-scatter.20.cloned.1.call-update) | async-done | bytes 3840016 | tf_op jit(solution)/shard_map/reduce_scatter | solution.py:281
  989.0 160.0 %reduce-scatter.24.cloned.1.call-done = bf16[400,6400]{1,0:T(8,128)(2,1)} async-done(((bf16[1600,6400]{1,0:T(8,128)(2,1)}), bf16[400,6400]{1,0:T(8,128)(2,1)}) %reduce-scatter.24.cloned.1.call-update) | async-done | bytes 5120016 | tf_op jit(solution)/shard_map/reduce_scatter | solution.py:213
  1149.0 157.8 %reduce-scatter.26.cloned.1.call-done = bf16[1600,1600]{1,0:T(8,128)(2,1)} async-done(((bf16[6400,1600]{1,0:T(8,128)(2,1)}), bf16[1600,1600]{1,0:T(8,128)(2,1)}) %reduce-scatter.26.cloned.1.call-update) | async-done | bytes 5120016 | tf_op jit(solution)/shard_map/reduce_scatter | solution.py:219
  1309.5 10.3 all-reduce.8
  1320.1 14.8 fusion.54
  1336.9 18.0 reduce-scatter.34.cloned.1.call-done
  1355.9 22.4 %reduce-scatter.36.cloned.1.call-done = bf16[400,2]{1,0:T(8,128)(2,1)} async-done(((bf16[1600,2]{1,0:T(8,128)(2,1)}), bf16[400,2]{1,0:T(8,128)(2,1)}) %reduce-scatter.36.cloned.1.call-update) | async-done | bytes 1616
  1379.4 39.0 %all-reduce.6 = (bf16[2,400]{1,0:T(2,128)(2,1)S(1)}, bf16[2,400]{1,0:T(2,128)(2,1)S(1)}, bf16[2,400]{1,0:T(2,128)(2,1)S(1)}, bf16[400]{0:T(512)(128)(2,1)S(1)}, ...) all-reduce(bf16[2,400]{1,0:T(2,128)(2,1)S(1)} %copy.73, ...), channel_id=1, replica_groups=mesh['ctx'=8,'wt'=4] {'ctx'}, use_global_device_ids=true, to_apply=%region_22.23 | all-reduce | flops 4800 | bytes 19200 | tf_op jit(solution)/shard_map/psum | solution.py:307
  1421.9 445.4 %all-reduce.12.cloned.1.call-done = (bf16[400,4800]{1,0:T(8,128)(2,1)}, bf16[400,1600]{1,0:T(8,128)(2,1)}, bf16[400,6400]{1,0:T(8,128)(2,1)}, bf16[1600,1600]{1,0:T(8,128)(2,1)}) async-done(((bf16[400,4800]{1,0:T(8,128)(2,1)}, bf16[400,1600]{1,0:T(8,128)(2,1)}, bf16[400,6400]{1,0:T(8,128)(2,1)}, bf16[1600,1600]{1,0:T(8,128)(2,1)}), (bf16[400,4800]{1,0:T(8,128)(2,1)}, bf16[400,1600]{1,0:T(8,128)(2,1)}, ...) | async-done | bytes 15360016 | tf_op jit(solution)/shard_map/psum | solution.py:309
  1867.3 6.0 convert_element_type.224
  (266 shorter events, 154.5 us)
Async XLA Ops:
  7.2 12.5 copy-start.34
  7.2 18.1 copy-start.5
  7.2 104.2 %all-gather.12.cloned.1.call-start = ((), (), s32[]{:S(2)}) async-start(), calls=%async_computation.9 | async-start | bytes 19456000 | tf_op jit(solution)/shard_map/all_gather | solution.py:144
  8.0 181.3 %all-gather.20.cloned.1.call-start = ((), (), s32[]{:S(2)}) async-start(), calls=%async_computation.17 | async-start | bytes 3686400 | tf_op jit(solution)/shard_map/all_gather | solution.py:166
  25.2 98.3 %copy-start.23 = (f32[1600]{0:T(1024)}, f32[1600]{0:T(1024)S(1)}, u32[]{:S(2)}) copy-start(f32[1600]{0:T(1024)S(1)} %get-tuple-element.614) | copy-start | bytes 19204
  25.3 98.3 %copy-start.21 = (f32[1600]{0:T(1024)}, f32[1600]{0:T(1024)S(1)}, u32[]{:S(2)}) copy-start(f32[1600]{0:T(1024)S(1)} %get-tuple-element.612) | copy-start | bytes 19204
  25.5 98.0 %copy-start.27 = (f32[128]{0:T(128)}, f32[128]{0:T(128)S(1)}, u32[]{:S(2)}) copy-start(f32[128]{0:T(128)S(1)} %broadcast_multiply_fusion.5) | copy-start | bytes 1540
  25.8 97.8 %copy-start.29 = (f32[128]{0:T(128)}, f32[128]{0:T(128)S(1)}, u32[]{:S(2)}) copy-start(f32[128]{0:T(128)S(1)} %add_rsqrt_fusion.1) | copy-start | bytes 1540
  124.6 130.1 %all-gather.22.cloned.1.call-start = ((), (), s32[]{:S(2)}) async-start(), calls=%async_computation.18 | async-start | bytes 3686400 | tf_op jit(solution)/shard_map/all_gather | solution.py:167
  125.3 169.9 %all-gather.14.cloned.1.call-start = ((), (), s32[]{:S(2)}) async-start(), calls=%async_computation.10 | async-start | bytes 6656000 | tf_op jit(solution)/shard_map/all_gather | solution.py:146
  125.9 299.7 %all-gather.16.cloned.1.call-start = ((), (), s32[]{:S(2)}) async-start(), calls=%async_computation.11 | async-start | bytes 25600000 | tf_op jit(solution)/shard_map/all_gather | solution.py:188
  126.5 14.3 copy-start.25
  126.5 433.9 %all-gather.18.cloned.1.call-start = ((), (), s32[]{:S(2)}) async-start(), calls=%async_computation.12 | async-start | bytes 26624000 | tf_op jit(solution)/shard_map/all_gather | solution.py:190
  127.1 604.5 %reduce-scatter.30.cloned.1.call-start = ((), (), s32[]{:S(2)}) async-start(), calls=%async_computation.20 | async-start | bytes 3833856
  287.0 13.0 copy-start.11
  573.0 12.1 copy-start.10
  573.0 12.1 copy-start.13
  654.0 159.0 %reduce-scatter.28.cloned.1.call-start = ((), (), s32[]{:S(2)}) async-start(), calls=%async_computation.19 | async-start | bytes 3833856
  675.4 192.1 %reduce-scatter.22.cloned.1.call-start = ((), (), s32[]{:S(2)}) async-start(), calls=%async_computation.14 | async-start | bytes 6656000 | tf_op jit(solution)/shard_map/reduce_scatter | solution.py:287
  680.7 137.3 %copy-start.22 = (f32[1600]{0:T(1024)S(1)}, f32[1600]{0:T(1024)}, u32[]{:S(2)}) copy-start(f32[1600]{0:T(1024)} %copy-done.21) | copy-start | bytes 19204
  680.7 137.3 %copy-start.24 = (f32[1600]{0:T(1024)S(1)}, f32[1600]{0:T(1024)}, u32[]{:S(2)}) copy-start(f32[1600]{0:T(1024)} %copy-done.23) | copy-start | bytes 19204
  680.7 137.3 %copy-start.28 = (f32[128]{0:T(128)S(1)}, f32[128]{0:T(128)}, u32[]{:S(2)}) copy-start(f32[128]{0:T(128)} %copy-done.27) | copy-start | bytes 1540
  680.7 137.3 %copy-start.30 = (f32[128]{0:T(128)S(1)}, f32[128]{0:T(128)}, u32[]{:S(2)}) copy-start(f32[128]{0:T(128)} %copy-done.29) | copy-start | bytes 1540
  680.7 308.3 %reduce-scatter.20.cloned.1.call-start = ((), (), s32[]{:S(2)}) async-start(), calls=%async_computation.13 | async-start | bytes 19456000 | tf_op jit(solution)/shard_map/reduce_scatter | solution.py:281
  827.5 321.5 %reduce-scatter.24.cloned.1.call-start = ((), (), s32[]{:S(2)}) async-start(), calls=%async_computation.15 | async-start | bytes 25600000 | tf_op jit(solution)/shard_map/reduce_scatter | solution.py:213
  839.7 467.1 %reduce-scatter.26.cloned.1.call-start = ((), (), s32[]{:S(2)}) async-start(), calls=%async_computation.16 | async-start | bytes 26624000 | tf_op jit(solution)/shard_map/reduce_scatter | solution.py:219
  851.4 484.5 %reduce-scatter.32.cloned.1.call-start = ((), (), s32[]{:S(2)}) async-start(), calls=%async_computation.21 | async-start | bytes 512000
  864.0 490.9 %reduce-scatter.34.cloned.1.call-start = ((), (), s32[]{:S(2)}) async-start(), calls=%async_computation.22 | async-start | bytes 512000
  865.1 513.3 %reduce-scatter.36.cloned.1.call-start = ((), (), s32[]{:S(2)}) async-start(), calls=%async_computation.23 | async-start | bytes 512000
  866.2 1001.1 %all-reduce.12.cloned.1.call-start = ((), (), s32[]{:S(2)}) async-start(), calls=%async_computation.24 | async-start | bytes 31334400 | tf_op jit(solution)/shard_map/psum | solution.py:309
  1320.1 14.8 copy-start.20
  1867.3 7.6 slice-start.2
  (34 other events, 124.2 us)
Sparse Core Ops, SparseCore 0:
  9.6 101.7 all-gather.11
  124.7 64.5 all-gather.19
  191.9 62.7 all-gather.21
  256.1 39.0 all-gather.13
  296.6 128.8 all-gather.15
  427.0 133.4 all-gather.17
  654.2 77.4 reduce-scatter.29
  736.2 76.7 reduce-scatter.27
  816.2 51.2 reduce-scatter.21
  870.2 118.7 reduce-scatter.19
  991.8 157.1 reduce-scatter.23
  1151.4 155.2 reduce-scatter.25
  1310.0 20.8 reduce-scatter.31
  1334.0 20.8 reduce-scatter.33
  1357.4 20.8 reduce-scatter.35
  1383.7 483.5 all-reduce.11
where the time goes:
time: 1900 us; the launch traced here: 1890 us
  waiting for transfers between devices  1510 us (79%)
  matrix products  163 us (9%)
  local copies, waits for them, and re-layouts  85.2 us (4%)
  blocking collectives  77 us (4%)
  other arithmetic  36.6 us (2%)
    psum x1, waiting for transfers between devices, on_device(): lax.psum(d_qkv_w.astype(jnp.bfloat16), 'ctx').astype(jnp.float32)  445 us
    unnamed x21, waiting for transfers between devices  170 us
    reduce_scatter x1, waiting for transfers between devices, on_device(): lax.psum_scatter(d_up_w.astype(jnp.bfloat16), 'wt', scatter_dimension=0,...  160 us
    reduce_scatter x1, waiting for transfers between devices, on_device(): lax.psum_scatter(d_down_w.astype(jnp.bfloat16), 'wt', scatter_dimension=0...  158 us
    all_gather x1, waiting for transfers between devices, on_device(): lax.all_gather(up_weight, 'wt', axis=0, tiled=True)  125 us
    all_gather x1, waiting for transfers between devices, on_device(): lax.all_gather(down_weight, 'wt', axis=0, tiled=True)  123 us
    reduce_scatter x1, waiting for transfers between devices, on_device(): lax.psum_scatter(d_qkv_whole.astype(jnp.bfloat16), 'wt', scatter_dimensio...  122 us
    all_gather x1, waiting for transfers between devices, on_device(): lax.all_gather(qkv_weight, 'wt', axis=0, tiled=True)  85.6 us
  transfers between devices with their start and end apart: 16, of which 15 were waited for; matrix products, arithmetic and copies ran while one was open for 8% of the time, Pallas kernels for 0%

commit v1 on v0

v1 whole, which is shorter than its diff:
```python
import functools
import math

import jax
import jax.numpy as jnp
from jax import lax
from jax.experimental import pallas as pl
from jax.experimental.pallas import tpu as pltpu
from jax.sharding import PartitionSpec as P

AXES = ("ctx", "wt")
F32 = jnp.float32
BF16 = jnp.bfloat16


def standardize(values):
    centred = values - jnp.mean(values, axis=-1, keepdims=True)
    scale = lax.rsqrt(jnp.mean(centred * centred, axis=-1, keepdims=True) + 1e-05)
    return (centred * scale, scale)


def finish_norm(scaled, normed, scale):
    inner = (
        scaled
        - jnp.mean(scaled, axis=-1, keepdims=True)
        - normed * jnp.mean(scaled * normed, axis=-1, keepdims=True)
    )
    return scale * inner


def gelu(values):
    return (
        0.5
        * values
        * (1.0 + jnp.tanh(0.7978845608028654 * (values + 0.044715 * values * values * values)))
    )


def dot(left, right):
    return jnp.dot(left, right, preferred_element_type=F32)


def over_rows(left, right):
    return lax.dot_general(left, right, (((0,), (0,)), ((), ())), preferred_element_type=F32)


def by_transpose(left, right):
    return lax.dot_general(left, right, (((1,), (1,)), ((), ())), preferred_element_type=F32)


def add_low(left, right):
    return (left.astype(F32) + right.astype(F32)).astype(BF16)


UNROLLED = 1024


def for_tiles(one, length, tile, key_axis):
    if length <= UNROLLED:
        shape = (tile, tile)
        key = lax.broadcasted_iota(jnp.int32, shape, key_axis)
        query = lax.broadcasted_iota(jnp.int32, shape, 1 - key_axis)
        for turn in range(length // tile):
            one(turn, turn * tile, pl.ds(turn * tile, tile), key <= query)
        return

    def turn_of(turn, carry):
        shape = (tile, length) if key_axis else (length, tile)
        key = lax.broadcasted_iota(jnp.int32, shape, key_axis)
        query = lax.broadcasted_iota(jnp.int32, shape, 1 - key_axis)
        one(turn, 0, pl.ds(0, length), key <= query + turn * tile)
        return carry

    lax.fori_loop(0, length // tile, turn_of, 0)


def attn_forward_kernel(tile, block, place_ref, qkv_ref, *refs):
    outs, (lse_ref, qs, ks, vs, os) = refs[:-5], refs[-5:]
    length, wide = os.shape

    for i in range(length // block):
        here = pl.ds(pl.multiple_of(place_ref[i] * block, block), block)
        there = slice(i * block, (i + 1) * block)
        qs[here, :] = qkv_ref[there, 0:wide] * 0.125
        ks[here, :] = qkv_ref[there, wide : 2 * wide]
        vs[here, :] = qkv_ref[there, 2 * wide : 3 * wide]
    lane = lax.broadcasted_iota(jnp.int32, (tile, 128), 1)

    def one(turn, before, near, allowed):
        mine = pl.ds(turn * tile, tile)
        stats = jnp.zeros((tile, 128), F32)
        for pair in range(wide // 128):
            cols = slice(pair * 128, (pair + 1) * 128)
            q = qs[mine, cols]
            halves = []
            for half in range(2):
                keep = (lane >= 64) if half else (lane < 64)
                qh = jnp.where(keep, q, jnp.zeros_like(q))
                edge = by_transpose(qh, ks[near, cols])
                edge = jnp.where(allowed, edge, -1e30)
                most = jnp.max(edge, axis=1, keepdims=True)
                if before:
                    past = by_transpose(qh, ks[0:before, cols])
                    most = jnp.maximum(most, jnp.max(past, axis=1, keepdims=True))
                edge = jnp.exp(edge - most)
                total = jnp.sum(edge, axis=1, keepdims=True)
                acc = dot(edge.astype(BF16), vs[near, cols])
                if before:
                    past = jnp.exp(past - most)
                    total = total + jnp.sum(past, axis=1, keepdims=True)
                    acc = acc + dot(past.astype(BF16), vs[0:before, cols])
                halves.append(acc / total)
                stats = jnp.where(lane == 2 * pair + half, most + jnp.log(total), stats)
            os[mine, cols] = jnp.where(lane < 64, halves[0], halves[1]).astype(BF16)
        lse_ref[mine, :] = stats

    for_tiles(one, length, tile, 1)

    for i in range(length // block):
        here = pl.ds(pl.multiple_of(place_ref[i] * block, block), block)
        outs[i // 2][(i % 2) * block : (i % 2 + 1) * block, :] = os[here, :]


def attn_backward_kernel(tile, block, place_ref, qkv_ref, lse_ref, *refs):
    grads, (out_ref, qs, ks, vs, gs, dq, dk, dv) = refs[:-8], refs[-8:]
    length, wide = gs.shape
    for i in range(length // block):
        here = pl.ds(pl.multiple_of(place_ref[i] * block, block), block)
        there = slice(i * block, (i + 1) * block)
        qs[here, :] = qkv_ref[there, 0:wide] * 0.125
        ks[here, :] = qkv_ref[there, wide : 2 * wide]
        vs[here, :] = qkv_ref[there, 2 * wide : 3 * wide]
        gs[here, :] = grads[i // 2][(i % 2) * block : (i % 2 + 1) * block, :]
    lane = lax.broadcasted_iota(jnp.int32, (tile, 128), 1)
    alone = length <= UNROLLED
    if not alone:
        dk[...] = jnp.zeros_like(dk)
        dv[...] = jnp.zeros_like(dv)

    def one(turn, before, near, allowed):
        mine = pl.ds(turn * tile, tile)
        lse = lse_ref[mine, :].T
        for pair in range(wide // 128):
            cols = slice(pair * 128, (pair + 1) * 128)
            q, g = qs[mine, cols], gs[mine, cols]
            halves = []
            for half in range(2):
                keep = (lane >= 64) if half else (lane < 64)
                qh = jnp.where(keep, q, jnp.zeros_like(q))
                gh = jnp.where(keep, g, jnp.zeros_like(g))
                row = lse[2 * pair + half : 2 * pair + half + 1, :]
                edge_p = by_transpose(ks[near, cols], qh)
                edge_p = jnp.where(allowed, jnp.exp(edge_p - row), 0.0)
                edge_t = edge_p * by_transpose(vs[near, cols], gh)
                delta = jnp.sum(edge_t, axis=0, keepdims=True)
                if before:
                    past_p = jnp.exp(by_transpose(ks[0:before, cols], qh) - row)
                    past_t = past_p * by_transpose(vs[0:before, cols], gh)
                    delta = delta + jnp.sum(past_t, axis=0, keepdims=True)
                edge_s = (edge_t - edge_p * delta).astype(BF16)
                own_v = dot(edge_p.astype(BF16), gh)
                own_k = dot(edge_s, qh)
                if half or not alone:
                    dv[near, cols] += own_v
                    dk[near, cols] += own_k
                else:
                    dv[near, cols] = own_v
                    dk[near, cols] = own_k
                acc = over_rows(edge_s, ks[near, cols])
                if before:
                    past_s = (past_t - past_p * delta).astype(BF16)
                    dv[0:before, cols] += dot(past_p.astype(BF16), gh)
                    dk[0:before, cols] += dot(past_s, qh)
                    acc = acc + over_rows(past_s, ks[0:before, cols])
                halves.append(acc)
            dq[mine, cols] = (jnp.where(lane < 64, halves[0], halves[1]) * 0.125).astype(BF16)

    for_tiles(one, length, tile, 0)

    for i in range(length // block):
        here = pl.ds(pl.multiple_of(place_ref[i] * block, block), block)
        there = slice(i * block, (i + 1) * block)
        out_ref[there, 0:wide] = dq[here, :]
        out_ref[there, wide : 2 * wide] = dk[here, :].astype(BF16)
        out_ref[there, 2 * wide : 3 * wide] = dv[here, :].astype(BF16)


SMEM = pl.BlockSpec(memory_space=pltpu.SMEM)
VMEM = pl.BlockSpec(memory_space=pltpu.VMEM)
LIMIT = 48 * 1024 * 1024


def attn_forward(qkv, place, block, tile):
    length, wide = qkv.shape[0], qkv.shape[1] // 3
    n = length // (2 * block)
    *outs, lse = pl.pallas_call(
        functools.partial(attn_forward_kernel, tile, block),
        out_shape=(jax.ShapeDtypeStruct((2 * block, wide), BF16),) * n
        + (jax.ShapeDtypeStruct((length, 128), F32),),
        in_specs=[SMEM, VMEM],
        out_specs=(VMEM,) * (n + 1),
        scratch_shapes=[pltpu.VMEM((length, wide), BF16)] * 4,
        compiler_params=pltpu.CompilerParams(vmem_limit_bytes=LIMIT),
        cost_estimate=pl.CostEstimate(
            flops=4 * length * length * wide,
            bytes_accessed=length * wide * 10,
            transcendentals=length * length * wide // 128,
        ),
    )(place, qkv)
    return outs, lse


def attn_backward(qkv, grads, lse, place, block, tile):
    length, wide = qkv.shape[0], qkv.shape[1] // 3
    return pl.pallas_call(
        functools.partial(attn_backward_kernel, tile, block),
        out_shape=jax.ShapeDtypeStruct((length, 3 * wide), BF16),
        in_specs=[SMEM] + [VMEM] * (2 + len(grads)),
        out_specs=VMEM,
        scratch_shapes=[pltpu.VMEM((length, wide), BF16)] * 5
        + [pltpu.VMEM((length, wide), F32)] * 2,
        compiler_params=pltpu.CompilerParams(vmem_limit_bytes=LIMIT),
        cost_estimate=pl.CostEstimate(
            flops=10 * length * length * wide,
            bytes_accessed=length * wide * 16,
            transcendentals=length * length * wide // 128,
        ),
    )(place, qkv, lse, *grads)


def rearrange(kernel, outs, numbers, arrays, scratch=()):
    size = sum(math.prod(o.shape) * o.dtype.itemsize for o in (*outs, *arrays))
    return pl.pallas_call(
        kernel,
        out_shape=tuple(jax.ShapeDtypeStruct(o.shape, o.dtype) for o in outs),
        in_specs=[SMEM] + [VMEM] * len(arrays),
        out_specs=(VMEM,) * len(outs),
        scratch_shapes=list(scratch),
        compiler_params=pltpu.CompilerParams(vmem_limit_bytes=LIMIT),
        cost_estimate=pl.CostEstimate(flops=0, bytes_accessed=size, transcendentals=0),
    )(jnp.stack(numbers).astype(jnp.int32), *arrays)


def shaped(shape, dtype=BF16):
    return jax.ShapeDtypeStruct(shape, dtype)


class Heads:
    def __init__(self, n, width):
        self.n, self.width = n, width
        self.full, self.rest = width // 128, width % 128
        self.slots = -(-(self.full + (self.rest > 0)) // n)
        self.wide = 128 * self.slots

    def pick_kernel(self, numbers, from_ref, out_ref):
        rows = from_ref.shape[0]
        for t in range(3):
            base = t * self.width
            first, off = base // 128, base % 128
            for j in range(self.slots):
                to = slice((t * self.slots + j) * 128, (t * self.slots + j + 1) * 128)
                p = j * self.n + numbers[0]

                @pl.when(p < self.full)
                def _():
                    start = pl.multiple_of((first + p) * 128, 128)
                    if off:
                        out_ref[:, to] = from_ref[:, pl.ds(start, 256)][:, off : off + 128]
                    else:
                        out_ref[:, to] = from_ref[:, pl.ds(start, 128)]

                @pl.when(p >= self.full)
                def _():
                    out_ref[:, to] = jnp.zeros((rows, 128), out_ref.dtype)

                if self.rest:
                    at = base + self.full * 128

                    @pl.when(p == self.full)
                    def _():
                        out_ref[:, to.start : to.start + self.rest] = from_ref[
                            :, at : at + self.rest
                        ]

    def pick(self, weight, c):
        out = shaped((weight.shape[0], 3 * self.wide))
        return rearrange(self.pick_kernel, [out], [c], [weight])[0]

    def join_kernel(self, numbers, *refs):
        out_ref = refs[-1]
        for d in range(self.n):
            for j in range(self.slots):
                p = j * self.n + (numbers[0] ^ d)
                value = refs[d].at[:, j * 128 : (j + 1) * 128]

                @pl.when(p < self.full)
                def _():
                    out_ref[:, pl.ds(pl.multiple_of(p * 128, 128), 128)] = value[...]

                if self.rest:

                    @pl.when(p == self.full)
                    def _():
                        out_ref[:, self.full * 128 :] = value[:, : self.rest]

    def join(self, blocks, c):
        out = shaped((blocks[0].shape[0], self.width))
        return rearrange(self.join_kernel, [out], [c], blocks)[0]

    def split_kernel(self, numbers, from_ref, *outs):
        rows = from_ref.shape[0]
        for d in range(self.n):
            for j in range(self.slots):
                p = j * self.n + (numbers[0] ^ d)
                to = slice(j * 128, (j + 1) * 128)

                @pl.when(p < self.full)
                def _():
                    outs[d][:, to] = from_ref[:, pl.ds(pl.multiple_of(p * 128, 128), 128)]

                @pl.when(p >= self.full)
                def _():
                    outs[d][:, to] = jnp.zeros((rows, 128), BF16)

                if self.rest:

                    @pl.when(p == self.full)
                    def _():
                        outs[d][:, to.start : to.start + self.rest] = from_ref[
                            :, self.full * 128 :
                        ]

    def split(self, value, c):
        out = shaped((value.shape[0], self.wide))
        return rearrange(self.split_kernel, [out] * self.n, [c], [value])

    def here(self, values, c):
        lead = values.shape[:-1]
        values = jnp.pad(values, [(0, 0)] * len(lead) + [(0, self.n * self.wide - self.width)])
        values = values.reshape(lead + (self.slots, self.n, 128))
        return lax.dynamic_index_in_dim(values, c, len(lead) + 1, False).reshape(
            lead + (self.wide,)
        )

    def back(self, values, c):
        lead = values.shape[:-1]
        zeros = jnp.zeros(lead + (self.slots, self.n, 128), values.dtype)
        values = values.reshape(lead + (self.slots, 1, 128))
        values = lax.dynamic_update_slice(zeros, values, (0,) * (len(lead) + 1) + (c, 0))
        return values.reshape(lead + (self.n * self.wide,))[..., : self.width]


def cut_kernel(per, numbers, from_ref, *outs):
    for r, out_ref in enumerate(outs):
        for part in range(from_ref.shape[1] // per):

            @pl.when(numbers[r] == part)
            def _():
                out_ref[...] = from_ref[:, part * per : (part + 1) * per]


def place_kernel(numbers, *refs):
    out_ref = refs[-1]
    for r, ref in enumerate(refs[:-1]):
        size = ref.shape[0]
        out_ref[pl.ds(pl.multiple_of(numbers[r] * size, 16), size), :] = ref[...]


def lay_kernel(plan, numbers, *refs):
    blocks, out_ref, held = refs[:-2], refs[-2], refs[-1]
    for r, ref in enumerate(blocks):
        held[numbers[r]] = ref[...]
    for b, from_rows, from_cols, rows, cols in plan:
        out_ref[rows, cols] = held[b, from_rows, from_cols].astype(F32)


def lay(blocks, numbers, plan, shape):
    steps = [
        (b, slice(r, r + h), slice(q, q + v), slice(tr, tr + h), slice(tq, tq + v))
        for b, (r, q), (h, v), (tr, tq) in plan
    ]
    scratch = [pltpu.VMEM((len(blocks),) + blocks[0].shape, BF16)]
    kernel = functools.partial(lay_kernel, steps)
    return rearrange(kernel, [shaped(shape, F32)], numbers, blocks, scratch)[0]


class Links:
    def __init__(self):
        self.n, self.m = lax.axis_size("ctx"), lax.axis_size("wt")
        self.nz = self.n // 2
        self.c, self.w = lax.axis_index("ctx"), lax.axis_index("wt")
        self.z, self.y = self.c // 2, self.c % 2

    def swap(self, value, dc, dw):
        pairs = [
            (c * self.m + w, (c ^ dc) * self.m + (w ^ dw))
            for c in range(self.n)
            for w in range(self.m)
        ]
        return lax.ppermute(value, AXES, pairs)

    def core(self, value):
        return self.swap(value, 0, 1)

    def x(self, value):
        return self.swap(value, 0, 2)

    def yy(self, value):
        return self.swap(value, 1, 0)


    def gather_wt(self, value):
        across = self.x(value)
        return [value, self.core(value), across, self.core(across)]

    def rows_wt(self, blocks):
        size, cols = blocks[0].shape
        return rearrange(
            place_kernel,
            [shaped((self.m * size, cols))],
            [self.w ^ r for r in range(self.m)],
            blocks,
        )[0]

    def trade_wt(self, pieces):
        far = self.x(pieces[3])
        return [pieces[0], self.core(pieces[1]), self.x(pieces[2]), self.core(far)]

    def reduce_wt(self, pieces):
        other = add_low(pieces[2], self.core(pieces[3]))
        mine = add_low(pieces[0], self.core(pieces[1]))
        return add_low(mine, self.x(other))


    def gather_ctx(self, value):
        far = [value] + [self.swap(value, 2 * d, 0) for d in range(1, self.nz)]
        return [part for one in far for part in (one, self.yy(one))]

    def sum_z(self, pieces):
        come = [self.swap(pieces[d], 2 * d, 0) for d in range(1, self.nz)]
        return sum((part.astype(F32) for part in come), pieces[0].astype(F32))


    def gather_plane(self, value):
        mine = [value, self.x(value), self.yy(value), self.swap(value, 1, 2)]
        return jnp.concatenate(mine + [self.core(part) for part in mine])

    def sum_plane(self, near, far):
        mine = add_low(near, self.core(far))
        size = mine.shape[0] // 4
        parts = [mine[i * size : (i + 1) * size] for i in range(4)]
        come = [self.swap(parts[3], 1, 2), self.yy(parts[2]), self.x(parts[1])]
        return sum((part.astype(F32) for part in come), parts[0].astype(F32))


def on_device(
    tokens,
    slots,
    norm_gains,
    norm_shifts,
    qkv_weight,
    qv_bias,
    proj_weight,
    proj_bias,
    up_weight,
    up_bias,
    down_weight,
    down_bias,
    cotangent,
):
    links = Links()
    n, m, nz, c, w, z, y = links.n, links.m, links.nz, links.c, links.w, links.z, links.y
    _, rows, width = tokens.shape
    heads = Heads(n, width)
    share = width // m
    block = rows // 2
    length = n * rows
    hid = up_weight.shape[1]
    per = hid // (2 * m)
    tile = 256 if length <= UNROLLED else 128
    near = rows * m

    own = tokens[0]
    seen = jnp.concatenate(links.gather_ctx(own))
    wqkv = links.rows_wt(links.gather_wt(heads.pick(qkv_weight, c)))

    small = jnp.concatenate(
        [
            norm_gains.reshape(-1),
            norm_shifts.reshape(-1),
            qv_bias.reshape(-1),
            proj_bias,
            down_bias,
            up_bias,
        ]
    )
    small = jnp.stack(links.gather_wt(small[None])).reshape(m, -1)
    number = jnp.arange(m, dtype=jnp.int32)
    small = dot((number[:, None] == (number[None, :] ^ w)).astype(BF16), small)
    pairs = small[:, : 6 * share].reshape(m, 3, 2, share).transpose(1, 2, 0, 3).reshape(3, 2, width)
    gains, shifts, qvb = pairs[0], pairs[1], pairs[2]
    bproj = small[:, 6 * share : 7 * share].reshape(width)
    bdown = small[:, 7 * share : 8 * share].reshape(width)
    bup = lax.dynamic_index_in_dim(small[:, 8 * share :].reshape(m * 2, per), w * 2 + y, 0, False)

    a1 = (standardize(seen.astype(F32))[0] * gains[0] + shifts[0]).astype(BF16)
    qvb_here = heads.here(qvb, c)
    bias = jnp.concatenate([qvb_here[0], jnp.zeros((heads.wide,), F32), qvb_here[1]])
    qkv = (dot(a1, wqkv) + bias).astype(BF16)

    table = jnp.arange(slots.shape[0], dtype=jnp.int32)
    wanted = (((table // 2) ^ c) * 2 + table % 2)[:, None] == table[None, :]
    place = jnp.sum(jnp.where(wanted, slots[None, :], 0), axis=1)

    heads_out, lse = attn_forward(qkv, place, block, tile)

    wproj = links.rows_wt(links.gather_wt(proj_weight))
    pieces = rearrange(
        functools.partial(cut_kernel, per),
        [shaped((share, per))] * m,
        [(w ^ r) * 2 + y for r in range(m)],
        [up_weight],
    )
    wup = links.rows_wt(links.trade_wt(pieces))
    wdown = lax.dynamic_slice_in_dim(down_weight, y * per, per, 0)
    grad_out = cotangent[0]
    grad_out_plane = links.gather_plane(grad_out)

    attended = heads.join(
        [heads_out[0]] + [links.swap(heads_out[d], d, 0) for d in range(1, n)], c
    )
    mid = own.astype(F32) + dot(attended, wproj) + bproj
    normed2, scale2 = standardize(mid)
    a2 = (normed2 * gains[1] + shifts[1]).astype(BF16)

    a2_plane = links.gather_plane(a2)
    pre = dot(a2_plane, wup) + bup
    activated, gelu_pull = jax.vjp(gelu, pre)
    hidden = activated.astype(BF16)
    grad_pre = gelu_pull(by_transpose(grad_out_plane, wdown))[0].astype(BF16)
    grad_a2 = links.sum_plane(
        by_transpose(grad_pre[:near], wup).astype(BF16),
        by_transpose(grad_pre[near:], wup).astype(BF16),
    )
    step = -(-(-(-per // nz)) // 8) * 8
    d_down = over_rows(hidden, grad_out_plane).astype(BF16)
    d_down = jnp.pad(d_down, [(0, step * nz - per), (0, 0)])
    d_down = links.sum_z(
        [lax.dynamic_slice_in_dim(d_down, (z ^ d) * step, step, 0) for d in range(nz)]
    ).astype(BF16)
    d_up = over_rows(a2_plane, grad_pre).astype(BF16)
    d_up = links.trade_wt(
        [lax.dynamic_slice_in_dim(d_up, (w ^ r) * share, share, 0) for r in range(m)]
    )
    cut = nz // m
    d_up = jnp.stack(d_up).reshape(m, share, cut, per // cut).transpose(0, 2, 1, 3)

    def up_term(d):
        b = z ^ d
        return lax.dynamic_slice(
            d_up, (w ^ (b // cut), b % cut, 0, 0), (1, 1, share, per // cut)
        ).reshape(share, per // cut)

    d_up = links.sum_z([up_term(d) for d in range(nz)]).astype(BF16)

    grad_out32 = grad_out.astype(F32)
    d_gain2 = jnp.sum(grad_a2 * normed2, axis=0)
    d_shift2 = jnp.sum(grad_a2, axis=0)
    grad_mid = grad_out32 + finish_norm(grad_a2 * gains[1], normed2, scale2)
    grad_proj = grad_mid.astype(BF16)

    grad_heads = heads.split(by_transpose(grad_proj, wproj).astype(BF16), c)
    grad_heads = [grad_heads[0]] + [links.swap(grad_heads[d], d, 0) for d in range(1, n)]
    grad_qkv = attn_backward(qkv, grad_heads, lse, place, block, tile)

    terms = []
    for d in [*range(1, nz), 0]:
        part = grad_qkv[2 * d * rows : 2 * (d + 1) * rows]
        other = by_transpose(part[rows:], wqkv).astype(BF16)
        terms.append(add_low(by_transpose(part[:rows], wqkv), links.yy(other)))
    grad_a1 = links.sum_z(terms[-1:] + terms[:-1])
    d_qkv = over_rows(a1, grad_qkv).astype(BF16)
    d_qkv = links.reduce_wt(
        [lax.dynamic_slice_in_dim(d_qkv, (w ^ r) * share, share, 0) for r in range(m)]
    )

    output = (
        mid
        + links.sum_plane(
            dot(hidden[:near], wdown).astype(BF16), dot(hidden[near:], wdown).astype(BF16)
        )
        + bdown
    )

    d_proj = over_rows(attended, grad_proj).astype(BF16)
    d_proj = links.reduce_wt(
        [lax.dynamic_slice_in_dim(d_proj, (w ^ r) * share, share, 0) for r in range(m)]
    )
    part = -(-(-(-share // n)) // 8) * 8
    d_proj = jnp.pad(d_proj, [(0, n * part - share), (0, 0)]).reshape(nz, 2, part, width)
    d_proj = add_low(
        lax.dynamic_index_in_dim(d_proj, y, 1, False),
        links.yy(lax.dynamic_index_in_dim(d_proj, 1 - y, 1, False)),
    )
    d_proj = links.sum_z(
        [lax.dynamic_index_in_dim(d_proj, z ^ d, 0, False) for d in range(nz)]
    ).astype(BF16)

    numbers = [c ^ d for d in range(n)]
    plan = [
        (b, (0, 0), (min(step, per - (b // 2) * step), width), ((b % 2) * per + (b // 2) * step, 0))
        for b in range(n)
        if (b // 2) * step < per
    ]
    d_down_weight = lay(links.gather_ctx(d_down), numbers, plan, (2 * per, width))
    size = per // cut
    plan = [
        (
            b,
            (0, 0),
            (share, size),
            (0, (b // 2 // cut) * 2 * per + (b % 2) * per + (b // 2 % cut) * size),
        )
        for b in range(n)
    ]
    d_up_weight = lay(links.gather_ctx(d_up), numbers, plan, (share, hid))
    plan = [
        (b, (0, 0), (min(part, share - b * part), width), (b * part, 0))
        for b in range(n)
        if b * part < share
    ]
    d_proj_weight = lay(links.gather_ctx(d_proj), numbers, plan, (share, width))
    plan = [
        (
            p % n,
            (0, (t * heads.slots + p // n) * 128),
            (share, min(128, width - p * 128)),
            (0, t * width + p * 128),
        )
        for t in range(3)
        for p in range(-(-width // 128))
    ]
    d_qkv_weight = lay(links.gather_ctx(d_qkv), numbers, plan, (share, 3 * width))

    normed1, scale1 = standardize(own.astype(F32))
    d_gain1 = jnp.sum(grad_a1 * normed1, axis=0)
    d_shift1 = jnp.sum(grad_a1, axis=0)
    d_tokens = grad_mid + finish_norm(grad_a1 * gains[0], normed1, scale1)

    col_sums = heads.back(jnp.sum(grad_qkv.astype(F32), axis=0).reshape(3, heads.wide), c)
    d_up_bias = lax.dynamic_update_slice(
        jnp.zeros((m * 2, per), F32),
        jnp.sum(grad_pre.astype(F32), axis=0)[None],
        (w * 2 + y, 0),
    ).reshape(m, hid // m)
    vectors = jnp.stack(
        [
            d_gain1,
            d_gain2,
            d_shift1,
            d_shift2,
            col_sums[0],
            col_sums[2],
            jnp.sum(grad_proj.astype(F32), axis=0),
            jnp.sum(grad_out32, axis=0),
        ]
    ).reshape(8, m, share)
    vectors = jnp.concatenate([vectors.transpose(1, 0, 2).reshape(m, 8 * share), d_up_bias], axis=1)
    for dc, dw in [(0, 1), (0, 2)] + [(1 << i, 0) for i in range(n.bit_length() - 1)]:
        vectors = vectors + links.swap(vectors, dc, dw)
    vectors = lax.dynamic_index_in_dim(vectors, w, 0, False)
    eight = vectors[: 8 * share].reshape(8, share)

    return (
        output.astype(BF16)[None],
        d_tokens.astype(BF16)[None],
        eight[0:2],
        eight[2:4],
        d_qkv_weight,
        eight[4:6],
        d_proj_weight,
        eight[6],
        d_up_weight,
        vectors[8 * share :],
        d_down_weight,
        eight[7],
    )


def solution(mesh):
    rows, whole = P("wt", "ctx", None), P(None, "wt")
    weight, vector = P("wt", None), P("wt")
    return jax.shard_map(
        on_device,
        mesh=mesh,
        in_specs=(
            rows,
            P(),
            whole,
            whole,
            weight,
            whole,
            weight,
            vector,
            weight,
            vector,
            weight,
            vector,
            rows,
        ),
        out_specs=(
            rows,
            rows,
            whole,
            whole,
            weight,
            whole,
            weight,
            vector,
            weight,
            vector,
            weight,
            vector,
        ),
        check_vma=False,
    )
```

time: 1900 us -> 730 us (0.38)
  waiting for transfers between devices: 1510 us -> 363 us
  starting transfers between devices: 0.9 us -> 143 us
  matrix products: 163 us -> 61.3 us
  blocking collectives: 77 us -> 0 us
  Pallas kernels: 0 us -> 51.1 us
    all_gather x6 -> x0, waiting for transfers between devices: 456 us -> none  [the longest x1 125 us: on_device(): lax.all_gather(up_weight, 'wt', axis=0, tiled=True)]
    psum x1 -> x0, waiting for transfers between devices: 445 us -> none  [on_device(): lax.psum(d_qkv_w.astype(jnp.bfloat16), 'ctx').astype(jnp.float32)]
    reduce_scatter x4 -> x0, waiting for transfers between devices: 441 us -> none  [the longest x1 160 us: on_device(): lax.psum_scatter(d_up_w.astype(jnp.bfloat16), 'wt', scatter_dimension=0,...]
    ppermute x0 -> x116, waiting for transfers between devices: none -> 363 us  [swap(): return lax.ppermute(value, AXES, pairs)]
    unnamed x21 -> x0, waiting for transfers between devices: 170 us -> none
    ppermute x0 -> x116, starting transfers between devices: none -> 143 us  [swap(): return lax.ppermute(value, AXES, pairs)]
    dot_general x18 -> x6, matrix products: 85.6 us -> 17.9 us  [dot(): return jnp.dot(left, right, preferred_element_type=F32)]
    pallas_call x0 -> x13, Pallas kernels: none -> 51.1 us  [the longest x11 33.3 us: rearrange(): pl.pallas_call(kernel, out_shape=tuple((jax.ShapeDtypeStruct(o.shape, o.d...]
  transfers between devices with their start and end apart: 16 -> 116, of which waited for: 15 -> 42; matrix products, arithmetic and copies ran while one was open for 8% -> 16% of each run, Pallas kernels for 0% -> 7%
where the time goes in v1:
time: 730 us; the launch traced here: 723 us
  waiting for transfers between devices  363 us (50%)
  starting transfers between devices  143 us (20%)
  local copies, waits for them, and re-layouts  70.4 us (10%)
  matrix products  61.3 us (8%)
  Pallas kernels  51.1 us (7%)
  other arithmetic  31.7 us (4%)
    ppermute x116, waiting for transfers between devices, swap(): return lax.ppermute(value, AXES, pairs)  363 us
    ppermute x116, starting transfers between devices, swap(): return lax.ppermute(value, AXES, pairs)  143 us
    unnamed x204, local copies, waits for them, and re-layouts  35.4 us
    pallas_call x11, Pallas kernels, rearrange(): pl.pallas_call(kernel, out_shape=tuple((jax.ShapeDtypeStruct(o.shape, o.d...  33.3 us
    dot_general x12, matrix products, by_transpose(): lax.dot_general(left, right, (((1,), (1,)), ((), ())), preferred_element_...  25.9 us
    dot_general x6, matrix products, dot(): return jnp.dot(left, right, preferred_element_type=F32)  17.9 us
    dot_general x4, matrix products, over_rows(): lax.dot_general(left, right, (((0,), (0,)), ((), ())), preferred_element_...  17.5 us
  transfers between devices with their start and end apart: 116, of which 42 were waited for; matrix products, arithmetic and copies ran while one was open for 16% of the time, Pallas kernels for 7%

profile of v1, /device:TPU:0, one launch (start us, length us, event | category | flops | bytes accessed | tf_op | source)
XLA Modules:
  0.0 723.1 jit_solution(14937160646496788622)
XLA Ops:
  33.5 6.5 collective-permute-done.1
  48.3 22.4 %collective-permute-done.3 = bf16[128,1600]{0,1:T(8,128)(2,1)S(1)} collective-permute-done((bf16[128,1600]{0,1:T(8,128)(2,1)S(1)}, bf16[128,1600]{0,1:T(8,128)(2,1)S(1)}, u32[]{:S(2)}, u32[]{:S(2)}) %collective-permute-start.3) | collective-permute-done | bytes 409632 | tf_op jit(solution)/shard_map/ppermute | solution.py:400
  74.8 6.1 collective-permute-done.4
  95.7 17.1 %collective-permute-done.21.refs_2_ = bf16[400,1600]{1,0:T(8,128)(2,1)S(1)} collective-permute-done((bf16[400,1600]{1,0:T(8,128)(2,1)}, bf16[400,1600]{1,0:T(8,128)(2,1)S(1)}, u32[]{:S(2)}, u32[]{:S(2)}) %collective-permute-start.21) | collective-permute-done | bytes 1280032 | tf_op jit(solution)/shard_map/ppermute | solution.py:400
  116.7 6.7 shard_map.222
  141.2 5.8 collective-permute-start.18
  171.9 7.3 %collective-permute-done.25 = bf16[128,1600]{0,1:T(8,128)(2,1)S(1)} collective-permute-done((bf16[128,1600]{0,1:T(8,128)(2,1)S(1)}, bf16[128,1600]{0,1:T(8,128)(2,1)S(1)}, u32[]{:S(2)}, u32[]{:S(2)}) %collective-permute-start.25) | collective-permute-done | bytes 409632 | tf_op jit(solution)/shard_map/ppermute | solution.py:400
  179.2 8.2 %collective-permute-done.24 = bf16[128,1600]{0,1:T(8,128)(2,1)S(1)} collective-permute-done((bf16[128,1600]{0,1:T(8,128)(2,1)S(1)}, bf16[128,1600]{0,1:T(8,128)(2,1)S(1)}, u32[]{:S(2)}, u32[]{:S(2)}) %collective-permute-start.24) | collective-permute-done | bytes 409632 | tf_op jit(solution)/shard_map/ppermute | solution.py:400
  219.9 6.7 collective-permute-done.94
  227.4 15.7 %collective-permute-done.108 = bf16[200,1600]{1,0:T(8,128)(2,1)S(1)} collective-permute-done((bf16[200,1600]{1,0:T(8,128)(2,1)S(1)}, bf16[200,1600]{1,0:T(8,128)(2,1)S(1)}, u32[]{:S(2)}, u32[]{:S(2)}) %collective-permute-start.108) | collective-permute-done | bytes 640032 | tf_op jit(solution)/shard_map/ppermute | solution.py:400
  247.0 24.1 %collective-permute-done.107 = bf16[200,1600]{1,0:T(8,128)(2,1)} collective-permute-done((bf16[200,1600]{1,0:T(8,128)(2,1)}, bf16[200,1600]{1,0:T(8,128)(2,1)}, u32[]{:S(2)}, u32[]{:S(2)}) %collective-permute-start.107) | collective-permute-done | bytes 640032 | tf_op jit(solution)/shard_map/ppermute | solution.py:400
  295.5 7.3 %collective-permute-done.48 = bf16[128,1600]{0,1:T(8,128)(2,1)S(1)} collective-permute-done((bf16[128,1600]{0,1:T(8,128)(2,1)S(1)}, bf16[128,1600]{0,1:T(8,128)(2,1)S(1)}, u32[]{:S(2)}, u32[]{:S(2)}) %collective-permute-start.48) | collective-permute-done | bytes 409632 | tf_op jit(solution)/shard_map/ppermute | solution.py:400
  304.9 7.3 %collective-permute-done.35 = bf16[128,1600]{0,1:T(8,128)(2,1)S(1)} collective-permute-done((bf16[128,1600]{0,1:T(8,128)(2,1)S(1)}, bf16[128,1600]{0,1:T(8,128)(2,1)S(1)}, u32[]{:S(2)}, u32[]{:S(2)}) %collective-permute-start.35) | collective-permute-done | bytes 409632 | tf_op jit(solution)/shard_map/ppermute | solution.py:400
  312.2 7.8 %collective-permute-done.37 = bf16[128,1600]{0,1:T(8,128)(2,1)S(1)} collective-permute-done((bf16[128,1600]{0,1:T(8,128)(2,1)S(1)}, bf16[128,1600]{0,1:T(8,128)(2,1)S(1)}, u32[]{:S(2)}, u32[]{:S(2)}) %collective-permute-start.37) | collective-permute-done | bytes 409632 | tf_op jit(solution)/shard_map/ppermute | solution.py:400
  359.1 11.1 %shard_map.228 = bf16[1024,768]{1,0:T(8,128)(2,1)S(1)} custom-call(s32[16]{0:T(128)S(1)} %select_reduce_fusion.place_ref, bf16[1024,768]{1,0:T(8,128)(2,1)S(1)} %copy-done.24, f32[1024,128]{1,0:T(8,128)S(1)} %copy-done.26, bf16[128,256]{1,0:T(8,128)(2,1)S(1)} %copy-done.18, bf16[128,256]{1,0:T(8,128)(2,1)S(1)} %copy-done.20, ...), custom_call_target="tpu_custom_call" | custom-call | flops 2684354560 | bytes 4194304 | tf_op jit(solution)/shard_map/pallas_call | solution.py:215
  381.9 7.1 collective-permute-done.57
  391.4 6.3 collective-permute-done.59
  401.0 11.0 %collective-permute-done.61 = bf16[128,1600]{0,1:T(8,128)(2,1)S(1)} collective-permute-done((bf16[128,1600]{0,1:T(8,128)(2,1)S(1)}, bf16[128,1600]{0,1:T(8,128)(2,1)S(1)}, u32[]{:S(2)}, u32[]{:S(2)}) %collective-permute-start.61) | collective-permute-done | bytes 409632 | tf_op jit(solution)/shard_map/ppermute | solution.py:400
  426.6 13.2 %collective-permute-done.60 = bf16[128,1600]{0,1:T(8,128)(2,1)} collective-permute-done((bf16[128,1600]{0,1:T(8,128)(2,1)}, bf16[128,1600]{0,1:T(8,128)(2,1)}, u32[]{:S(2)}, u32[]{:S(2)}) %collective-permute-start.60) | collective-permute-done | bytes 409632 | tf_op jit(solution)/shard_map/ppermute | solution.py:400
  458.9 13.4 %collective-permute-done.113.refs_5_ = bf16[200,1600]{1,0:T(8,128)(2,1)} collective-permute-done((bf16[200,1600]{1,0:T(8,128)(2,1)}, bf16[200,1600]{1,0:T(8,128)(2,1)}, u32[]{:S(2)}, u32[]{:S(2)}) %collective-permute-start.113) | collective-permute-done | bytes 640032 | tf_op jit(solution)/shard_map/ppermute | solution.py:400
  479.2 6.7 collective-permute-done.111.refs_3_
  493.9 25.0 %collective-permute-done.97 = bf16[400,800]{1,0:T(8,128)(2,1)S(1)} collective-permute-done((bf16[400,800]{1,0:T(8,128)(2,1)}, bf16[400,800]{1,0:T(8,128)(2,1)S(1)}, u32[]{:S(2)}, u32[]{:S(2)}) %collective-permute-start.97) | collective-permute-done | bytes 640032 | tf_op jit(solution)/shard_map/ppermute | solution.py:400
  524.1 12.4 %collective-permute-done.64 = f32[4,4800]{1,0:T(4,128)S(1)} collective-permute-done((f32[4,4800]{1,0:T(4,128)S(1)}, f32[4,4800]{1,0:T(4,128)S(1)}, u32[]{:S(2)}, u32[]{:S(2)}) %collective-permute-start.64) | collective-permute-done | bytes 76832 | tf_op jit(solution)/shard_map/ppermute | solution.py:400
  536.5 14.4 %collective-permute-start.102 = (bf16[400,800]{1,0:T(8,128)(2,1)S(1)}, bf16[400,800]{1,0:T(8,128)(2,1)S(1)}, u32[]{:S(2)}, u32[]{:S(2)}) collective-permute-start(bf16[400,800]{1,0:T(8,128)(2,1)S(1)} %fusion.30.refs_0_), channel_id=1, source_target_pairs={{0,16},{1,17},{2,18},{3,19},{4,20},{5,21},{6,22},{7,23},{8,24},{9,... | collective-permute-start | bytes 1920008 | tf_op jit(solution)/shard_map/ppermute | solution.py:400
  553.5 7.3 %shard_map.232 = f32[1600,1600]{1,0:T(8,128)} custom-call(s32[8]{0:T(128)S(1)} %stack.180.numbers, bf16[200,1600]{1,0:T(8,128)(2,1)S(1)} %add_convert_fusion.6.refs_0_, bf16[200,1600]{1,0:T(8,128)(2,1)} %collective-permute-done.109.refs_1_, bf16[200,1600]{1,0:T(8,128)(2,1)} %collective-permute-done.110.refs_2_, bf16[200,1600]{1,0:T(8,128)(2,1)S(1)} %copy-done.6, ...), custom_call_target="tpu_custom_call" | custom-call | bytes 15360000 | tf_op jit(solution)/shard_map/pallas_call | solution.py:233
  563.8 20.9 %collective-permute-done.102.refs_4_ = bf16[400,800]{1,0:T(8,128)(2,1)S(1)} collective-permute-done((bf16[400,800]{1,0:T(8,128)(2,1)S(1)}, bf16[400,800]{1,0:T(8,128)(2,1)S(1)}, u32[]{:S(2)}, u32[]{:S(2)}) %collective-permute-start.102) | collective-permute-done | bytes 640032 | tf_op jit(solution)/shard_map/ppermute | solution.py:400
  593.2 40.7 %collective-permute-done.65 = f32[4,4800]{1,0:T(4,128)S(1)} collective-permute-done((f32[4,4800]{1,0:T(4,128)S(1)}, f32[4,4800]{1,0:T(4,128)S(1)}, u32[]{:S(2)}, u32[]{:S(2)}) %collective-permute-start.65) | collective-permute-done | bytes 76832 | tf_op jit(solution)/shard_map/ppermute | solution.py:400
  636.0 6.8 shard_map.231
  654.5 7.1 collective-permute-done.67
  661.5 13.5 %collective-permute-done.74.refs_4_ = bf16[400,768]{1,0:T(8,128)(2,1)S(1)} collective-permute-done((bf16[400,768]{1,0:T(8,128)(2,1)S(1)}, bf16[400,768]{1,0:T(8,128)(2,1)S(1)}, u32[]{:S(2)}, u32[]{:S(2)}) %collective-permute-start.74) | collective-permute-done | bytes 614432 | tf_op jit(solution)/shard_map/ppermute | solution.py:400
  678.5 6.0 collective-permute-done.84
  702.1 5.9 collective-permute-done.88.refs_4_
  (546 shorter events, 342.7 us)
Async XLA Ops:
  8.1 87.1 %collective-permute-start.40 = (bf16[128,1600]{0,1:T(8,128)(2,1)}, bf16[128,1600]{0,1:T(8,128)(2,1)}, u32[]{:S(2)}, u32[]{:S(2)}) collective-permute-start(bf16[128,1600]{0,1:T(8,128)(2,1)} %bitcast.120), channel_id=1, source_target_pairs={{0,6},{1,7},{2,4},{3,5},{4,2},{5,3},{6,0},{7,1},{8,14},{9,15},{10,... | collective-permute-start | bytes 1228808 | tf_op jit(solution)/shard_map/ppermute | solution.py:400
  9.6 113.8 %collective-permute-start.39 = (bf16[128,1600]{0,1:T(8,128)(2,1)}, bf16[128,1600]{0,1:T(8,128)(2,1)}, u32[]{:S(2)}, u32[]{:S(2)}) collective-permute-start(bf16[128,1600]{0,1:T(8,128)(2,1)} %bitcast.121), channel_id=1, source_target_pairs={{0,4},{1,5},{2,6},{3,7},{4,0},{5,1},{6,2},{7,3},{8,12},{9,13},{10,... | collective-permute-start | bytes 1228808 | tf_op jit(solution)/shard_map/ppermute | solution.py:400
  9.7 36.3 %collective-permute-start.38 = (bf16[128,1600]{0,1:T(8,128)(2,1)}, bf16[128,1600]{0,1:T(8,128)(2,1)S(1)}, u32[]{:S(2)}, u32[]{:S(2)}) collective-permute-start(bf16[128,1600]{0,1:T(8,128)(2,1)} %bitcast.122), channel_id=1, source_target_pairs={{0,2},{1,3},{2,0},{3,1},{4,6},{5,7},{6,4},{7,5},{8,10},{9,11},{10,... | collective-permute-start | bytes 1228808 | tf_op jit(solution)/shard_map/ppermute | solution.py:400
  93.8 33.5 %collective-permute-start.41 = (bf16[128,1600]{0,1:T(8,128)(2,1)S(1)}, bf16[128,1600]{0,1:T(8,128)(2,1)S(1)}, u32[]{:S(2)}, u32[]{:S(2)}) collective-permute-start(bf16[128,1600]{0,1:T(8,128)(2,1)S(1)} %bitcast.123), channel_id=1, source_target_pairs={{0,1},{1,0},{2,3},{3,2},{4,5},{5,4},{6,7},{7,6},{8,9},{9,8},{10,11... | collective-permute-start | bytes 1228808 | tf_op jit(solution)/shard_map/ppermute | solution.py:400
  94.4 60.5 %collective-permute-start.20 = (bf16[400,1600]{1,0:T(8,128)(2,1)}, bf16[400,1600]{1,0:T(8,128)(2,1)S(1)}, u32[]{:S(2)}, u32[]{:S(2)}) collective-permute-start(bf16[400,1600]{1,0:T(8,128)(2,1)} %refs_0_.1), channel_id=1, source_target_pairs={{0,1},{1,0},{2,3},{3,2},{4,5},{5,4},{6,7},{7,6},{8,9},{9,8},{10,11... | collective-permute-start | bytes 3840008 | tf_op jit(solution)/shard_map/ppermute | solution.py:400
  112.8 42.6 %collective-permute-start.22 = (bf16[400,1600]{1,0:T(8,128)(2,1)S(1)}, bf16[400,1600]{1,0:T(8,128)(2,1)S(1)}, u32[]{:S(2)}, u32[]{:S(2)}) collective-permute-start(bf16[400,1600]{1,0:T(8,128)(2,1)S(1)} %collective-permute-done.21.refs_2_), channel_id=1, source_target_pairs={{0,1},{1,0},{2,3},{3,2},{4,5},{5,4},{6,7},{7,6},{8,9},{9,8},{10,11... | collective-permute-start | bytes 3840008 | tf_op jit(solution)/shard_map/ppermute | solution.py:400
  210.2 32.9 %collective-permute-start.108 = (bf16[200,1600]{1,0:T(8,128)(2,1)S(1)}, bf16[200,1600]{1,0:T(8,128)(2,1)S(1)}, u32[]{:S(2)}, u32[]{:S(2)}) collective-permute-start(bf16[200,1600]{1,0:T(8,128)(2,1)S(1)} %get-tuple-element.82), channel_id=1, source_target_pairs={{0,24},{1,25},{2,26},{3,27},{4,28},{5,29},{6,30},{7,31},{8,16},{9,... | collective-permute-start | bytes 1920008 | tf_op jit(solution)/shard_map/ppermute | solution.py:400
  216.0 62.3 %collective-permute-start.45 = (bf16[512,1600]{0,1:T(8,128)(2,1)}, bf16[512,1600]{0,1:T(8,128)(2,1)}, u32[]{:S(2)}, u32[]{:S(2)}) collective-permute-start(bf16[512,1600]{0,1:T(8,128)(2,1)} %convolution_convert_fusion.4), channel_id=1, source_target_pairs={{0,1},{1,0},{2,3},{3,2},{4,5},{5,4},{6,7},{7,6},{8,9},{9,8},{10,11... | collective-permute-start | bytes 4915208 | tf_op jit(solution)/shard_map/ppermute | solution.py:400
  216.0 55.1 %collective-permute-start.107 = (bf16[200,1600]{1,0:T(8,128)(2,1)}, bf16[200,1600]{1,0:T(8,128)(2,1)}, u32[]{:S(2)}, u32[]{:S(2)}) collective-permute-start(bf16[200,1600]{1,0:T(8,128)(2,1)} %get-tuple-element.83), channel_id=1, source_target_pairs={{0,16},{1,17},{2,18},{3,19},{4,20},{5,21},{6,22},{7,23},{8,24},{9,... | collective-permute-start | bytes 1920008 | tf_op jit(solution)/shard_map/ppermute | solution.py:400
  226.7 46.5 %collective-permute-start.93 = (bf16[400,800]{1,0:T(8,128)(2,1)}, bf16[400,800]{1,0:T(8,128)(2,1)}, u32[]{:S(2)}, u32[]{:S(2)}) collective-permute-start(bf16[400,800]{1,0:T(8,128)(2,1)} %get-tuple-element.79), channel_id=1, source_target_pairs={{0,2},{1,3},{2,0},{3,1},{4,6},{5,7},{6,4},{7,5},{8,10},{9,11},{10,... | collective-permute-start | bytes 1920008 | tf_op jit(solution)/shard_map/ppermute | solution.py:400
  227.4 45.8 %collective-permute-start.92 = (bf16[400,800]{1,0:T(8,128)(2,1)}, bf16[400,800]{1,0:T(8,128)(2,1)}, u32[]{:S(2)}, u32[]{:S(2)}) collective-permute-start(bf16[400,800]{1,0:T(8,128)(2,1)} %get-tuple-element.80), channel_id=1, source_target_pairs={{0,1},{1,0},{2,3},{3,2},{4,5},{5,4},{6,7},{7,6},{8,9},{9,8},{10,11... | collective-permute-start | bytes 1920008 | tf_op jit(solution)/shard_map/ppermute | solution.py:400
  354.0 62.3 %collective-permute-start.114 = (bf16[200,1600]{1,0:T(8,128)(2,1)S(1)}, bf16[200,1600]{1,0:T(8,128)(2,1)}, u32[]{:S(2)}, u32[]{:S(2)}) collective-permute-start(bf16[200,1600]{1,0:T(8,128)(2,1)S(1)} %add_convert_fusion.6.refs_0_), channel_id=1, source_target_pairs={{0,24},{1,25},{2,26},{3,27},{4,28},{5,29},{6,30},{7,31},{8,16},{9,... | collective-permute-start | bytes 1920008 | tf_op jit(solution)/shard_map/ppermute | solution.py:400
  356.6 63.8 %collective-permute-start.112 = (bf16[200,1600]{1,0:T(8,128)(2,1)S(1)}, bf16[200,1600]{1,0:T(8,128)(2,1)}, u32[]{:S(2)}, u32[]{:S(2)}) collective-permute-start(bf16[200,1600]{1,0:T(8,128)(2,1)S(1)} %add_convert_fusion.6.refs_0_), channel_id=1, source_target_pairs={{0,16},{1,17},{2,18},{3,19},{4,20},{5,21},{6,22},{7,23},{8,24},{9,... | collective-permute-start | bytes 1920008 | tf_op jit(solution)/shard_map/ppermute | solution.py:400
  381.0 44.6 %collective-permute-start.56 = (bf16[128,1600]{0,1:T(8,128)(2,1)}, bf16[128,1600]{0,1:T(8,128)(2,1)}, u32[]{:S(2)}, u32[]{:S(2)}) collective-permute-start(bf16[128,1600]{0,1:T(8,128)(2,1)} %convolution_convert_fusion.11), channel_id=1, source_target_pairs={{0,4},{1,5},{2,6},{3,7},{4,0},{5,1},{6,2},{7,3},{8,12},{9,13},{10,... | collective-permute-start | bytes 1228808 | tf_op jit(solution)/shard_map/ppermute | solution.py:400
  420.4 52.6 %collective-permute-start.79 = (bf16[400,1600]{1,0:T(8,128)(2,1)}, bf16[400,1600]{1,0:T(8,128)(2,1)}, u32[]{:S(2)}, u32[]{:S(2)}) collective-permute-start(bf16[400,1600]{1,0:T(8,128)(2,1)} %get-tuple-element.73), channel_id=1, source_target_pairs={{0,1},{1,0},{2,3},{3,2},{4,5},{5,4},{6,7},{7,6},{8,9},{9,8},{10,11... | collective-permute-start | bytes 3840008 | tf_op jit(solution)/shard_map/ppermute | solution.py:400
  453.4 33.3 %collective-permute-start.96 = (bf16[400,800]{1,0:T(8,128)(2,1)}, bf16[400,800]{1,0:T(8,128)(2,1)S(1)}, u32[]{:S(2)}, u32[]{:S(2)}) collective-permute-start(bf16[400,800]{1,0:T(8,128)(2,1)} %get-tuple-element.74), channel_id=1, source_target_pairs={{0,8},{1,9},{2,10},{3,11},{4,12},{5,13},{6,14},{7,15},{8,0},{9,1},... | collective-permute-start | bytes 1920008 | tf_op jit(solution)/shard_map/ppermute | solution.py:400
  456.0 33.8 %collective-permute-start.98 = (bf16[400,800]{1,0:T(8,128)(2,1)}, bf16[400,800]{1,0:T(8,128)(2,1)S(1)}, u32[]{:S(2)}, u32[]{:S(2)}) collective-permute-start(bf16[400,800]{1,0:T(8,128)(2,1)} %get-tuple-element.75), channel_id=1, source_target_pairs={{0,24},{1,25},{2,26},{3,27},{4,28},{5,29},{6,30},{7,31},{8,16},{9,... | collective-permute-start | bytes 1920008 | tf_op jit(solution)/shard_map/ppermute | solution.py:400
  473.1 45.9 %collective-permute-start.97 = (bf16[400,800]{1,0:T(8,128)(2,1)}, bf16[400,800]{1,0:T(8,128)(2,1)S(1)}, u32[]{:S(2)}, u32[]{:S(2)}) collective-permute-start(bf16[400,800]{1,0:T(8,128)(2,1)} %get-tuple-element.76), channel_id=1, source_target_pairs={{0,16},{1,17},{2,18},{3,19},{4,20},{5,21},{6,22},{7,23},{8,24},{9,... | collective-permute-start | bytes 1920008 | tf_op jit(solution)/shard_map/ppermute | solution.py:400
  486.7 100.0 %collective-permute-start.78 = (bf16[400,1600]{1,0:T(8,128)(2,1)}, bf16[400,1600]{1,0:T(8,128)(2,1)}, u32[]{:S(2)}, u32[]{:S(2)}) collective-permute-start(bf16[400,1600]{1,0:T(8,128)(2,1)} %get-tuple-element.72), channel_id=1, source_target_pairs={{0,1},{1,0},{2,3},{3,2},{4,5},{5,4},{6,7},{7,6},{8,9},{9,8},{10,11... | collective-permute-start | bytes 3840008 | tf_op jit(solution)/shard_map/ppermute | solution.py:400
  486.7 35.0 %collective-permute-start.68 = (bf16[400,768]{1,0:T(8,128)(2,1)}, bf16[400,768]{1,0:T(8,128)(2,1)}, u32[]{:S(2)}, u32[]{:S(2)}) collective-permute-start(bf16[400,768]{1,0:T(8,128)(2,1)} %get-tuple-element.84), channel_id=1, source_target_pairs={{0,1},{1,0},{2,3},{3,2},{4,5},{5,4},{6,7},{7,6},{8,9},{9,8},{10,11... | collective-permute-start | bytes 1843208 | tf_op jit(solution)/shard_map/ppermute | solution.py:400
  489.8 97.7 %collective-permute-start.80 = (bf16[400,1600]{1,0:T(8,128)(2,1)}, bf16[400,1600]{1,0:T(8,128)(2,1)}, u32[]{:S(2)}, u32[]{:S(2)}) collective-permute-start(bf16[400,1600]{1,0:T(8,128)(2,1)} %add_convert_fusion.4), channel_id=1, source_target_pairs={{0,2},{1,3},{2,0},{3,1},{4,6},{5,7},{6,4},{7,5},{8,10},{9,11},{10,... | collective-permute-start | bytes 3840008 | tf_op jit(solution)/shard_map/ppermute | solution.py:400
  493.2 57.6 %collective-permute-start.70 = (bf16[400,768]{1,0:T(8,128)(2,1)}, bf16[400,768]{1,0:T(8,128)(2,1)}, u32[]{:S(2)}, u32[]{:S(2)}) collective-permute-start(bf16[400,768]{1,0:T(8,128)(2,1)} %add_convert_fusion.8), channel_id=1, source_target_pairs={{0,2},{1,3},{2,0},{3,1},{4,6},{5,7},{6,4},{7,5},{8,10},{9,11},{10,... | collective-permute-start | bytes 1843208 | tf_op jit(solution)/shard_map/ppermute | solution.py:400
  521.8 40.8 %collective-permute-start.104 = (bf16[400,800]{1,0:T(8,128)(2,1)S(1)}, bf16[400,800]{1,0:T(8,128)(2,1)S(1)}, u32[]{:S(2)}, u32[]{:S(2)}) collective-permute-start(bf16[400,800]{1,0:T(8,128)(2,1)S(1)} %fusion.30.refs_0_), channel_id=1, source_target_pairs={{0,24},{1,25},{2,26},{3,27},{4,28},{5,29},{6,30},{7,31},{8,16},{9,... | collective-permute-start | bytes 1920008 | tf_op jit(solution)/shard_map/ppermute | solution.py:400
  536.5 48.2 %collective-permute-start.102 = (bf16[400,800]{1,0:T(8,128)(2,1)S(1)}, bf16[400,800]{1,0:T(8,128)(2,1)S(1)}, u32[]{:S(2)}, u32[]{:S(2)}) collective-permute-start(bf16[400,800]{1,0:T(8,128)(2,1)S(1)} %fusion.30.refs_0_), channel_id=1, source_target_pairs={{0,16},{1,17},{2,18},{3,19},{4,20},{5,21},{6,22},{7,23},{8,24},{9,... | collective-permute-start | bytes 1920008 | tf_op jit(solution)/shard_map/ppermute | solution.py:400
  550.8 34.6 %collective-permute-start.100 = (bf16[400,800]{1,0:T(8,128)(2,1)S(1)}, bf16[400,800]{1,0:T(8,128)(2,1)}, u32[]{:S(2)}, u32[]{:S(2)}) collective-permute-start(bf16[400,800]{1,0:T(8,128)(2,1)S(1)} %fusion.30.refs_0_), channel_id=1, source_target_pairs={{0,8},{1,9},{2,10},{3,11},{4,12},{5,13},{6,14},{7,15},{8,0},{9,1},... | collective-permute-start | bytes 1920008 | tf_op jit(solution)/shard_map/ppermute | solution.py:400
  584.7 50.1 %collective-permute-start.105 = (bf16[400,800]{1,0:T(8,128)(2,1)S(1)}, bf16[400,800]{1,0:T(8,128)(2,1)S(1)}, u32[]{:S(2)}, u32[]{:S(2)}) collective-permute-start(bf16[400,800]{1,0:T(8,128)(2,1)S(1)} %collective-permute-done.104.refs_6_), channel_id=1, source_target_pairs={{0,4},{1,5},{2,6},{3,7},{4,0},{5,1},{6,2},{7,3},{8,12},{9,13},{10,... | collective-permute-start | bytes 1920008 | tf_op jit(solution)/shard_map/ppermute | solution.py:400
  585.5 50.5 %collective-permute-start.103 = (bf16[400,800]{1,0:T(8,128)(2,1)S(1)}, bf16[400,800]{1,0:T(8,128)(2,1)S(1)}, u32[]{:S(2)}, u32[]{:S(2)}) collective-permute-start(bf16[400,800]{1,0:T(8,128)(2,1)S(1)} %collective-permute-done.102.refs_4_), channel_id=1, source_target_pairs={{0,4},{1,5},{2,6},{3,7},{4,0},{5,1},{6,2},{7,3},{8,12},{9,13},{10,... | collective-permute-start | bytes 1920008 | tf_op jit(solution)/shard_map/ppermute | solution.py:400
  586.7 49.3 %collective-permute-start.101 = (bf16[400,800]{1,0:T(8,128)(2,1)}, bf16[400,800]{1,0:T(8,128)(2,1)S(1)}, u32[]{:S(2)}, u32[]{:S(2)}) collective-permute-start(bf16[400,800]{1,0:T(8,128)(2,1)} %collective-permute-done.100.refs_2_), channel_id=1, source_target_pairs={{0,4},{1,5},{2,6},{3,7},{4,0},{5,1},{6,2},{7,3},{8,12},{9,13},{10,... | collective-permute-start | bytes 1920008 | tf_op jit(solution)/shard_map/ppermute | solution.py:400
  587.5 46.4 %collective-permute-start.65 = (f32[4,4800]{1,0:T(4,128)S(1)}, f32[4,4800]{1,0:T(4,128)S(1)}, u32[]{:S(2)}, u32[]{:S(2)}) collective-permute-start(f32[4,4800]{1,0:T(4,128)S(1)} %add.404), channel_id=1, source_target_pairs={{0,4},{1,5},{2,6},{3,7},{4,0},{5,1},{6,2},{7,3},{8,12},{9,13},{10,... | collective-permute-start | bytes 230408 | tf_op jit(solution)/shard_map/ppermute | solution.py:400
  591.8 56.0 %collective-permute-start.76 = (bf16[400,768]{1,0:T(8,128)(2,1)S(1)}, bf16[400,768]{1,0:T(8,128)(2,1)S(1)}, u32[]{:S(2)}, u32[]{:S(2)}) collective-permute-start(bf16[400,768]{1,0:T(8,128)(2,1)S(1)} %add_convert_fusion.7.refs_0_), channel_id=1, source_target_pairs={{0,24},{1,25},{2,26},{3,27},{4,28},{5,29},{6,30},{7,31},{8,16},{9,... | collective-permute-start | bytes 1843208 | tf_op jit(solution)/shard_map/ppermute | solution.py:400
  647.8 45.6 %collective-permute-start.71 = (bf16[400,768]{1,0:T(8,128)(2,1)S(1)}, bf16[400,768]{1,0:T(8,128)(2,1)S(1)}, u32[]{:S(2)}, u32[]{:S(2)}) collective-permute-start(bf16[400,768]{1,0:T(8,128)(2,1)S(1)} %add_convert_fusion.7.refs_0_), channel_id=1, source_target_pairs={{0,4},{1,5},{2,6},{3,7},{4,0},{5,1},{6,2},{7,3},{8,12},{9,13},{10,... | collective-permute-start | bytes 1843208 | tf_op jit(solution)/shard_map/ppermute | solution.py:400
  653.5 40.8 %collective-permute-start.77 = (bf16[400,768]{1,0:T(8,128)(2,1)S(1)}, bf16[400,768]{1,0:T(8,128)(2,1)S(1)}, u32[]{:S(2)}, u32[]{:S(2)}) collective-permute-start(bf16[400,768]{1,0:T(8,128)(2,1)S(1)} %collective-permute-done.76.refs_6_), channel_id=1, source_target_pairs={{0,4},{1,5},{2,6},{3,7},{4,0},{5,1},{6,2},{7,3},{8,12},{9,13},{10,... | collective-permute-start | bytes 1843208 | tf_op jit(solution)/shard_map/ppermute | solution.py:400
  (174 other events, 3195.3 us)

commit v2 on v1

v2 whole, which is shorter than its diff:
```python
import functools
import math

import jax
import jax.numpy as jnp
from jax import lax
from jax.experimental import pallas as pl
from jax.experimental.layout import Layout, with_layout_constraint
from jax.experimental.pallas import tpu as pltpu
from jax.sharding import PartitionSpec as P

AXES = ("ctx", "wt")
F32 = jnp.float32
BF16 = jnp.bfloat16


def standardize(values):
    centred = values - jnp.mean(values, axis=-1, keepdims=True)
    scale = lax.rsqrt(jnp.mean(centred * centred, axis=-1, keepdims=True) + 1e-05)
    return (centred * scale, scale)


def finish_norm(scaled, normed, scale):
    inner = (
        scaled
        - jnp.mean(scaled, axis=-1, keepdims=True)
        - normed * jnp.mean(scaled * normed, axis=-1, keepdims=True)
    )
    return scale * inner


def gelu(values):
    return (
        0.5
        * values
        * (1.0 + jnp.tanh(0.7978845608028654 * (values + 0.044715 * values * values * values)))
    )


def dot(left, right):
    return jnp.dot(left, right, preferred_element_type=F32)


def over_rows(left, right):
    return lax.dot_general(left, right, (((0,), (0,)), ((), ())), preferred_element_type=F32)


def by_transpose(left, right):
    return lax.dot_general(left, right, (((1,), (1,)), ((), ())), preferred_element_type=F32)


def add_low(left, right):
    return (left.astype(F32) + right.astype(F32)).astype(BF16)


UNROLLED = 1024
BUMP = 2
TURNS = "mdmuodmpuoudmupdgquqpqgudpqppuqgpp"


def for_tiles(one, length, tile, key_axis):
    if length <= UNROLLED:
        shape = (tile, tile)
        key = lax.broadcasted_iota(jnp.int32, shape, key_axis)
        query = lax.broadcasted_iota(jnp.int32, shape, 1 - key_axis)
        for turn in range(length // tile):
            one(turn, turn * tile, pl.ds(turn * tile, tile), key <= query)
        return

    def turn_of(turn, carry):
        shape = (tile, length) if key_axis else (length, tile)
        key = lax.broadcasted_iota(jnp.int32, shape, key_axis)
        query = lax.broadcasted_iota(jnp.int32, shape, 1 - key_axis)
        one(turn, 0, pl.ds(0, length), key <= query + turn * tile)
        return carry

    lax.fori_loop(0, length // tile, turn_of, 0)


def attn_forward_kernel(tile, block, place_ref, slots_ref, qkv_ref, out_ref, lse_ref, qs, ks, vs, os):
    length, wide = os.shape

    for i in range(length // block):
        here = pl.ds(pl.multiple_of(place_ref[i] * block, block), block)
        there = slice(i * block, (i + 1) * block)
        qs[here, :] = qkv_ref[there, 0:wide] * 0.125
        ks[here, :] = qkv_ref[there, wide : 2 * wide]
        vs[here, :] = qkv_ref[there, 2 * wide : 3 * wide]
    lane = lax.broadcasted_iota(jnp.int32, (tile, 128), 1)

    def one(turn, before, near, allowed):
        mine = pl.ds(turn * tile, tile)
        stats = jnp.zeros((tile, 128), F32)
        for pair in range(wide // 128):
            cols = slice(pair * 128, (pair + 1) * 128)
            q = qs[mine, cols]
            halves = []
            for half in range(2):
                keep = (lane >= 64) if half else (lane < 64)
                qh = jnp.where(keep, q, jnp.zeros_like(q))
                edge = by_transpose(qh, ks[near, cols])
                edge = jnp.where(allowed, edge, -1e30)
                most = jnp.max(edge, axis=1, keepdims=True)
                if before:
                    past = by_transpose(qh, ks[0:before, cols])
                    most = jnp.maximum(most, jnp.max(past, axis=1, keepdims=True))
                edge = jnp.exp(edge - most)
                total = jnp.sum(edge, axis=1, keepdims=True)
                acc = dot(edge.astype(BF16), vs[near, cols])
                if before:
                    past = jnp.exp(past - most)
                    total = total + jnp.sum(past, axis=1, keepdims=True)
                    acc = acc + dot(past.astype(BF16), vs[0:before, cols])
                halves.append(acc / total)
                stats = jnp.where(lane == 2 * pair + half, most + jnp.log(total), stats)
            os[mine, cols] = jnp.where(lane < 64, halves[0], halves[1]).astype(BF16)
        lse_ref[mine, :] = stats

    for_tiles(one, length, tile, 1)

    for i in range(length // block):
        here = pl.ds(pl.multiple_of(slots_ref[i] * block, block), block)
        out_ref[i // 2, (i % 2) * block : (i % 2 + 1) * block, :] = os[here, :]


def attn_backward_kernel(
    tile, block, place_ref, slots_ref, qkv_ref, lse_ref, grad_ref, out_ref, qs, ks, vs, gs, dq, dk, dv
):
    length, wide = gs.shape
    for i in range(length // block):
        here = pl.ds(pl.multiple_of(place_ref[i] * block, block), block)
        there = slice(i * block, (i + 1) * block)
        qs[here, :] = qkv_ref[there, 0:wide] * 0.125
        ks[here, :] = qkv_ref[there, wide : 2 * wide]
        vs[here, :] = qkv_ref[there, 2 * wide : 3 * wide]
        far = pl.ds(pl.multiple_of(slots_ref[i] * block, block), block)
        gs[far, :] = grad_ref[i // 2, (i % 2) * block : (i % 2 + 1) * block, :]
    lane = lax.broadcasted_iota(jnp.int32, (tile, 128), 1)
    alone = length <= UNROLLED
    if not alone:
        dk[...] = jnp.zeros_like(dk)
        dv[...] = jnp.zeros_like(dv)

    def one(turn, before, near, allowed):
        mine = pl.ds(turn * tile, tile)
        lse = lse_ref[mine, :].T
        for pair in range(wide // 128):
            cols = slice(pair * 128, (pair + 1) * 128)
            q, g = qs[mine, cols], gs[mine, cols]
            halves = []
            for half in range(2):
                keep = (lane >= 64) if half else (lane < 64)
                qh = jnp.where(keep, q, jnp.zeros_like(q))
                gh = jnp.where(keep, g, jnp.zeros_like(g))
                row = lse[2 * pair + half : 2 * pair + half + 1, :]
                edge_p = by_transpose(ks[near, cols], qh)
                edge_p = jnp.where(allowed, jnp.exp(edge_p - row), 0.0)
                edge_t = edge_p * by_transpose(vs[near, cols], gh)
                delta = jnp.sum(edge_t, axis=0, keepdims=True)
                if before:
                    past_p = jnp.exp(by_transpose(ks[0:before, cols], qh) - row)
                    past_t = past_p * by_transpose(vs[0:before, cols], gh)
                    delta = delta + jnp.sum(past_t, axis=0, keepdims=True)
                edge_s = (edge_t - edge_p * delta).astype(BF16)
                own_v = dot(edge_p.astype(BF16), gh)
                own_k = dot(edge_s, qh)
                if half or not alone:
                    dv[near, cols] += own_v
                    dk[near, cols] += own_k
                else:
                    dv[near, cols] = own_v
                    dk[near, cols] = own_k
                acc = over_rows(edge_s, ks[near, cols])
                if before:
                    past_s = (past_t - past_p * delta).astype(BF16)
                    dv[0:before, cols] += dot(past_p.astype(BF16), gh)
                    dk[0:before, cols] += dot(past_s, qh)
                    acc = acc + over_rows(past_s, ks[0:before, cols])
                halves.append(acc)
            dq[mine, cols] = (jnp.where(lane < 64, halves[0], halves[1]) * 0.125).astype(BF16)

    for_tiles(one, length, tile, 0)

    for i in range(length // block):
        here = pl.ds(pl.multiple_of(place_ref[i] * block, block), block)
        there = slice(i * block, (i + 1) * block)
        out_ref[there, 0:wide] = dq[here, :]
        out_ref[there, wide : 2 * wide] = dk[here, :].astype(BF16)
        out_ref[there, 2 * wide : 3 * wide] = dv[here, :].astype(BF16)


SMEM = pl.BlockSpec(memory_space=pltpu.SMEM)
VMEM = pl.BlockSpec(memory_space=pltpu.VMEM)
LIMIT = 48 * 1024 * 1024


def attn_forward(qkv, place, slots, block, tile):
    length, wide = qkv.shape[0], qkv.shape[1] // 3
    return pl.pallas_call(
        functools.partial(attn_forward_kernel, tile, block),
        out_shape=(
            jax.ShapeDtypeStruct((length // (2 * block), 2 * block, wide), BF16),
            jax.ShapeDtypeStruct((length, 128), F32),
        ),
        in_specs=[SMEM, SMEM, VMEM],
        out_specs=(VMEM, VMEM),
        scratch_shapes=[pltpu.VMEM((length, wide), BF16)] * 4,
        compiler_params=pltpu.CompilerParams(vmem_limit_bytes=LIMIT),
        cost_estimate=pl.CostEstimate(
            flops=4 * length * length * wide,
            bytes_accessed=length * wide * 10,
            transcendentals=length * length * wide // 128,
        ),
    )(place, slots, qkv)


def attn_backward(qkv, grads, lse, place, slots, block, tile):
    length, wide = qkv.shape[0], qkv.shape[1] // 3
    return pl.pallas_call(
        functools.partial(attn_backward_kernel, tile, block),
        out_shape=jax.ShapeDtypeStruct((length, 3 * wide), BF16),
        in_specs=[SMEM, SMEM, VMEM, VMEM, VMEM],
        out_specs=VMEM,
        scratch_shapes=[pltpu.VMEM((length, wide), BF16)] * 5
        + [pltpu.VMEM((length, wide), F32)] * 2,
        compiler_params=pltpu.CompilerParams(vmem_limit_bytes=LIMIT),
        cost_estimate=pl.CostEstimate(
            flops=10 * length * length * wide,
            bytes_accessed=length * wide * 16,
            transcendentals=length * length * wide // 128,
        ),
    )(place, slots, qkv, lse, grads)


def rearrange(kernel, outs, numbers, arrays, scratch=()):
    size = sum(math.prod(o.shape) * o.dtype.itemsize for o in (*outs, *arrays))
    return pl.pallas_call(
        kernel,
        out_shape=tuple(jax.ShapeDtypeStruct(o.shape, o.dtype) for o in outs),
        in_specs=[SMEM] + [VMEM] * len(arrays),
        out_specs=(VMEM,) * len(outs),
        scratch_shapes=list(scratch),
        compiler_params=pltpu.CompilerParams(vmem_limit_bytes=LIMIT),
        cost_estimate=pl.CostEstimate(flops=0, bytes_accessed=size, transcendentals=0),
    )(jnp.stack(numbers).astype(jnp.int32), *arrays)


def shaped(shape, dtype=BF16):
    return jax.ShapeDtypeStruct(shape, dtype)


class Heads:
    def __init__(self, n, width):
        self.n, self.width = n, width
        self.full, self.rest = width // 128, width % 128
        self.slots = -(-(self.full + (self.rest > 0)) // n)
        self.wide = 128 * self.slots

    def pick_kernel(self, numbers, from_ref, more_ref, out_ref):
        rows = from_ref.shape[0]
        out_ref[rows:, :] = more_ref[...]
        out_ref = out_ref.at[:rows]
        for t in range(3):
            base = t * self.width
            first, off = base // 128, base % 128
            for j in range(self.slots):
                to = slice((t * self.slots + j) * 128, (t * self.slots + j + 1) * 128)
                p = j * self.n + numbers[0]

                @pl.when(p < self.full)
                def _():
                    start = pl.multiple_of((first + p) * 128, 128)
                    if off:
                        out_ref[:, to] = from_ref[:, pl.ds(start, 256)][:, off : off + 128]
                    else:
                        out_ref[:, to] = from_ref[:, pl.ds(start, 128)]

                @pl.when(p >= self.full)
                def _():
                    out_ref[:, to] = jnp.zeros((rows, 128), out_ref.dtype)

                if self.rest:
                    at = base + self.full * 128

                    @pl.when(p == self.full)
                    def _():
                        out_ref[:, to.start : to.start + self.rest] = from_ref[
                            :, at : at + self.rest
                        ]

    def pick(self, weight, more, c):
        out = shaped((weight.shape[0] + more.shape[0], 3 * self.wide))
        return rearrange(self.pick_kernel, [out], [c], [weight, more])[0]

    def join_kernel(self, from_ref, out_ref):
        for p in range(self.full + (self.rest > 0)):
            size = min(128, self.width - p * 128)
            j, owner = divmod(p, self.n)
            out_ref[:, p * 128 : p * 128 + size] = from_ref[owner, :, j * 128 : j * 128 + size]

    def split_kernel(self, from_ref, out_ref):
        for p in range(self.n * self.slots):
            size = max(0, min(128, self.width - p * 128))
            j, owner = divmod(p, self.n)
            if size:
                out_ref[owner, :, j * 128 : j * 128 + size] = from_ref[:, p * 128 : p * 128 + size]
            if size < 128:
                out_ref[owner, :, j * 128 + size : (j + 1) * 128] = jnp.zeros(
                    (out_ref.shape[1], 128 - size), out_ref.dtype
                )

    def turned(self, kernel, value, shape):
        return pl.pallas_call(
            kernel,
            out_shape=shaped(shape),
            in_specs=[VMEM],
            out_specs=VMEM,
            cost_estimate=pl.CostEstimate(
                flops=0, bytes_accessed=4 * math.prod(shape), transcendentals=0
            ),
        )(value)

    def join(self, blocks):
        return self.turned(self.join_kernel, blocks, (blocks.shape[1], self.width))

    def split(self, value):
        return self.turned(self.split_kernel, value, (self.n, value.shape[0], self.wide))

    def here(self, values, c):
        lead = values.shape[:-1]
        values = jnp.pad(values, [(0, 0)] * len(lead) + [(0, self.n * self.wide - self.width)])
        values = values.reshape(lead + (self.slots, self.n, 128))
        return lax.dynamic_index_in_dim(values, c, len(lead) + 1, False).reshape(
            lead + (self.wide,)
        )

    def back(self, values, c):
        lead = values.shape[:-1]
        zeros = jnp.zeros(lead + (self.slots, self.n, 128), values.dtype)
        values = values.reshape(lead + (self.slots, 1, 128))
        values = lax.dynamic_update_slice(zeros, values, (0,) * (len(lead) + 1) + (c, 0))
        return values.reshape(lead + (self.n * self.wide,))[..., : self.width]


def cut_kernel(per, numbers, from_ref, *outs):
    r = 0
    for out_ref in outs:
        for k in range(out_ref.shape[0]):
            for part in range(from_ref.shape[1] // per):

                @pl.when(numbers[r] == part)
                def _():
                    out_ref[k] = from_ref[:, part * per : (part + 1) * per]

            r += 1


def place_kernel(size, numbers, *refs):
    out_ref, r = refs[-1], 0
    for ref in refs[:-1]:
        for k in range(ref.shape[0]):
            to = pl.ds(pl.multiple_of(numbers[r] * size, 16), size)
            out_ref[to, :] = ref[k, :size, :]
            r += 1


def lay_kernel(plan, numbers, *refs):
    blocks, out_ref, held = refs[:-2], refs[-2], refs[-1]
    r = 0
    for ref in blocks:
        for k in range(ref.shape[0]):
            held[numbers[r]] = ref[k]
            r += 1
    for b, from_rows, from_cols, rows, cols in plan:
        out_ref[rows, cols] = held[b, from_rows, from_cols].astype(F32)


def lay(blocks, numbers, plan, shape):
    steps = [
        (b, slice(r, r + h), slice(q, q + v), slice(tr, tr + h), slice(tq, tq + v))
        for b, (r, q), (h, v), (tr, tq) in plan
    ]
    scratch = [pltpu.VMEM((len(numbers),) + blocks[0].shape[1:], BF16)]
    kernel = functools.partial(lay_kernel, steps)
    return rearrange(kernel, [shaped(shape, F32)], numbers, blocks, scratch)[0]


def by_rows(value):
    return with_layout_constraint(value, Layout(major_to_minor=tuple(range(value.ndim))))


def after(value, *others):
    return lax.optimization_barrier((value,) + others)[0]


def together(*values):
    return lax.optimization_barrier(values)


class Links:
    def __init__(self):
        self.n, self.m = lax.axis_size("ctx"), lax.axis_size("wt")
        self.c, self.w = lax.axis_index("ctx"), lax.axis_index("wt")
        self.bits = [1 << i for i in range(self.n.bit_length() - 1)]

    def swap(self, value, dc, dw):
        pairs = [
            (c * self.m + w, (c ^ dc) * self.m + (w ^ dw))
            for c in range(self.n)
            for w in range(self.m)
        ]
        return lax.ppermute(value, AXES, pairs)

    def core(self, value):
        return self.swap(value, 0, 1)

    def x(self, value):
        return self.swap(value, 0, 2)


    def gather_wt(self, value, *others):
        near = jnp.stack([value, after(self.x(value), *others)])
        return [near, self.core(near)]

    def trade_wt(self, own, near, far):
        (far,) = yield [(far, 0, 2)]
        (come,) = yield [(jnp.concatenate([near, far[1:]]), 0, 1)]
        return [own, far[:1], come]

    def sum_wt(self, near, far):
        (come,) = yield [(far, 0, 1)]
        (far,) = yield [(add_low(near[1], come[1]), 0, 2)]
        return add_low(add_low(near[0], come[0]), far)

    def rows_wt(self, blocks, size, numbers=(0, 2, 1, 3)):
        return rearrange(
            functools.partial(place_kernel, size),
            [shaped((self.m * size, blocks[0].shape[2]))],
            [self.w ^ r for r in numbers],
            blocks,
        )[0]


    def gather(self, value, bits):
        blocks = value[None]
        for bit in bits:
            (come,) = yield [(blocks, bit, 0)]
            if bit != bits[-1]:
                blocks = jnp.concatenate([blocks, come])
        return [blocks, come]

    def gathered(self, bits):
        found = [0]
        for bit in bits:
            found = found + [d | bit for d in found]
        return found

    def halving(self, bits):
        found = [0]
        for bit in reversed(bits):
            found = [d | bit for d in found] + found
        return found

    def halve(self, terms, bits):
        for bit in bits:
            half = terms.shape[0] // 2
            (come,) = yield [(terms[:half], bit, 0)]
            terms = add_low(terms[half:], come)
        return terms[0]


    def gather_plane(self, value):
        parts = [value, self.x(value), self.swap(value, 2, 0), self.swap(value, 2, 2)]
        return jnp.concatenate(parts + [self.core(part) for part in parts])

    def sum_plane(self, near, far):
        (come,) = yield [(far, 0, 1)]
        mine = add_low(near(), come)
        size = mine.shape[0] // 4
        parts = [mine[i * size : (i + 1) * size] for i in range(4)]
        come = yield [(parts[3], 2, 2), (parts[2], 2, 0), (parts[1], 0, 2)]
        return sum((part.astype(F32) for part in come), parts[0].astype(F32))


class Traffic:
    AHEAD = 4

    def __init__(self, links, chains):
        self.links, self.chains, self.results = links, chains, {}
        self.come, self.last, self.open = {}, None, []

    def step(self, name):
        chain, come = self.chains[name], self.come.get(name)
        if come is not None:
            self.open = [part for part in self.open if not any(part is other for other in come)]
            come = [after(part, self.last) for part in come]
        try:
            sends = chain.send(come)
        except StopIteration as end:
            self.results[name] = end.value
            self.come.pop(name, None)
            self.chains.pop(name)
            return
        self.come[name] = []
        for value, dc, dw in sends:
            ties = [] if self.last is None else [self.last]
            if dc is not None:
                while len(self.open) > self.AHEAD:
                    ties.append(self.open.pop(0))
            self.last = after(value, *ties)
            if dc is None:
                come = lax.all_to_all(self.last, "ctx", 0, 0, tiled=True)
            else:
                come = self.links.swap(self.last, dc, dw)
                self.open.append(come)
            self.come[name].append(come)

    def run(self, turns):
        for name in turns:
            if name in self.chains:
                self.step(name)
        while self.chains:
            for name in list(self.chains):
                self.step(name)


def on_device(
    tokens,
    slots,
    norm_gains,
    norm_shifts,
    qkv_weight,
    qv_bias,
    proj_weight,
    proj_bias,
    up_weight,
    up_bias,
    down_weight,
    down_bias,
    cotangent,
):
    links = Links()
    n, m, c, w = links.n, links.m, links.c, links.w
    _, rows, width = tokens.shape
    heads = Heads(n, width)
    share = width // m
    block = rows // 2
    length = n * rows
    hid = up_weight.shape[1]
    per = hid // (2 * m)
    tile = 256 if length <= UNROLLED else 128
    near = rows * m
    nq = n // 2
    cut = nq // m

    def half_of(c):
        return (c >> 1) & 1

    def place_of(c):
        return ((c >> 2) << 1) | (c & 1)

    half, place_q = half_of(c), place_of(c)
    spread = links.bits[:1] + links.bits[2:]
    order = links.halving(links.bits)

    own = tokens[0]
    small = jnp.concatenate(
        [
            norm_gains.reshape(-1),
            norm_shifts.reshape(-1),
            qv_bias.reshape(-1),
            proj_bias,
            down_bias,
            up_bias,
        ]
    )
    entries = small.shape[0]
    more = -(-(-(-entries // (3 * heads.wide))) // 16) * 16
    small = jnp.pad(small, [(0, more * 3 * heads.wide - entries)]).reshape(more, 3 * heads.wide)
    seen = {0: own}
    for bit in reversed(links.bits[1:]):
        seen.update({d | bit: links.swap(seen[d], bit, 0) for d in list(seen)})
    firsts = [0] + [bit for bit in links.bits[1:]]
    rest = [d for d in seen if d not in firsts]
    seen[1] = links.swap(own, 1, 0)
    for batch in (firsts[1:], rest):
        sent = links.swap(jnp.concatenate([seen[d] for d in batch]), 1, 0)
        seen.update({d | 1: sent[i * rows : (i + 1) * rows] for i, d in enumerate(batch)})
    found = links.gather_wt(heads.pick(qkv_weight, small, c))
    wqkv = links.rows_wt(found, share)
    small = jnp.concatenate([part[:, share:].reshape(2, -1)[:, :entries] for part in found])
    seen = jnp.concatenate([seen[d] for d in order])

    far_bits = links.bits[:1:-1]
    bits = {
        "down": [*far_bits, 2, 1],
        "up": [*far_bits, 1, 2],
        "qkv": [*far_bits, 2, 1],
        "proj": [*far_bits, 1, 2],
        "up sum": [1, *far_bits],
        "down sum": [1, *far_bits],
        "proj sum": [1, 2, *far_bits],
    }
    pieces = rearrange(
        functools.partial(cut_kernel, per),
        [shaped((k, share, per)) for k in (1, 1, 2)],
        [(w ^ r) * 2 + half for r in range(m)],
        [up_weight],
    )
    pieces = [pieces[0], pieces[1], after(pieces[2], found[0])]
    wdown = lax.dynamic_slice_in_dim(down_weight, half * per, per, 0)
    grad_out = cotangent[0]

    number = jnp.arange(m, dtype=jnp.int32)
    sources = jnp.array([0, 2, 1, 3], jnp.int32) ^ w
    small = dot((number[:, None] == sources[None, :]).astype(BF16), small)
    vectors = small[:, : 6 * share].reshape(m, 3, 2, share).transpose(1, 2, 0, 3)
    gains, shifts, qvb = vectors.reshape(3, 2, width)
    bproj = small[:, 6 * share : 7 * share].reshape(width)
    bdown = small[:, 7 * share : 8 * share].reshape(width)
    bup = small[:, 8 * share :].reshape(m * 2, per)
    bup = lax.dynamic_index_in_dim(bup, w * 2 + half, 0, False)

    a1 = (standardize(seen.astype(F32))[0] * gains[0] + shifts[0]).astype(BF16)
    qvb_here = heads.here(qvb, c)
    bias = jnp.concatenate([qvb_here[0], jnp.zeros((heads.wide,), F32), qvb_here[1]])
    qkv = (dot(a1, wqkv) + bias).astype(BF16)

    table = jnp.arange(slots.shape[0], dtype=jnp.int32)
    wanted = jnp.array(order, jnp.int32)
    wanted = ((wanted[:, None] ^ c) * 2 + jnp.arange(2, dtype=jnp.int32)).reshape(-1)
    place = jnp.sum(jnp.where(wanted[:, None] == table[None, :], slots[None, :], 0), axis=1)

    grad_out_plane = links.gather_plane(after(grad_out, seen))
    heads_out, lse = attn_forward(qkv, place, slots, block, tile)

    wproj = links.gather_wt(after(proj_weight, found[0]), heads_out)
    wproj = links.rows_wt(wproj, share)
    attended = lax.all_to_all(heads_out, "ctx", 0, 0, tiled=True)
    attended = heads.join(after(attended, wproj))
    far = after(links.x(pieces[2]), attended)
    wup = [pieces[0], far[:1], links.core(jnp.concatenate([pieces[1], far[1:]]))]
    wup = links.rows_wt(wup, share)
    mid = own.astype(F32) + dot(attended, wproj) + bproj
    normed2, scale2 = standardize(mid)
    a2 = (normed2 * gains[1] + shifts[1]).astype(BF16)

    a2_plane = links.gather_plane(a2)
    grad_out32 = grad_out.astype(F32)
    middle = length // 2
    step = -(-(-(-per // nq)) // 8) * 8
    part = -(-(-(-share // n)) // 8) * 8
    kept = {}

    def main_chain():
        pre = dot(a2_plane, wup) + bup
        activated, gelu_pull = jax.vjp(gelu, pre)
        hidden = activated.astype(BF16)
        grad_pre = gelu_pull(by_transpose(grad_out_plane, wdown))[0].astype(BF16)
        kept.update(hidden=hidden, grad_pre=grad_pre)
        grad_a2 = yield from links.sum_plane(
            lambda: by_transpose(grad_pre[:near], wup),
            by_transpose(grad_pre[near:], wup).astype(BF16),
        )
        grad_mid = grad_out32 + finish_norm(grad_a2 * gains[1], normed2, scale2)
        grad_proj = grad_mid.astype(BF16)
        kept.update(grad_a2=grad_a2, grad_mid=grad_mid, grad_proj=grad_proj)
        grad_heads = heads.split(by_transpose(grad_proj, wproj).astype(BF16))
        word = after(jnp.zeros((8, 128), F32), grad_heads)
        (grad_heads,) = yield [(grad_heads, None, None)]
        for _ in range(BUMP):
            word = links.core(word)
        grad_heads = after(grad_heads, word)
        grad_qkv = attn_backward(qkv, grad_heads, lse, place, slots, block, tile)
        normed1 = standardize(after(seen, word).astype(F32))[0]
        other, mine = by_transpose(grad_qkv[:middle], wqkv), by_transpose(grad_qkv[middle:], wqkv)
        d_gain1 = jnp.sum(other * normed1[:middle] + mine * normed1[middle:], axis=0)
        kept.update(grad_qkv=grad_qkv, other=other.astype(BF16), mine=mine, d_gain1=d_gain1)

    def down_chain():
        found = by_rows(over_rows(kept["hidden"], grad_out_plane).astype(BF16))
        found = jnp.pad(found, [(0, step * nq - per), (0, 0)])
        found = [
            lax.dynamic_slice_in_dim(found, (place_q ^ place_of(d)) * step, step, 0)
            for d in links.halving(bits["down sum"])
        ]
        found = yield from links.halve(jnp.stack(found), bits["down sum"])
        return (yield from links.gather(found, bits["down"]))

    def up_chain():
        found = by_rows(over_rows(a2_plane, kept["grad_pre"]).astype(BF16))
        pieces = [lax.dynamic_slice_in_dim(found, (w ^ r) * share, share, 0) for r in range(m)]
        found = yield from links.trade_wt(pieces[0][None], pieces[1][None], jnp.stack(pieces[2:]))
        found = jnp.concatenate(found).reshape(m, share, cut, per // cut).transpose(0, 2, 1, 3)
        terms = []
        for d in links.halving(bits["up sum"]):
            b = place_q ^ place_of(d)
            r = w ^ (b // cut)
            r = (r & 1) * 2 + (r >> 1)
            term = lax.dynamic_slice(found, (r, b % cut, 0, 0), (1, 1, share, per // cut))
            terms.append(term[0, 0])
        found = yield from links.halve(jnp.stack(terms), bits["up sum"])
        return (yield from links.gather(found, bits["up"]))

    def output_chain():
        hidden = kept["hidden"]
        near_part = dot(hidden[:near], wdown).astype(BF16)
        far_part = dot(hidden[near:], wdown).astype(BF16)
        return (yield from links.sum_plane(lambda: near_part, far_part))

    def proj_chain():
        found = by_rows(over_rows(attended, kept["grad_proj"]).astype(BF16))
        pieces = [
            lax.dynamic_slice_in_dim(found, (w ^ r) * share, share, 0) for r in (0, 2, 1, 3)
        ]
        found = yield from links.sum_wt(jnp.stack(pieces[:2]), jnp.stack(pieces[2:]))
        found = jnp.pad(found, [(0, n * part - share), (0, 0)])
        found = [
            lax.dynamic_slice_in_dim(found, (c ^ d) * part, part, 0)
            for d in links.halving(bits["proj sum"])
        ]
        found = yield from links.halve(jnp.stack(found), bits["proj sum"])
        return (yield from links.gather(found, bits["proj"]))

    def input_chain():
        (come,) = yield [(kept["other"], 1, 0)]
        terms = add_low(kept["mine"], come).reshape(n // 2, rows, width)
        return (yield from links.halve(terms, links.bits[1:]))

    def qkv_chain():
        grad_a2, grad_proj, grad_qkv = (kept[name] for name in ("grad_a2", "grad_proj", "grad_qkv"))
        sums = jnp.sum(grad_qkv.astype(F32), axis=0)
        d_shift1 = dot(sums[None], wqkv.astype(F32).T)[0]
        sums = heads.back(sums.reshape(3, heads.wide), c)
        d_up_bias = lax.dynamic_update_slice(
            jnp.zeros((m * 2, per), F32),
            jnp.sum(kept["grad_pre"].astype(F32), axis=0)[None],
            (w * 2 + half, 0),
        ).reshape(m, hid // m)
        vectors = [
            kept["d_gain1"],
            jnp.sum(grad_a2 * normed2, axis=0),
            d_shift1,
            jnp.sum(grad_a2, axis=0),
            sums[0],
            sums[2],
            jnp.sum(grad_proj.astype(F32), axis=0),
            jnp.sum(grad_out32, axis=0),
        ]
        vectors = jnp.concatenate([v.reshape(m, share) for v in vectors] + [d_up_bias], axis=1)
        vectors = jnp.pad(vectors, [(0, 0), (0, more * 3 * heads.wide - entries)])
        vectors = vectors.astype(BF16).reshape(m * more, 3 * heads.wide)
        found = by_rows(over_rows(a1, grad_qkv).astype(BF16))
        pieces = [
            jnp.concatenate(
                [
                    lax.dynamic_slice_in_dim(found, (w ^ r) * share, share, 0),
                    lax.dynamic_slice_in_dim(vectors, (w ^ r) * more, more, 0),
                ]
            )
            for r in (0, 2, 1, 3)
        ]
        found = yield from links.sum_wt(jnp.stack(pieces[:2]), jnp.stack(pieces[2:]))
        return (yield from links.gather(found, bits["qkv"]))

    chains = {
        "m": main_chain(),
        "d": down_chain(),
        "u": up_chain(),
        "g": input_chain(),
        "q": qkv_chain(),
        "p": proj_chain(),
        "o": output_chain(),
    }
    traffic = Traffic(links, chains)
    traffic.run(TURNS)
    d_down, d_up, d_qkv, d_proj = (traffic.results[name] for name in "duqp")
    output, grad_a1 = traffic.results["o"], traffic.results["g"].astype(F32)
    grad_mid = kept["grad_mid"]

    output = mid + output + bdown
    own1, scale1 = standardize(own.astype(F32))
    d_tokens = grad_mid + finish_norm(grad_a1 * gains[0], own1, scale1)

    def owners(name):
        return [c ^ d for d in links.gathered(bits[name])]

    plan = [
        (
            b,
            (0, 0),
            (min(step, per - place_of(b) * step), width),
            (half_of(b) * per + place_of(b) * step, 0),
        )
        for b in range(n)
        if place_of(b) * step < per
    ]
    d_down_weight = lay(d_down, owners("down"), plan, (2 * per, width))
    size = per // cut
    plan = [
        (
            b,
            (0, 0),
            (share, size),
            (
                0,
                (place_of(b) // cut) * 2 * per + half_of(b) * per + (place_of(b) % cut) * size,
            ),
        )
        for b in range(n)
    ]
    d_up_weight = lay(d_up, owners("up"), plan, (share, hid))
    plan = [
        (b, (0, 0), (min(part, share - b * part), width), (b * part, 0))
        for b in range(n)
        if b * part < share
    ]
    d_proj_weight = lay(d_proj, owners("proj"), plan, (share, width))
    plan = [
        (
            p % n,
            (0, (t * heads.slots + p // n) * 128),
            (share, min(128, width - p * 128)),
            (0, t * width + p * 128),
        )
        for t in range(3)
        for p in range(-(-width // 128))
    ]
    d_qkv_weight = lay(d_qkv, owners("qkv"), plan, (share, 3 * width))
    vectors = sum(jnp.sum(part[:, share:].astype(F32), axis=0) for part in d_qkv)
    vectors = vectors.reshape(-1)[:entries]
    eight = vectors[: 8 * share].reshape(8, share)

    return (
        output.astype(BF16)[None],
        d_tokens.astype(BF16)[None],
        eight[0:2],
        eight[2:4],
        d_qkv_weight,
        eight[4:6],
        d_proj_weight,
        eight[6],
        d_up_weight,
        vectors[8 * share :],
        d_down_weight,
        eight[7],
    )


def solution(mesh):
    rows, whole = P("wt", "ctx", None), P(None, "wt")
    weight, vector = P("wt", None), P("wt")
    return jax.shard_map(
        on_device,
        mesh=mesh,
        in_specs=(
            rows,
            P(),
            whole,
            whole,
            weight,
            whole,
            weight,
            vector,
            weight,
            vector,
            weight,
            vector,
            rows,
        ),
        out_specs=(
            rows,
            rows,
            whole,
            whole,
            weight,
            whole,
            weight,
            vector,
            weight,
            vector,
            weight,
            vector,
        ),
        check_vma=False,
    )
```

time: 730 us -> 631 us (0.86)
  waiting for transfers between devices: 363 us -> 278 us
  starting transfers between devices: 143 us -> 71.3 us
  other arithmetic: 31.7 us -> 73.2 us
  matrix products: 61.3 us -> 68.9 us
    ppermute x116 -> x64, waiting for transfers between devices: 363 us -> 275 us  [swap(): return lax.ppermute(value, AXES, pairs)]
    ppermute x116 -> x64, starting transfers between devices: 143 us -> 61.3 us  [swap(): return lax.ppermute(value, AXES, pairs)]
    concatenate x0 -> x12, other arithmetic: none -> 19.5 us  [the longest x8 17.6 us: gather(): blocks = jnp.concatenate([blocks, come])]
    all_to_all x0 -> x2, starting transfers between devices: none -> 10 us  [the longest x1 6.15 us: on_device(): attended = lax.all_to_all(heads_out, 'ctx', 0, 0, tiled=True)]
    another operation x1 -> x10, other arithmetic: 2.17 us -> 11.2 us  [the longest x1 3.12 us: proj_chain(): jnp.stack(pieces[2:])]
    convert_element_type x6 -> x14, other arithmetic: 11.8 us -> 19.8 us  [add_low(): return (left.astype(F32) + right.astype(F32)).astype(BF16)]
    dot_general x6 -> x7, matrix products: 17.9 us -> 24.2 us  [dot(): return jnp.dot(left, right, preferred_element_type=F32)]
    unnamed x204 -> x183, local copies, waits for them, and re-layouts: 35.4 us -> 29.4 us
  transfers between devices with their start and end apart: 116 -> 66, of which waited for: 42 -> 26; matrix products, arithmetic and copies ran while one was open for 16% -> 29% of each run, Pallas kernels for 7% -> 8%
where the time goes in v2:
time: 631 us; the launch traced here: 620 us
  waiting for transfers between devices  278 us (44%)
  other arithmetic  73.2 us (12%)
  starting transfers between devices  71.3 us (11%)
  local copies, waits for them, and re-layouts  70.1 us (11%)
  matrix products  68.9 us (11%)
  Pallas kernels  55.4 us (9%)
    ppermute x64, waiting for transfers between devices, swap(): return lax.ppermute(value, AXES, pairs)  275 us
    ppermute x64, starting transfers between devices, swap(): return lax.ppermute(value, AXES, pairs)  61.3 us
    pallas_call x9, Pallas kernels, rearrange(): pl.pallas_call(kernel, out_shape=tuple((jax.ShapeDtypeStruct(o.shape, o.d...  34.2 us
    unnamed x183, local copies, waits for them, and re-layouts  29.4 us
    dot_general x6, matrix products, by_transpose(): lax.dot_general(left, right, (((1,), (1,)), ((), ())), preferred_element_...  25.9 us
    dot_general x7, matrix products, dot(): return jnp.dot(left, right, preferred_element_type=F32)  24.2 us
    convert_element_type x14, other arithmetic, add_low(): return (left.astype(F32) + right.astype(F32)).astype(BF16)  19.8 us
    dot_general x4, matrix products, over_rows(): lax.dot_general(left, right, (((0,), (0,)), ((), ())), preferred_element_...  18.9 us
  transfers between devices with their start and end apart: 66, of which 26 were waited for; matrix products, arithmetic and copies ran while one was open for 29% of the time, Pallas kernels for 8%

profile of v2, /device:TPU:0, one launch (start us, length us, event | category | flops | bytes accessed | tf_op | source)
XLA Modules:
  0.0 619.6 jit_solution(12708431213299270468)
XLA Ops:
  16.5 6.8 %collective-permute-done = bf16[128,1600]{0,1:T(8,128)(2,1)S(1)} collective-permute-done((bf16[128,1600]{0,1:T(8,128)(2,1)}, bf16[128,1600]{0,1:T(8,128)(2,1)S(1)}, u32[]{:S(2)}, u32[]{:S(2)}) %collective-permute-start) | collective-permute-done | bytes 409632 | tf_op jit(solution)/shard_map/ppermute | solution.py:412
  26.6 7.4 %collective-permute-done.1 = bf16[128,1600]{0,1:T(8,128)(2,1)} collective-permute-done((bf16[128,1600]{0,1:T(8,128)(2,1)S(1)}, bf16[128,1600]{0,1:T(8,128)(2,1)}, u32[]{:S(2)}, u32[]{:S(2)}) %collective-permute-start.1) | collective-permute-done | bytes 409632 | tf_op jit(solution)/shard_map/ppermute | solution.py:412
  39.1 14.9 %collective-permute-done.2 = bf16[128,1600]{0,1:T(8,128)(2,1)} collective-permute-done((bf16[128,1600]{0,1:T(8,128)(2,1)}, bf16[128,1600]{0,1:T(8,128)(2,1)}, u32[]{:S(2)}, u32[]{:S(2)}) %collective-permute-start.2) | collective-permute-done | bytes 409632 | tf_op jit(solution)/shard_map/ppermute | solution.py:412
  68.8 6.8 %shard_map.240 = (bf16[8,128,256]{2,1,0:T(8,128)(2,1)S(1)}, f32[1024,128]{1,0:T(8,128)S(1)}) custom-call(s32[16]{0:T(128)S(1)} %select_reduce_fusion.place_ref, s32[16]{0:T(128)S(1)} %copy-done.8, bf16[1024,768]{1,0:T(8,128)(2,1)S(1)} %add_convert_fusion.3.qkv_ref), custom_call_target="tpu_custom_call" | custom-call | flops 1073741824 | bytes 2621440 | tf_op jit(solution)/shard_map/pallas_call | solution.py:199
  94.3 6.1 collective-permute-done.20
  102.2 6.9 %collective-permute-done.21 = bf16[128,1600]{0,1:T(8,128)(2,1)} collective-permute-done((bf16[128,1600]{0,1:T(8,128)(2,1)}, bf16[128,1600]{0,1:T(8,128)(2,1)}, u32[]{:S(2)}, u32[]{:S(2)}) %collective-permute-start.21) | collective-permute-done | bytes 409632 | tf_op jit(solution)/shard_map/ppermute | solution.py:412
  112.2 6.1 all-to-all-start
  125.5 4.5 shard_map.241
  134.6 5.0 fusion.85
  146.2 5.8 collective-permute-done.10
  153.7 6.6 %collective-permute-done.12 = bf16[128,1600]{0,1:T(8,128)(2,1)S(1)} collective-permute-done((bf16[128,1600]{0,1:T(8,128)(2,1)S(1)}, bf16[128,1600]{0,1:T(8,128)(2,1)S(1)}, u32[]{:S(2)}, u32[]{:S(2)}) %collective-permute-start.12) | collective-permute-done | bytes 409632 | tf_op jit(solution)/shard_map/ppermute | solution.py:412
  168.2 7.6 %convert_reduce_fusion.2 = (bf16[800]{0:T(1024)(128)(2,1)S(1)}, bf16[1024,800]{0,1:T(8,128)(2,1)S(1)}) fusion(bf16[1024,1600]{0,1:T(8,128)(2,1)} %constant_dynamic-update-slice_fusion.15, bf16[1600,1600]{1,0:T(8,128)(2,1)S(1)} %bitcast.170, s32[]{:T(128)S(6)} %select_n.120, f32[1024,800]{0,1:T(8,128)S(1)} %get-tuple-element.259, f32[800]{0:T(1024)S(1)} %fusion.69), kind=kOutput, calls=%fused_computation.32 | convolution fusion | flops 2643557632 | bytes 10860100 | tf_op jit(solution)/shard_map/dot_general | solution.py:49
  179.0 5.3 convolution_convert_fusion.2
  192.0 5.2 convolution_convert_fusion.5
  197.2 5.0 convolution_convert_fusion.6
  221.3 4.5 collective-permute-done.30
  225.8 8.0 %collective-permute-done.32 = bf16[128,1600]{0,1:T(8,128)(2,1)S(1)} collective-permute-done((bf16[128,1600]{0,1:T(8,128)(2,1)S(1)}, bf16[128,1600]{0,1:T(8,128)(2,1)S(1)}, u32[]{:S(2)}, u32[]{:S(2)}) %collective-permute-start.32) | collective-permute-done | bytes 409632 | tf_op jit(solution)/shard_map/ppermute | solution.py:412
  275.4 4.5 collective-permute-done.36
  288.5 10.7 %shard_map.246 = bf16[1024,768]{1,0:T(8,128)(2,1)S(1)} custom-call(s32[16]{0:T(128)S(1)} %select_reduce_fusion.place_ref, s32[16]{0:T(128)S(1)} %copy-done.8, bf16[1024,768]{1,0:T(8,128)(2,1)S(1)} %copy-done.10, f32[1024,128]{1,0:T(8,128)S(1)} %copy-done.12, bf16[8,128,256]{2,1,0:T(8,128)(2,1)S(1)} %all-to-all-done.1.grad_ref), custom_call_target="tpu_custom_call" | custom-call | flops 2684354560 | bytes 4194304 | tf_op jit(solution)/shard_map/pallas_call | solution.py:219
  302.9 7.1 %fusion.76 = (bf16[512,1600]{0,1:T(8,128)(2,1)}, bf16[1600]{0:T(1024)(128)(2,1)S(1)}) fusion(f32[512,1600]{0,1:T(8,128)} %fusion.44, f32[1024,1600]{0,1:T(8,128)} %fusion.2, bf16[1600,768]{1,0:T(8,128)(2,1)S(1)} %copy-done.1, bf16[1024,768]{1,0:T(8,128)(2,1)} %copy-done.3), kind=kOutput, calls=%fused_computation.239 | convolution fusion | flops 1262385664 | bytes 14716032 | tf_op jit(solution)/shard_map/dot_general | solution.py:49
  311.7 5.6 convolution_convert_fusion.3
  325.1 9.4 %collective-permute-done.41 = bf16[1,200,1600]{2,1,0:T(8,128)(2,1)} collective-permute-done((bf16[1,200,1600]{2,1,0:T(8,128)(2,1)}, bf16[1,200,1600]{2,1,0:T(8,128)(2,1)}, u32[]{:S(2)}, u32[]{:S(2)}) %collective-permute-start.41) | collective-permute-done | bytes 640032 | tf_op jit(solution)/shard_map/ppermute | solution.py:412
  341.9 29.6 %collective-permute-done.45 = bf16[1,400,800]{2,1,0:T(8,128)(2,1)} collective-permute-done((bf16[1,400,800]{2,1,0:T(8,128)(2,1)S(1)}, bf16[1,400,800]{2,1,0:T(8,128)(2,1)}, u32[]{:S(2)}, u32[]{:S(2)}) %collective-permute-start.45) | collective-permute-done | bytes 640032 | tf_op jit(solution)/shard_map/ppermute | solution.py:412
  381.7 9.1 %collective-permute-done.50 = bf16[416,768]{1,0:T(8,128)(2,1)S(1)} collective-permute-done((bf16[416,768]{1,0:T(8,128)(2,1)S(1)}, bf16[416,768]{1,0:T(8,128)(2,1)S(1)}, u32[]{:S(2)}, u32[]{:S(2)}) %collective-permute-start.50) | collective-permute-done | bytes 639008 | tf_op jit(solution)/shard_map/ppermute | solution.py:412
  398.2 23.7 %collective-permute-done.48 = bf16[1,400,800]{2,1,0:T(8,128)(2,1)} collective-permute-done((bf16[1,400,800]{2,1,0:T(8,128)(2,1)S(1)}, bf16[1,400,800]{2,1,0:T(8,128)(2,1)}, u32[]{:S(2)}, u32[]{:S(2)}) %collective-permute-start.48) | collective-permute-done | bytes 640032 | tf_op jit(solution)/shard_map/ppermute | solution.py:412
  436.9 5.6 collective-permute-done.51
  452.2 17.5 %collective-permute-done.53 = bf16[1,56,1600]{2,1,0:T(8,128)(2,1)S(1)} collective-permute-done((bf16[1,56,1600]{2,1,0:T(8,128)(2,1)S(1)}, bf16[1,56,1600]{2,1,0:T(8,128)(2,1)S(1)}, u32[]{:S(2)}, u32[]{:S(2)}) %collective-permute-start.53) | collective-permute-done | bytes 179232 | tf_op jit(solution)/shard_map/ppermute | solution.py:412
  483.0 12.5 %collective-permute-done.55 = bf16[2,128,1600]{1,2,0:T(8,128)(2,1)S(1)} collective-permute-done((bf16[2,128,1600]{1,2,0:T(8,128)(2,1)}, bf16[2,128,1600]{1,2,0:T(8,128)(2,1)S(1)}, u32[]{:S(2)}, u32[]{:S(2)}) %collective-permute-start.55) | collective-permute-done | bytes 819232 | tf_op jit(solution)/shard_map/ppermute | solution.py:412
  501.2 80.0 %collective-permute-done.58 = bf16[2,56,1600]{2,1,0:T(8,128)(2,1)} collective-permute-done((bf16[2,56,1600]{2,1,0:T(8,128)(2,1)}, bf16[2,56,1600]{2,1,0:T(8,128)(2,1)}, u32[]{:S(2)}, u32[]{:S(2)}) %collective-permute-start.58) | collective-permute-done | bytes 358432 | tf_op jit(solution)/shard_map/ppermute | solution.py:412
  588.2 7.8 %shard_map.250 = f32[1600,1600]{1,0:T(8,128)} custom-call(s32[8]{0:T(128)S(1)} %stack.244.numbers, bf16[4,200,1600]{2,1,0:T(8,128)(2,1)} %pad_maximum_fusion.4.refs_0_, bf16[4,200,1600]{2,1,0:T(8,128)(2,1)} %collective-permute-done.63.refs_1_), custom_call_target="tpu_custom_call" | custom-call | bytes 15360000 | tf_op jit(solution)/shard_map/pallas_call | solution.py:237
  600.5 7.5 %shard_map.249 = f32[400,6400]{1,0:T(8,128)} custom-call(s32[8]{0:T(128)S(1)} %stack.245.numbers, bf16[4,400,800]{2,1,0:T(8,128)(2,1)S(1)} %pad_maximum_fusion.1.refs_0_, bf16[4,400,800]{2,1,0:T(8,128)(2,1)} %collective-permute-done.62.refs_1_), custom_call_target="tpu_custom_call" | custom-call | bytes 15360000 | tf_op jit(solution)/shard_map/pallas_call | solution.py:237
  609.0 6.8 %shard_map.247 = f32[400,4800]{1,0:T(8,128)} custom-call(s32[8]{0:T(128)S(1)} %stack.244.numbers, bf16[4,416,768]{2,1,0:T(8,128)(2,1)} %pad_maximum_fusion.5.refs_0_, bf16[4,416,768]{2,1,0:T(8,128)(2,1)} %collective-permute-done.60.refs_1_), custom_call_target="tpu_custom_call" | custom-call | bytes 12791808 | tf_op jit(solution)/shard_map/pallas_call | solution.py:237
  (471 shorter events, 267.1 us)
Async XLA Ops:
  6.3 50.2 %collective-permute-start.5 = (bf16[128,1600]{0,1:T(8,128)(2,1)}, bf16[128,1600]{0,1:T(8,128)(2,1)}, u32[]{:S(2)}, u32[]{:S(2)}) collective-permute-start(bf16[128,1600]{0,1:T(8,128)(2,1)} %bitcast.153), channel_id=1, source_target_pairs={{0,4},{1,5},{2,6},{3,7},{4,0},{5,1},{6,2},{7,3},{8,12},{9,13},{10,... | collective-permute-start | bytes 1228808 | tf_op jit(solution)/shard_map/ppermute | solution.py:412
  25.1 30.1 %collective-permute-start.4 = (bf16[256,1600]{0,1:T(8,128)(2,1)}, bf16[256,1600]{0,1:T(8,128)(2,1)}, u32[]{:S(2)}, u32[]{:S(2)}) collective-permute-start(bf16[256,1600]{0,1:T(8,128)(2,1)} %pad_maximum_fusion.16), channel_id=1, source_target_pairs={{0,4},{1,5},{2,6},{3,7},{4,0},{5,1},{6,2},{7,3},{8,12},{9,13},{10,... | collective-permute-start | bytes 2457608 | tf_op jit(solution)/shard_map/ppermute | solution.py:412
  37.6 38.8 %collective-permute-start.8 = (bf16[400,1600]{1,0:T(8,128)(2,1)}, bf16[400,1600]{1,0:T(8,128)(2,1)}, u32[]{:S(2)}, u32[]{:S(2)}) collective-permute-start(bf16[400,1600]{1,0:T(8,128)(2,1)} %param.21), channel_id=1, source_target_pairs={{0,2},{1,3},{2,0},{3,1},{4,6},{5,7},{6,4},{7,5},{8,10},{9,11},{10,... | collective-permute-start | bytes 3840008 | tf_op jit(solution)/shard_map/ppermute | solution.py:412
  78.2 47.3 %collective-permute-start.9 = (bf16[2,400,1600]{2,1,0:T(8,128)(2,1)S(1)}, bf16[2,400,1600]{2,1,0:T(8,128)(2,1)}, u32[]{:S(2)}, u32[]{:S(2)}) collective-permute-start(bf16[2,400,1600]{2,1,0:T(8,128)(2,1)S(1)} %pad_maximum_fusion.2.refs_0_), channel_id=1, source_target_pairs={{0,1},{1,0},{2,3},{3,2},{4,5},{5,4},{6,7},{7,6},{8,9},{9,8},{10,11... | collective-permute-start | bytes 7680008 | tf_op jit(solution)/shard_map/ppermute | solution.py:412
  87.2 56.7 %collective-permute-start.17 = (bf16[2,400,800]{2,1,0:T(8,128)(2,1)}, bf16[2,400,800]{2,1,0:T(8,128)(2,1)}, u32[]{:S(2)}, u32[]{:S(2)}) collective-permute-start(bf16[2,400,800]{2,1,0:T(8,128)(2,1)} %copy-done.7), channel_id=1, source_target_pairs={{0,2},{1,3},{2,0},{3,1},{4,6},{5,7},{6,4},{7,5},{8,10},{9,11},{10,... | collective-permute-start | bytes 3840008 | tf_op jit(solution)/shard_map/ppermute | solution.py:412
  178.8 30.1 %collective-permute-start.26 = (bf16[512,1600]{0,1:T(8,128)(2,1)}, bf16[512,1600]{0,1:T(8,128)(2,1)}, u32[]{:S(2)}, u32[]{:S(2)}) collective-permute-start(bf16[512,1600]{0,1:T(8,128)(2,1)} %convolution_convert_fusion.4), channel_id=1, source_target_pairs={{0,1},{1,0},{2,3},{3,2},{4,5},{5,4},{6,7},{7,6},{8,9},{9,8},{10,11... | collective-permute-start | bytes 4915208 | tf_op jit(solution)/shard_map/ppermute | solution.py:412
  186.6 32.1 %collective-permute-start.27 = (bf16[2,200,1600]{2,1,0:T(8,128)(2,1)}, bf16[2,200,1600]{2,1,0:T(8,128)(2,1)}, u32[]{:S(2)}, u32[]{:S(2)}) collective-permute-start(bf16[2,200,1600]{2,1,0:T(8,128)(2,1)} %pad_maximum_fusion.12), channel_id=1, source_target_pairs={{0,4},{1,5},{2,6},{3,7},{4,0},{5,1},{6,2},{7,3},{8,12},{9,13},{10,... | collective-permute-start | bytes 3840008 | tf_op jit(solution)/shard_map/ppermute | solution.py:412
  216.1 48.5 %collective-permute-start.29 = (bf16[2,400,800]{2,1,0:T(8,128)(2,1)}, bf16[2,400,800]{2,1,0:T(8,128)(2,1)}, u32[]{:S(2)}, u32[]{:S(2)}) collective-permute-start(bf16[2,400,800]{2,1,0:T(8,128)(2,1)} %pad_maximum_fusion.8), channel_id=1, source_target_pairs={{0,2},{1,3},{2,0},{3,1},{4,6},{5,7},{6,4},{7,5},{8,10},{9,11},{10,... | collective-permute-start | bytes 3840008 | tf_op jit(solution)/shard_map/ppermute | solution.py:412
  218.7 51.3 %collective-permute-start.28 = (bf16[512,1600]{0,1:T(8,128)(2,1)}, bf16[512,1600]{0,1:T(8,128)(2,1)}, u32[]{:S(2)}, u32[]{:S(2)}) collective-permute-start(bf16[512,1600]{0,1:T(8,128)(2,1)} %convolution_convert_fusion.5), channel_id=1, source_target_pairs={{0,1},{1,0},{2,3},{3,2},{4,5},{5,4},{6,7},{7,6},{8,9},{9,8},{10,11... | collective-permute-start | bytes 4915208 | tf_op jit(solution)/shard_map/ppermute | solution.py:412
  242.0 37.8 %collective-permute-start.36 = (bf16[1,200,1600]{2,1,0:T(8,128)(2,1)}, bf16[1,200,1600]{2,1,0:T(8,128)(2,1)}, u32[]{:S(2)}, u32[]{:S(2)}) collective-permute-start(bf16[1,200,1600]{2,1,0:T(8,128)(2,1)} %slice.329), channel_id=1, source_target_pairs={{0,16},{1,17},{2,18},{3,19},{4,20},{5,21},{6,22},{7,23},{8,24},{9,... | collective-permute-start | bytes 1920008 | tf_op jit(solution)/shard_map/ppermute | solution.py:412
  249.2 36.8 %all-to-all-start.1 = ((bf16[8,128,256]{2,1,0:T(8,128)(2,1)}), bf16[8,128,256]{2,1,0:T(8,128)(2,1)S(1)}, u32[]{:S(2)}, u32[]{:S(2)}) async-start(bf16[8,128,256]{2,1,0:T(8,128)(2,1)} %shard_map.245), calls=%async_computation.1 | async-start | bytes 1048576 | tf_op jit(solution)/shard_map/all_to_all | solution.py:512
  273.3 51.7 %collective-permute-start.33 = (bf16[128,1600]{0,1:T(8,128)(2,1)}, bf16[128,1600]{0,1:T(8,128)(2,1)}, u32[]{:S(2)}, u32[]{:S(2)}) collective-permute-start(bf16[128,1600]{0,1:T(8,128)(2,1)} %get-tuple-element.126), channel_id=1, source_target_pairs={{0,10},{1,11},{2,8},{3,9},{4,14},{5,15},{6,12},{7,13},{8,2},{9,3},... | collective-permute-start | bytes 1228808 | tf_op jit(solution)/shard_map/ppermute | solution.py:412
  273.6 63.1 %collective-permute-start.42 = (bf16[128,1600]{0,1:T(8,128)(2,1)}, bf16[128,1600]{0,1:T(8,128)(2,1)}, u32[]{:S(2)}, u32[]{:S(2)}) collective-permute-start(bf16[128,1600]{0,1:T(8,128)(2,1)} %get-tuple-element.127), channel_id=1, source_target_pairs={{0,8},{1,9},{2,10},{3,11},{4,12},{5,13},{6,14},{7,15},{8,0},{9,1},... | collective-permute-start | bytes 1228808 | tf_op jit(solution)/shard_map/ppermute | solution.py:412
  279.9 56.9 %collective-permute-start.43 = (bf16[128,1600]{0,1:T(8,128)(2,1)}, bf16[128,1600]{0,1:T(8,128)(2,1)}, u32[]{:S(2)}, u32[]{:S(2)}) collective-permute-start(bf16[128,1600]{0,1:T(8,128)(2,1)} %get-tuple-element.128), channel_id=1, source_target_pairs={{0,2},{1,3},{2,0},{3,1},{4,6},{5,7},{6,4},{7,5},{8,10},{9,11},{10,... | collective-permute-start | bytes 1228808 | tf_op jit(solution)/shard_map/ppermute | solution.py:412
  283.5 36.0 %collective-permute-start.37 = (bf16[2,400,800]{2,1,0:T(8,128)(2,1)}, bf16[2,400,800]{2,1,0:T(8,128)(2,1)}, u32[]{:S(2)}, u32[]{:S(2)}) collective-permute-start(bf16[2,400,800]{2,1,0:T(8,128)(2,1)} %pad_maximum_fusion.10), channel_id=1, source_target_pairs={{0,4},{1,5},{2,6},{3,7},{4,0},{5,1},{6,2},{7,3},{8,12},{9,13},{10,... | collective-permute-start | bytes 3840008 | tf_op jit(solution)/shard_map/ppermute | solution.py:412
  302.8 31.6 %collective-permute-start.41 = (bf16[1,200,1600]{2,1,0:T(8,128)(2,1)}, bf16[1,200,1600]{2,1,0:T(8,128)(2,1)}, u32[]{:S(2)}, u32[]{:S(2)}) collective-permute-start(bf16[1,200,1600]{2,1,0:T(8,128)(2,1)} %add_convert_fusion.10), channel_id=1, source_target_pairs={{0,16},{1,17},{2,18},{3,19},{4,20},{5,21},{6,22},{7,23},{8,24},{9,... | collective-permute-start | bytes 1920008 | tf_op jit(solution)/shard_map/ppermute | solution.py:412
  336.7 36.2 %collective-permute-start.44 = (bf16[2,416,768]{2,1,0:T(8,128)(2,1)}, bf16[2,416,768]{2,1,0:T(8,128)(2,1)}, u32[]{:S(2)}, u32[]{:S(2)}) collective-permute-start(bf16[2,416,768]{2,1,0:T(8,128)(2,1)} %pad_maximum_fusion.14), channel_id=1, source_target_pairs={{0,1},{1,0},{2,3},{3,2},{4,5},{5,4},{6,7},{7,6},{8,9},{9,8},{10,11... | collective-permute-start | bytes 3833864 | tf_op jit(solution)/shard_map/ppermute | solution.py:412
  336.7 38.5 %collective-permute-start.38 = (bf16[400,1600]{1,0:T(8,128)(2,1)}, bf16[400,1600]{1,0:T(8,128)(2,1)}, u32[]{:S(2)}, u32[]{:S(2)}) collective-permute-start(bf16[400,1600]{1,0:T(8,128)(2,1)} %fusion.17), channel_id=1, source_target_pairs={{0,2},{1,3},{2,0},{3,1},{4,6},{5,7},{6,4},{7,5},{8,10},{9,11},{10,... | collective-permute-start | bytes 3840008 | tf_op jit(solution)/shard_map/ppermute | solution.py:412
  338.2 33.3 %collective-permute-start.45 = (bf16[1,400,800]{2,1,0:T(8,128)(2,1)S(1)}, bf16[1,400,800]{2,1,0:T(8,128)(2,1)}, u32[]{:S(2)}, u32[]{:S(2)}) collective-permute-start(bf16[1,400,800]{2,1,0:T(8,128)(2,1)S(1)} %slice.335), channel_id=1, source_target_pairs={{0,16},{1,17},{2,18},{3,19},{4,20},{5,21},{6,22},{7,23},{8,24},{9,... | collective-permute-start | bytes 1920008 | tf_op jit(solution)/shard_map/ppermute | solution.py:412
  338.2 86.0 %collective-permute-start.47 = (bf16[2,200,1600]{2,1,0:T(8,128)(2,1)}, bf16[2,200,1600]{2,1,0:T(8,128)(2,1)}, u32[]{:S(2)}, u32[]{:S(2)}) collective-permute-start(bf16[2,200,1600]{2,1,0:T(8,128)(2,1)} %pad_maximum_fusion.13), channel_id=1, source_target_pairs={{0,8},{1,9},{2,10},{3,11},{4,12},{5,13},{6,14},{7,15},{8,0},{9,1},... | collective-permute-start | bytes 3840008 | tf_op jit(solution)/shard_map/ppermute | solution.py:412
  340.1 54.6 %collective-permute-start.49 = (bf16[512,1600]{0,1:T(8,128)(2,1)}, bf16[512,1600]{0,1:T(8,128)(2,1)S(1)}, u32[]{:S(2)}, u32[]{:S(2)}) collective-permute-start(bf16[512,1600]{0,1:T(8,128)(2,1)} %get-tuple-element.144), channel_id=1, source_target_pairs={{0,4},{1,5},{2,6},{3,7},{4,0},{5,1},{6,2},{7,3},{8,12},{9,13},{10,... | collective-permute-start | bytes 4915208 | tf_op jit(solution)/shard_map/ppermute | solution.py:412
  372.8 49.1 %collective-permute-start.48 = (bf16[1,400,800]{2,1,0:T(8,128)(2,1)S(1)}, bf16[1,400,800]{2,1,0:T(8,128)(2,1)}, u32[]{:S(2)}, u32[]{:S(2)}) collective-permute-start(bf16[1,400,800]{2,1,0:T(8,128)(2,1)S(1)} %add_convert_fusion.9), channel_id=1, source_target_pairs={{0,16},{1,17},{2,18},{3,19},{4,20},{5,21},{6,22},{7,23},{8,24},{9,... | collective-permute-start | bytes 1920008 | tf_op jit(solution)/shard_map/ppermute | solution.py:412
  380.1 47.6 %collective-permute-start.46 = (bf16[4,56,1600]{2,1,0:T(8,128)(2,1)}, bf16[4,56,1600]{2,1,0:T(8,128)(2,1)}, u32[]{:S(2)}, u32[]{:S(2)}) collective-permute-start(bf16[4,56,1600]{2,1,0:T(8,128)(2,1)} %pad_maximum_fusion.17), channel_id=1, source_target_pairs={{0,4},{1,5},{2,6},{3,7},{4,0},{5,1},{6,2},{7,3},{8,12},{9,13},{10,... | collective-permute-start | bytes 2150408 | tf_op jit(solution)/shard_map/ppermute | solution.py:412
  392.2 42.5 %collective-permute-start.52 = (bf16[1,416,768]{2,1,0:T(8,128)(2,1)S(1)}, bf16[1,416,768]{2,1,0:T(8,128)(2,1)}, u32[]{:S(2)}, u32[]{:S(2)}) collective-permute-start(bf16[1,416,768]{2,1,0:T(8,128)(2,1)S(1)} %fusion.48), channel_id=1, source_target_pairs={{0,16},{1,17},{2,18},{3,19},{4,20},{5,21},{6,22},{7,23},{8,24},{9,... | collective-permute-start | bytes 1916936 | tf_op jit(solution)/shard_map/ppermute | solution.py:412
  429.5 43.7 %collective-permute-start.57 = (bf16[2,400,800]{2,1,0:T(8,128)(2,1)}, bf16[2,400,800]{2,1,0:T(8,128)(2,1)}, u32[]{:S(2)}, u32[]{:S(2)}) collective-permute-start(bf16[2,400,800]{2,1,0:T(8,128)(2,1)} %pad_maximum_fusion.11), channel_id=1, source_target_pairs={{0,4},{1,5},{2,6},{3,7},{4,0},{5,1},{6,2},{7,3},{8,12},{9,13},{10,... | collective-permute-start | bytes 3840008 | tf_op jit(solution)/shard_map/ppermute | solution.py:412
  436.9 41.1 %collective-permute-start.56 = (bf16[2,416,768]{2,1,0:T(8,128)(2,1)}, bf16[2,416,768]{2,1,0:T(8,128)(2,1)}, u32[]{:S(2)}, u32[]{:S(2)}) collective-permute-start(bf16[2,416,768]{2,1,0:T(8,128)(2,1)} %pad_maximum_fusion.15), channel_id=1, source_target_pairs={{0,8},{1,9},{2,10},{3,11},{4,12},{5,13},{6,14},{7,15},{8,0},{9,1},... | collective-permute-start | bytes 3833864 | tf_op jit(solution)/shard_map/ppermute | solution.py:412
  444.6 143.7 %collective-permute-start.63 = (bf16[4,200,1600]{2,1,0:T(8,128)(2,1)}, bf16[4,200,1600]{2,1,0:T(8,128)(2,1)}, u32[]{:S(2)}, u32[]{:S(2)}) collective-permute-start(bf16[4,200,1600]{2,1,0:T(8,128)(2,1)} %pad_maximum_fusion.4.refs_0_), channel_id=1, source_target_pairs={{0,4},{1,5},{2,6},{3,7},{4,0},{5,1},{6,2},{7,3},{8,12},{9,13},{10,... | collective-permute-start | bytes 7680008 | tf_op jit(solution)/shard_map/ppermute | solution.py:412
  449.7 45.8 %collective-permute-start.55 = (bf16[2,128,1600]{1,2,0:T(8,128)(2,1)}, bf16[2,128,1600]{1,2,0:T(8,128)(2,1)S(1)}, u32[]{:S(2)}, u32[]{:S(2)}) collective-permute-start(bf16[2,128,1600]{1,2,0:T(8,128)(2,1)} %copy.44), channel_id=1, source_target_pairs={{0,8},{1,9},{2,10},{3,11},{4,12},{5,13},{6,14},{7,15},{8,0},{9,1},... | collective-permute-start | bytes 2457608 | tf_op jit(solution)/shard_map/ppermute | solution.py:412
  475.4 125.2 %collective-permute-start.62 = (bf16[4,400,800]{2,1,0:T(8,128)(2,1)S(1)}, bf16[4,400,800]{2,1,0:T(8,128)(2,1)}, u32[]{:S(2)}, u32[]{:S(2)}) collective-permute-start(bf16[4,400,800]{2,1,0:T(8,128)(2,1)S(1)} %pad_maximum_fusion.1.refs_0_), channel_id=1, source_target_pairs={{0,8},{1,9},{2,10},{3,11},{4,12},{5,13},{6,14},{7,15},{8,0},{9,1},... | collective-permute-start | bytes 7680008 | tf_op jit(solution)/shard_map/ppermute | solution.py:412
  481.2 126.9 %collective-permute-start.60 = (bf16[4,416,768]{2,1,0:T(8,128)(2,1)}, bf16[4,416,768]{2,1,0:T(8,128)(2,1)}, u32[]{:S(2)}, u32[]{:S(2)}) collective-permute-start(bf16[4,416,768]{2,1,0:T(8,128)(2,1)} %pad_maximum_fusion.5.refs_0_), channel_id=1, source_target_pairs={{0,4},{1,5},{2,6},{3,7},{4,0},{5,1},{6,2},{7,3},{8,12},{9,13},{10,... | collective-permute-start | bytes 7667720 | tf_op jit(solution)/shard_map/ppermute | solution.py:412
  497.3 83.8 %collective-permute-start.58 = (bf16[2,56,1600]{2,1,0:T(8,128)(2,1)}, bf16[2,56,1600]{2,1,0:T(8,128)(2,1)}, u32[]{:S(2)}, u32[]{:S(2)}) collective-permute-start(bf16[2,56,1600]{2,1,0:T(8,128)(2,1)} %pad_maximum_fusion.19), channel_id=1, source_target_pairs={{0,4},{1,5},{2,6},{3,7},{4,0},{5,1},{6,2},{7,3},{8,12},{9,13},{10,... | collective-permute-start | bytes 1075208 | tf_op jit(solution)/shard_map/ppermute | solution.py:412
  499.6 87.2 %collective-permute-start.59 = (bf16[1,128,1600]{1,2,0:T(8,128)(2,1)}, bf16[1,128,1600]{1,2,0:T(8,128)(2,1)S(1)}, u32[]{:S(2)}, u32[]{:S(2)}) collective-permute-start(bf16[1,128,1600]{1,2,0:T(8,128)(2,1)} %slice.349), channel_id=1, source_target_pairs={{0,16},{1,17},{2,18},{3,19},{4,20},{5,21},{6,22},{7,23},{8,24},{9,... | collective-permute-start | bytes 1228808 | tf_op jit(solution)/shard_map/ppermute | solution.py:412
  (113 other events, 1342.2 us)

commit v3 on v2

--- a/solution.py
+++ b/solution.py
@@ -55,7 +55,8 @@
 
 UNROLLED = 1024
 BUMP = 2
-TURNS = "mdmuodmpuoudmupdgquqpqgudpqppuqgpp"
+SPLIT = ("down", "up", "qkv")
+TURNS = "mdmudmpudupmgduqpugqdqpuopqpopuqpg"
 
 
 def for_tiles(one, length, tile, key_axis):
@@ -418,8 +419,8 @@
         return self.swap(value, 0, 2)
 
 
-    def gather_wt(self, value, *others):
-        near = jnp.stack([value, after(self.x(value), *others)])
+    def gather_wt(self, value):
+        near = jnp.stack([value, self.x(value)])
         return [near, self.core(near)]
 
     def trade_wt(self, own, near, far):
@@ -441,12 +442,18 @@
         )[0]
 
 
-    def gather(self, value, bits):
+    def gather(self, value, bits, split):
         blocks = value[None]
-        for bit in bits:
+        for bit in bits[:-2]:
             (come,) = yield [(blocks, bit, 0)]
-            if bit != bits[-1]:
-                blocks = jnp.concatenate([blocks, come])
+            blocks = jnp.concatenate([blocks, come])
+        if split:
+            come, first = yield [(blocks, bits[-2], 0), (blocks, bits[-1], 0)]
+            (second,) = yield [(come, bits[-1], 0)]
+            return [blocks, come, first, second]
+        (come,) = yield [(blocks, bits[-2], 0)]
+        blocks = jnp.concatenate([blocks, come])
+        (come,) = yield [(blocks, bits[-1], 0)]
         return [blocks, come]
 
     def gathered(self, bits):
@@ -469,8 +476,11 @@
         return terms[0]
 
 
-    def gather_plane(self, value):
-        parts = [value, self.x(value), self.swap(value, 2, 0), self.swap(value, 2, 2)]
+    def plane_hops(self, value):
+        return [self.x(value), self.swap(value, 2, 0), self.swap(value, 2, 2)]
+
+    def gather_plane(self, value, come):
+        parts = [value] + come
         return jnp.concatenate(parts + [self.core(part) for part in parts])
 
     def sum_plane(self, near, far):
@@ -514,6 +524,9 @@
                 come = self.links.swap(self.last, dc, dw)
                 self.open.append(come)
             self.come[name].append(come)
+
+    def now(self, value):
+        return after(value, self.last)
 
     def run(self, turns):
         for name in turns:
@@ -584,19 +597,24 @@
     rest = [d for d in seen if d not in firsts]
     seen[1] = links.swap(own, 1, 0)
     for batch in (firsts[1:], rest):
-        sent = links.swap(jnp.concatenate([seen[d] for d in batch]), 1, 0)
+        sent = links.swap(after(jnp.concatenate([seen[d] for d in batch]), seen[1]), 1, 0)
         seen.update({d | 1: sent[i * rows : (i + 1) * rows] for i, d in enumerate(batch)})
     found = links.gather_wt(heads.pick(qkv_weight, small, c))
     wqkv = links.rows_wt(found, share)
     small = jnp.concatenate([part[:, share:].reshape(2, -1)[:, :entries] for part in found])
-    seen = jnp.concatenate([seen[d] for d in order])
+    word = seen[1][:16, :128]
+    for _ in range(5):
+        word = links.core(word)
+    last = seen[links.n - 1]
+    seen = after(jnp.concatenate([seen[d] for d in order]), word)
+    wqkv = after(wqkv, word)
 
     far_bits = links.bits[:1:-1]
     bits = {
         "down": [*far_bits, 2, 1],
-        "up": [*far_bits, 1, 2],
-        "qkv": [*far_bits, 2, 1],
-        "proj": [*far_bits, 1, 2],
+        "up": [*far_bits, 2, 1],
+        "qkv": [*far_bits, 1, 2],
+        "proj": [*far_bits, 2, 1],
         "up sum": [1, *far_bits],
         "down sum": [1, *far_bits],
         "proj sum": [1, 2, *far_bits],
@@ -607,7 +625,8 @@
         [(w ^ r) * 2 + half for r in range(m)],
         [up_weight],
     )
-    pieces = [pieces[0], pieces[1], after(pieces[2], found[0])]
+    wproj = links.gather_wt(proj_weight)
+    up_far = links.x(after(pieces[2], wproj[0]))
     wdown = lax.dynamic_slice_in_dim(down_weight, half * per, per, 0)
     grad_out = cotangent[0]
 
@@ -631,21 +650,23 @@
     wanted = ((wanted[:, None] ^ c) * 2 + jnp.arange(2, dtype=jnp.int32)).reshape(-1)
     place = jnp.sum(jnp.where(wanted[:, None] == table[None, :], slots[None, :], 0), axis=1)
 
-    grad_out_plane = links.gather_plane(after(grad_out, seen))
+    come = links.plane_hops(after(grad_out, last))
     heads_out, lse = attn_forward(qkv, place, slots, block, tile)
 
-    wproj = links.gather_wt(after(proj_weight, found[0]), heads_out)
-    wproj = links.rows_wt(wproj, share)
+    wproj = links.rows_wt([after(part, heads_out) for part in wproj], share)
     attended = lax.all_to_all(heads_out, "ctx", 0, 0, tiled=True)
-    attended = heads.join(after(attended, wproj))
-    far = after(links.x(pieces[2]), attended)
+    attended = heads.join(after(attended, wproj, up_far))
+    grad_out_plane = links.gather_plane(
+        after(grad_out, attended), [after(part, attended) for part in come]
+    )
+    far = after(up_far, attended)
     wup = [pieces[0], far[:1], links.core(jnp.concatenate([pieces[1], far[1:]]))]
     wup = links.rows_wt(wup, share)
     mid = own.astype(F32) + dot(attended, wproj) + bproj
     normed2, scale2 = standardize(mid)
     a2 = (normed2 * gains[1] + shifts[1]).astype(BF16)
 
-    a2_plane = links.gather_plane(a2)
+    a2_plane = links.gather_plane(a2, links.plane_hops(a2))
     grad_out32 = grad_out.astype(F32)
     middle = length // 2
     step = -(-(-(-per // nq)) // 8) * 8
@@ -685,7 +706,7 @@
             for d in links.halving(bits["down sum"])
         ]
         found = yield from links.halve(jnp.stack(found), bits["down sum"])
-        return (yield from links.gather(found, bits["down"]))
+        return (yield from links.gather(found, bits["down"], "down" in SPLIT))
 
     def up_chain():
         found = by_rows(over_rows(a2_plane, kept["grad_pre"]).astype(BF16))
@@ -700,7 +721,7 @@
             term = lax.dynamic_slice(found, (r, b % cut, 0, 0), (1, 1, share, per // cut))
             terms.append(term[0, 0])
         found = yield from links.halve(jnp.stack(terms), bits["up sum"])
-        return (yield from links.gather(found, bits["up"]))
+        return (yield from links.gather(found, bits["up"], "up" in SPLIT))
 
     def output_chain():
         hidden = kept["hidden"]
@@ -720,7 +741,7 @@
             for d in links.halving(bits["proj sum"])
         ]
         found = yield from links.halve(jnp.stack(found), bits["proj sum"])
-        return (yield from links.gather(found, bits["proj"]))
+        return (yield from links.gather(found, bits["proj"], "proj" in SPLIT))
 
     def input_chain():
         (come,) = yield [(kept["other"], 1, 0)]
@@ -761,7 +782,7 @@
             for r in (0, 2, 1, 3)
         ]
         found = yield from links.sum_wt(jnp.stack(pieces[:2]), jnp.stack(pieces[2:]))
-        return (yield from links.gather(found, bits["qkv"]))
+        return (yield from links.gather(found, bits["qkv"], "qkv" in SPLIT))
 
     chains = {
         "m": main_chain(),

time: 631 us -> 571 us (0.905)
  waiting for transfers between devices: 278 us -> 229 us
  local copies, waits for them, and re-layouts: 70.1 us -> 62.5 us
  starting transfers between devices: 71.3 us -> 77.9 us
    ppermute x64 -> x72, waiting for transfers between devices: 275 us -> 226 us  [swap(): return lax.ppermute(value, AXES, pairs)]
    concatenate x8 -> x5, other arithmetic: 17.6 us -> 6.07 us  [gather(): blocks = jnp.concatenate([blocks, come])]
    ppermute x64 -> x72, starting transfers between devices: 61.3 us -> 68.7 us  [swap(): return lax.ppermute(value, AXES, pairs)]
    unnamed x183 -> x165, local copies, waits for them, and re-layouts: 29.4 us -> 24.4 us
  transfers between devices with their start and end apart: 66 -> 74, of which waited for: 26 -> 28; matrix products, arithmetic and copies ran while one was open for 29% -> 29% of each run, Pallas kernels for 8% -> 9%
where the time goes in v3:
time: 571 us; the launch traced here: 563 us
  waiting for transfers between devices  229 us (40%)
  starting transfers between devices  77.9 us (14%)
  matrix products  67.9 us (12%)
  other arithmetic  66.9 us (12%)
  local copies, waits for them, and re-layouts  62.5 us (11%)
  Pallas kernels  56.2 us (10%)
    ppermute x72, waiting for transfers between devices, swap(): return lax.ppermute(value, AXES, pairs)  226 us
    ppermute x72, starting transfers between devices, swap(): return lax.ppermute(value, AXES, pairs)  68.7 us
    pallas_call x9, Pallas kernels, rearrange(): pl.pallas_call(kernel, out_shape=tuple((jax.ShapeDtypeStruct(o.shape, o.d...  35 us
    dot_general x6, matrix products, by_transpose(): lax.dot_general(left, right, (((1,), (1,)), ((), ())), preferred_element_...  25.3 us
    dot_general x7, matrix products, dot(): return jnp.dot(left, right, preferred_element_type=F32)  24.6 us
    unnamed x165, local copies, waits for them, and re-layouts  24.4 us
    convert_element_type x14, other arithmetic, add_low(): return (left.astype(F32) + right.astype(F32)).astype(BF16)  22.3 us
    dot_general x4, matrix products, over_rows(): lax.dot_general(left, right, (((0,), (0,)), ((), ())), preferred_element_...  18 us
  transfers between devices with their start and end apart: 74, of which 28 were waited for; matrix products, arithmetic and copies ran while one was open for 29% of the time, Pallas kernels for 9%

profile of v3, /device:TPU:0, one launch (start us, length us, event | category | flops | bytes accessed | tf_op | source)
XLA Modules:
  0.0 562.9 jit_solution(7824863427593386804)
XLA Ops:
  17.1 7.6 %collective-permute-done = bf16[128,1600]{0,1:T(8,128)(2,1)S(1)} collective-permute-done((bf16[128,1600]{0,1:T(8,128)(2,1)}, bf16[128,1600]{0,1:T(8,128)(2,1)S(1)}, u32[]{:S(2)}, u32[]{:S(2)}) %collective-permute-start) | collective-permute-done | bytes 409632 | tf_op jit(solution)/shard_map/ppermute | solution.py:413
  28.4 6.6 %collective-permute-done.1 = bf16[128,1600]{0,1:T(8,128)(2,1)} collective-permute-done((bf16[128,1600]{0,1:T(8,128)(2,1)S(1)}, bf16[128,1600]{0,1:T(8,128)(2,1)}, u32[]{:S(2)}, u32[]{:S(2)}) %collective-permute-start.1) | collective-permute-done | bytes 409632 | tf_op jit(solution)/shard_map/ppermute | solution.py:413
  35.8 5.0 shard_map.242
  42.4 13.8 %collective-permute-done.3 = bf16[128,1600]{0,1:T(8,128)(2,1)} collective-permute-done((bf16[128,1600]{0,1:T(8,128)(2,1)}, bf16[128,1600]{0,1:T(8,128)(2,1)}, u32[]{:S(2)}, u32[]{:S(2)}) %collective-permute-start.3) | collective-permute-done | bytes 409632 | tf_op jit(solution)/shard_map/ppermute | solution.py:413
  68.5 5.5 add_convert_fusion.3.qkv_ref
  74.0 6.7 %shard_map.240 = (bf16[8,128,256]{2,1,0:T(8,128)(2,1)S(1)}, f32[1024,128]{1,0:T(8,128)S(1)}) custom-call(s32[16]{0:T(128)S(1)} %select_reduce_fusion.place_ref, s32[16]{0:T(128)S(1)} %copy-done.14, bf16[1024,768]{1,0:T(8,128)(2,1)S(1)} %add_convert_fusion.3.qkv_ref), custom_call_target="tpu_custom_call" | custom-call | flops 1073741824 | bytes 2621440 | tf_op jit(solution)/shard_map/pallas_call | solution.py:200
  83.5 4.6 all-to-all-start
  94.0 5.3 shard_map.241
  105.4 5.0 fusion.85
  112.0 5.4 collective-permute-done.24
  125.9 8.8 %collective-permute-done.16 = bf16[128,1600]{0,1:T(8,128)(2,1)S(1)} collective-permute-done((bf16[128,1600]{0,1:T(8,128)(2,1)S(1)}, bf16[128,1600]{0,1:T(8,128)(2,1)S(1)}, u32[]{:S(2)}, u32[]{:S(2)}) %collective-permute-start.16) | collective-permute-done | bytes 409632 | tf_op jit(solution)/shard_map/ppermute | solution.py:413
  147.5 5.1 convert_reduce_fusion.2
  162.4 6.0 %convolution_convert_fusion.1 = bf16[1600,800]{1,0:T(8,128)(2,1)S(1)} fusion(bf16[1024,1600]{0,1:T(8,128)(2,1)} %copy-done.56, bf16[1024,800]{0,1:T(8,128)(2,1)} %copy-done.64), kind=kOutput, calls=%fused_computation.18 | convolution fusion | flops 2622720000 | bytes 7475200 | tf_op jit(solution)/shard_map/dot_general | solution.py:45
  181.0 12.7 %collective-permute-done.34 = bf16[2,200,1600]{2,1,0:T(8,128)(2,1)} collective-permute-done((bf16[2,200,1600]{2,1,0:T(8,128)(2,1)}, bf16[2,200,1600]{2,1,0:T(8,128)(2,1)}, u32[]{:S(2)}, u32[]{:S(2)}) %collective-permute-start.34) | collective-permute-done | bytes 1280032 | tf_op jit(solution)/shard_map/ppermute | solution.py:413
  213.0 4.6 all-to-all-start.1
  251.1 10.7 %shard_map.246 = bf16[1024,768]{1,0:T(8,128)(2,1)S(1)} custom-call(s32[16]{0:T(128)S(1)} %select_reduce_fusion.place_ref, s32[16]{0:T(128)S(1)} %copy-done.14, bf16[1024,768]{1,0:T(8,128)(2,1)S(1)} %copy-done.16, f32[1024,128]{1,0:T(8,128)S(1)} %copy-done.18, bf16[8,128,256]{2,1,0:T(8,128)(2,1)S(1)} %all-to-all-done.1.grad_ref), custom_call_target="tpu_custom_call" | custom-call | flops 2684354560 | bytes 4194304 | tf_op jit(solution)/shard_map/pallas_call | solution.py:220
  265.3 9.1 %fusion.16 = (bf16[1600]{0:T(1024)(128)(2,1)S(1)}, bf16[512,1600]{0,1:T(8,128)(2,1)}, f32[512,1600]{0,1:T(8,128)}) fusion(f32[1024,1600]{0,1:T(8,128)} %fusion.2, f32[512,1600]{0,1:T(8,128)} %fusion.46, bf16[1600,768]{1,0:T(8,128)(2,1)S(1)} %shard_map.239, bf16[1024,768]{1,0:T(8,128)(2,1)} %copy-done.1), kind=kOutput, calls=%fused_computation.29 | convolution fusion | flops 1262385664 | bytes 17992832 | tf_op jit(solution)/shard_map/dot_general | solution.py:49
  274.9 4.6 convolution_convert_fusion.3
  296.0 16.1 %collective-permute-done.46 = bf16[512,1600]{0,1:T(8,128)(2,1)} collective-permute-done((bf16[512,1600]{0,1:T(8,128)(2,1)}, bf16[512,1600]{0,1:T(8,128)(2,1)}, u32[]{:S(2)}, u32[]{:S(2)}) %collective-permute-start.46) | collective-permute-done | bytes 1638432 | tf_op jit(solution)/shard_map/ppermute | solution.py:413
  312.1 13.8 %collective-permute-done.44 = bf16[1,400,800]{2,1,0:T(8,128)(2,1)S(1)} collective-permute-done((bf16[1,400,800]{2,1,0:T(8,128)(2,1)S(1)}, bf16[1,400,800]{2,1,0:T(8,128)(2,1)S(1)}, u32[]{:S(2)}, u32[]{:S(2)}) %collective-permute-start.44) | collective-permute-done | bytes 640032 | tf_op jit(solution)/shard_map/ppermute | solution.py:413
  336.3 5.1 convolution_convert_fusion.5
  358.5 15.7 %collective-permute-done.47 = bf16[1,400,800]{2,1,0:T(8,128)(2,1)} collective-permute-done((bf16[1,400,800]{2,1,0:T(8,128)(2,1)}, bf16[1,400,800]{2,1,0:T(8,128)(2,1)}, u32[]{:S(2)}, u32[]{:S(2)}) %collective-permute-start.47) | collective-permute-done | bytes 640032 | tf_op jit(solution)/shard_map/ppermute | solution.py:413
  375.8 5.5 collective-permute-done.52
  384.3 20.6 %collective-permute-done.55 = bf16[2,56,1600]{2,1,0:T(8,128)(2,1)S(1)} collective-permute-done((bf16[2,56,1600]{2,1,0:T(8,128)(2,1)}, bf16[2,56,1600]{2,1,0:T(8,128)(2,1)S(1)}, u32[]{:S(2)}, u32[]{:S(2)}) %collective-permute-start.55) | collective-permute-done | bytes 358432 | tf_op jit(solution)/shard_map/ppermute | solution.py:413
  411.7 18.3 %collective-permute-done.57 = bf16[1,416,768]{2,1,0:T(8,128)(2,1)S(1)} collective-permute-done((bf16[1,416,768]{2,1,0:T(8,128)(2,1)}, bf16[1,416,768]{2,1,0:T(8,128)(2,1)S(1)}, u32[]{:S(2)}, u32[]{:S(2)}) %collective-permute-start.57) | collective-permute-done | bytes 639008 | tf_op jit(solution)/shard_map/ppermute | solution.py:413
  441.4 22.9 %collective-permute-done.61.refs_2_ = bf16[2,400,800]{2,1,0:T(8,128)(2,1)S(1)} collective-permute-done((bf16[2,400,800]{2,1,0:T(8,128)(2,1)S(1)}, bf16[2,400,800]{2,1,0:T(8,128)(2,1)S(1)}, u32[]{:S(2)}, u32[]{:S(2)}) %collective-permute-start.61) | collective-permute-done | bytes 1280032 | tf_op jit(solution)/shard_map/ppermute | solution.py:413
  469.0 17.4 %collective-permute-done.62.refs_1_ = bf16[2,416,768]{2,1,0:T(8,128)(2,1)} collective-permute-done((bf16[2,416,768]{2,1,0:T(8,128)(2,1)S(1)}, bf16[2,416,768]{2,1,0:T(8,128)(2,1)}, u32[]{:S(2)}, u32[]{:S(2)}) %collective-permute-start.62) | collective-permute-done | bytes 1277984 | tf_op jit(solution)/shard_map/ppermute | solution.py:413
  505.2 9.8 %collective-permute-done.65 = bf16[128,1600]{0,1:T(8,128)(2,1)S(1)} collective-permute-done((bf16[128,1600]{0,1:T(8,128)(2,1)}, bf16[128,1600]{0,1:T(8,128)(2,1)S(1)}, u32[]{:S(2)}, u32[]{:S(2)}) %collective-permute-start.65) | collective-permute-done | bytes 409632 | tf_op jit(solution)/shard_map/ppermute | solution.py:413
  517.7 7.4 %shard_map.250 = f32[1600,1600]{1,0:T(8,128)} custom-call(s32[8]{0:T(128)S(1)} %stack.245.numbers, bf16[2,200,1600]{2,1,0:T(8,128)(2,1)} %pad_maximum_fusion.11.refs_0_, bf16[2,200,1600]{2,1,0:T(8,128)(2,1)} %collective-permute-done.50.refs_1_, bf16[2,200,1600]{2,1,0:T(8,128)(2,1)} %collective-permute-done.71.refs_2_, bf16[2,200,1600]{2,1,0:T(8,128)(2,1)S(1)} %copy-done.10), custom_call_target="tpu_custom_call" | custom-call | bytes 15360000 | tf_op jit(solution)/shard_map/pallas_call | solution.py:238
  525.1 15.0 %collective-permute-done.67 = bf16[1,128,1600]{1,2,0:T(8,128)(2,1)S(1)} collective-permute-done((bf16[1,128,1600]{1,2,0:T(8,128)(2,1)S(1)}, bf16[1,128,1600]{1,2,0:T(8,128)(2,1)S(1)}, u32[]{:S(2)}, u32[]{:S(2)}) %collective-permute-start.67) | collective-permute-done | bytes 409632 | tf_op jit(solution)/shard_map/ppermute | solution.py:413
  543.9 7.1 %shard_map.249 = f32[400,6400]{1,0:T(8,128)} custom-call(s32[8]{0:T(128)S(1)} %stack.245.numbers, bf16[2,400,800]{2,1,0:T(8,128)(2,1)S(1)} %pad_maximum_fusion.9.refs_0_, bf16[2,400,800]{2,1,0:T(8,128)(2,1)} %collective-permute-done.58.refs_1_, bf16[2,400,800]{2,1,0:T(8,128)(2,1)S(1)} %copy-done.6, bf16[2,400,800]{2,1,0:T(8,128)(2,1)S(1)} %collective-permute-done.70.refs_3_), custom_call_target="tpu_custom_call" | custom-call | bytes 15360000 | tf_op jit(solution)/shard_map/pallas_call | solution.py:238
  556.1 6.0 %shard_map.247 = f32[400,4800]{1,0:T(8,128)} custom-call(s32[8]{0:T(128)S(1)} %stack.244.numbers, bf16[2,416,768]{2,1,0:T(8,128)(2,1)S(1)} %pad_maximum_fusion.4.refs_0_, bf16[2,416,768]{2,1,0:T(8,128)(2,1)} %collective-permute-done.62.refs_1_, bf16[2,416,768]{2,1,0:T(8,128)(2,1)} %collective-permute-done.64.refs_2_, bf16[2,416,768]{2,1,0:T(8,128)(2,1)S(1)} %copy-done.8), custom_call_target="tpu_custom_call" | custom-call | bytes 12791808 | tf_op jit(solution)/shard_map/pallas_call | solution.py:238
  (469 shorter events, 252.7 us)
Async XLA Ops:
  16.5 45.5 %collective-permute-start.13 = (bf16[400,1600]{1,0:T(8,128)(2,1)}, bf16[400,1600]{1,0:T(8,128)(2,1)}, u32[]{:S(2)}, u32[]{:S(2)}) collective-permute-start(bf16[400,1600]{1,0:T(8,128)(2,1)} %param.21), channel_id=1, source_target_pairs={{0,2},{1,3},{2,0},{3,1},{4,6},{5,7},{6,4},{7,5},{8,10},{9,11},{10,... | collective-permute-start | bytes 3840008 | tf_op jit(solution)/shard_map/ppermute | solution.py:413
  26.5 30.9 %collective-permute-start.5 = (bf16[256,1600]{0,1:T(8,128)(2,1)}, bf16[256,1600]{0,1:T(8,128)(2,1)}, u32[]{:S(2)}, u32[]{:S(2)}) collective-permute-start(bf16[256,1600]{0,1:T(8,128)(2,1)} %pad_maximum_fusion.13), channel_id=1, source_target_pairs={{0,4},{1,5},{2,6},{3,7},{4,0},{5,1},{6,2},{7,3},{8,12},{9,13},{10,... | collective-permute-start | bytes 2457608 | tf_op jit(solution)/shard_map/ppermute | solution.py:413
  65.5 34.5 %collective-permute-start.15 = (bf16[2,400,800]{2,1,0:T(8,128)(2,1)}, bf16[2,400,800]{2,1,0:T(8,128)(2,1)}, u32[]{:S(2)}, u32[]{:S(2)}) collective-permute-start(bf16[2,400,800]{2,1,0:T(8,128)(2,1)} %get-tuple-element.121), channel_id=1, source_target_pairs={{0,2},{1,3},{2,0},{3,1},{4,6},{5,7},{6,4},{7,5},{8,10},{9,11},{10,... | collective-permute-start | bytes 3840008 | tf_op jit(solution)/shard_map/ppermute | solution.py:413
  90.0 31.6 %collective-permute-start.25 = (bf16[128,1600]{0,1:T(8,128)(2,1)}, bf16[128,1600]{0,1:T(8,128)(2,1)}, u32[]{:S(2)}, u32[]{:S(2)}) collective-permute-start(bf16[128,1600]{0,1:T(8,128)(2,1)} %bitcast.156), channel_id=1, source_target_pairs={{0,8},{1,9},{2,10},{3,11},{4,12},{5,13},{6,14},{7,15},{8,0},{9,1},... | collective-permute-start | bytes 1228808 | tf_op jit(solution)/shard_map/ppermute | solution.py:413
  92.0 31.9 %collective-permute-start.26 = (bf16[128,1600]{0,1:T(8,128)(2,1)}, bf16[128,1600]{0,1:T(8,128)(2,1)}, u32[]{:S(2)}, u32[]{:S(2)}) collective-permute-start(bf16[128,1600]{0,1:T(8,128)(2,1)} %bitcast.157), channel_id=1, source_target_pairs={{0,10},{1,11},{2,8},{3,9},{4,14},{5,15},{6,12},{7,13},{8,2},{9,3},... | collective-permute-start | bytes 1228808 | tf_op jit(solution)/shard_map/ppermute | solution.py:413
  161.8 31.8 %collective-permute-start.34 = (bf16[2,200,1600]{2,1,0:T(8,128)(2,1)}, bf16[2,200,1600]{2,1,0:T(8,128)(2,1)}, u32[]{:S(2)}, u32[]{:S(2)}) collective-permute-start(bf16[2,200,1600]{2,1,0:T(8,128)(2,1)} %pad_maximum_fusion.10), channel_id=1, source_target_pairs={{0,4},{1,5},{2,6},{3,7},{4,0},{5,1},{6,2},{7,3},{8,12},{9,13},{10,... | collective-permute-start | bytes 3840008 | tf_op jit(solution)/shard_map/ppermute | solution.py:413
  179.5 48.7 %collective-permute-start.32 = (bf16[2,400,800]{2,1,0:T(8,128)(2,1)}, bf16[2,400,800]{2,1,0:T(8,128)(2,1)}, u32[]{:S(2)}, u32[]{:S(2)}) collective-permute-start(bf16[2,400,800]{2,1,0:T(8,128)(2,1)} %pad_maximum_fusion.6), channel_id=1, source_target_pairs={{0,2},{1,3},{2,0},{3,1},{4,6},{5,7},{6,4},{7,5},{8,10},{9,11},{10,... | collective-permute-start | bytes 3840008 | tf_op jit(solution)/shard_map/ppermute | solution.py:413
  196.3 38.5 %collective-permute-start.38 = (bf16[1,200,1600]{2,1,0:T(8,128)(2,1)}, bf16[1,200,1600]{2,1,0:T(8,128)(2,1)}, u32[]{:S(2)}, u32[]{:S(2)}) collective-permute-start(bf16[1,200,1600]{2,1,0:T(8,128)(2,1)} %slice.342), channel_id=1, source_target_pairs={{0,16},{1,17},{2,18},{3,19},{4,20},{5,21},{6,22},{7,23},{8,24},{9,... | collective-permute-start | bytes 1920008 | tf_op jit(solution)/shard_map/ppermute | solution.py:413
  213.0 35.6 %all-to-all-start.1 = ((bf16[8,128,256]{2,1,0:T(8,128)(2,1)}), bf16[8,128,256]{2,1,0:T(8,128)(2,1)S(1)}, u32[]{:S(2)}, u32[]{:S(2)}) async-start(bf16[8,128,256]{2,1,0:T(8,128)(2,1)} %shard_map.245), calls=%async_computation.1 | async-start | bytes 1048576 | tf_op jit(solution)/shard_map/all_to_all | solution.py:522
  237.0 42.5 %collective-permute-start.40 = (bf16[1,200,1600]{2,1,0:T(8,128)(2,1)}, bf16[1,200,1600]{2,1,0:T(8,128)(2,1)}, u32[]{:S(2)}, u32[]{:S(2)}) collective-permute-start(bf16[1,200,1600]{2,1,0:T(8,128)(2,1)} %add_convert_fusion.10), channel_id=1, source_target_pairs={{0,16},{1,17},{2,18},{3,19},{4,20},{5,21},{6,22},{7,23},{8,24},{9,... | collective-permute-start | bytes 1920008 | tf_op jit(solution)/shard_map/ppermute | solution.py:413
  242.5 46.1 %collective-permute-start.39 = (bf16[2,400,800]{2,1,0:T(8,128)(2,1)}, bf16[2,400,800]{2,1,0:T(8,128)(2,1)}, u32[]{:S(2)}, u32[]{:S(2)}) collective-permute-start(bf16[2,400,800]{2,1,0:T(8,128)(2,1)} %pad_maximum_fusion.8), channel_id=1, source_target_pairs={{0,4},{1,5},{2,6},{3,7},{4,0},{5,1},{6,2},{7,3},{8,12},{9,13},{10,... | collective-permute-start | bytes 3840008 | tf_op jit(solution)/shard_map/ppermute | solution.py:413
  247.2 43.9 %collective-permute-start.45 = (bf16[400,1600]{1,0:T(8,128)(2,1)}, bf16[400,1600]{1,0:T(8,128)(2,1)}, u32[]{:S(2)}, u32[]{:S(2)}) collective-permute-start(bf16[400,1600]{1,0:T(8,128)(2,1)} %fusion.18), channel_id=1, source_target_pairs={{0,2},{1,3},{2,0},{3,1},{4,6},{5,7},{6,4},{7,5},{8,10},{9,11},{10,... | collective-permute-start | bytes 3840008 | tf_op jit(solution)/shard_map/ppermute | solution.py:413
  274.4 37.7 %collective-permute-start.46 = (bf16[512,1600]{0,1:T(8,128)(2,1)}, bf16[512,1600]{0,1:T(8,128)(2,1)}, u32[]{:S(2)}, u32[]{:S(2)}) collective-permute-start(bf16[512,1600]{0,1:T(8,128)(2,1)} %get-tuple-element.156), channel_id=1, source_target_pairs={{0,4},{1,5},{2,6},{3,7},{4,0},{5,1},{6,2},{7,3},{8,12},{9,13},{10,... | collective-permute-start | bytes 4915208 | tf_op jit(solution)/shard_map/ppermute | solution.py:413
  282.0 49.3 %collective-permute-start.50 = (bf16[2,200,1600]{2,1,0:T(8,128)(2,1)}, bf16[2,200,1600]{2,1,0:T(8,128)(2,1)}, u32[]{:S(2)}, u32[]{:S(2)}) collective-permute-start(bf16[2,200,1600]{2,1,0:T(8,128)(2,1)} %pad_maximum_fusion.11.refs_0_), channel_id=1, source_target_pairs={{0,8},{1,9},{2,10},{3,11},{4,12},{5,13},{6,14},{7,15},{8,0},{9,1},... | collective-permute-start | bytes 3840008 | tf_op jit(solution)/shard_map/ppermute | solution.py:413
  291.0 34.9 %collective-permute-start.44 = (bf16[1,400,800]{2,1,0:T(8,128)(2,1)S(1)}, bf16[1,400,800]{2,1,0:T(8,128)(2,1)S(1)}, u32[]{:S(2)}, u32[]{:S(2)}) collective-permute-start(bf16[1,400,800]{2,1,0:T(8,128)(2,1)S(1)} %slice.346), channel_id=1, source_target_pairs={{0,16},{1,17},{2,18},{3,19},{4,20},{5,21},{6,22},{7,23},{8,24},{9,... | collective-permute-start | bytes 1920008 | tf_op jit(solution)/shard_map/ppermute | solution.py:413
  291.1 40.3 %collective-permute-start.49 = (bf16[2,416,768]{2,1,0:T(8,128)(2,1)}, bf16[2,416,768]{2,1,0:T(8,128)(2,1)}, u32[]{:S(2)}, u32[]{:S(2)}) collective-permute-start(bf16[2,416,768]{2,1,0:T(8,128)(2,1)} %pad_maximum_fusion.12), channel_id=1, source_target_pairs={{0,1},{1,0},{2,3},{3,2},{4,5},{5,4},{6,7},{7,6},{8,9},{9,8},{10,11... | collective-permute-start | bytes 3833864 | tf_op jit(solution)/shard_map/ppermute | solution.py:413
  335.8 45.5 %collective-permute-start.53 = (bf16[2,200,1600]{2,1,0:T(8,128)(2,1)}, bf16[2,200,1600]{2,1,0:T(8,128)(2,1)S(1)}, u32[]{:S(2)}, u32[]{:S(2)}) collective-permute-start(bf16[2,200,1600]{2,1,0:T(8,128)(2,1)} %collective-permute-done.50.refs_1_), channel_id=1, source_target_pairs={{0,4},{1,5},{2,6},{3,7},{4,0},{5,1},{6,2},{7,3},{8,12},{9,13},{10,... | collective-permute-start | bytes 3840008 | tf_op jit(solution)/shard_map/ppermute | solution.py:413
  341.4 32.8 %collective-permute-start.47 = (bf16[1,400,800]{2,1,0:T(8,128)(2,1)}, bf16[1,400,800]{2,1,0:T(8,128)(2,1)}, u32[]{:S(2)}, u32[]{:S(2)}) collective-permute-start(bf16[1,400,800]{2,1,0:T(8,128)(2,1)} %add_convert_fusion.9), channel_id=1, source_target_pairs={{0,16},{1,17},{2,18},{3,19},{4,20},{5,21},{6,22},{7,23},{8,24},{9,... | collective-permute-start | bytes 1920008 | tf_op jit(solution)/shard_map/ppermute | solution.py:413
  346.0 35.2 %collective-permute-start.52 = (bf16[2,128,1600]{1,2,0:T(8,128)(2,1)}, bf16[2,128,1600]{1,2,0:T(8,128)(2,1)S(1)}, u32[]{:S(2)}, u32[]{:S(2)}) collective-permute-start(bf16[2,128,1600]{1,2,0:T(8,128)(2,1)} %copy.43), channel_id=1, source_target_pairs={{0,8},{1,9},{2,10},{3,11},{4,12},{5,13},{6,14},{7,15},{8,0},{9,1},... | collective-permute-start | bytes 2457608 | tf_op jit(solution)/shard_map/ppermute | solution.py:413
  356.1 48.8 %collective-permute-start.55 = (bf16[2,56,1600]{2,1,0:T(8,128)(2,1)}, bf16[2,56,1600]{2,1,0:T(8,128)(2,1)S(1)}, u32[]{:S(2)}, u32[]{:S(2)}) collective-permute-start(bf16[2,56,1600]{2,1,0:T(8,128)(2,1)} %slice.353), channel_id=1, source_target_pairs={{0,8},{1,9},{2,10},{3,11},{4,12},{5,13},{6,14},{7,15},{8,0},{9,1},... | collective-permute-start | bytes 1075208 | tf_op jit(solution)/shard_map/ppermute | solution.py:413
  375.7 58.1 %collective-permute-start.58 = (bf16[2,400,800]{2,1,0:T(8,128)(2,1)S(1)}, bf16[2,400,800]{2,1,0:T(8,128)(2,1)}, u32[]{:S(2)}, u32[]{:S(2)}) collective-permute-start(bf16[2,400,800]{2,1,0:T(8,128)(2,1)S(1)} %pad_maximum_fusion.9.refs_0_), channel_id=1, source_target_pairs={{0,8},{1,9},{2,10},{3,11},{4,12},{5,13},{6,14},{7,15},{8,0},{9,1},... | collective-permute-start | bytes 3840008 | tf_op jit(solution)/shard_map/ppermute | solution.py:413
  381.3 55.2 %collective-permute-start.54 = (bf16[512,1600]{0,1:T(8,128)(2,1)}, bf16[512,1600]{0,1:T(8,128)(2,1)}, u32[]{:S(2)}, u32[]{:S(2)}) collective-permute-start(bf16[512,1600]{0,1:T(8,128)(2,1)} %convolution_convert_fusion.5), channel_id=1, source_target_pairs={{0,1},{1,0},{2,3},{3,2},{4,5},{5,4},{6,7},{7,6},{8,9},{9,8},{10,11... | collective-permute-start | bytes 4915208 | tf_op jit(solution)/shard_map/ppermute | solution.py:413
  383.2 46.8 %collective-permute-start.57 = (bf16[1,416,768]{2,1,0:T(8,128)(2,1)}, bf16[1,416,768]{2,1,0:T(8,128)(2,1)S(1)}, u32[]{:S(2)}, u32[]{:S(2)}) collective-permute-start(bf16[1,416,768]{2,1,0:T(8,128)(2,1)} %fusion.48), channel_id=1, source_target_pairs={{0,16},{1,17},{2,18},{3,19},{4,20},{5,21},{6,22},{7,23},{8,24},{9,... | collective-permute-start | bytes 1916936 | tf_op jit(solution)/shard_map/ppermute | solution.py:413
  410.1 85.3 %collective-permute-start.71 = (bf16[2,200,1600]{2,1,0:T(8,128)(2,1)}, bf16[2,200,1600]{2,1,0:T(8,128)(2,1)}, u32[]{:S(2)}, u32[]{:S(2)}) collective-permute-start(bf16[2,200,1600]{2,1,0:T(8,128)(2,1)} %pad_maximum_fusion.11.refs_0_), channel_id=1, source_target_pairs={{0,4},{1,5},{2,6},{3,7},{4,0},{5,1},{6,2},{7,3},{8,12},{9,13},{10,... | collective-permute-start | bytes 3840008 | tf_op jit(solution)/shard_map/ppermute | solution.py:413
  430.0 34.3 %collective-permute-start.61 = (bf16[2,400,800]{2,1,0:T(8,128)(2,1)S(1)}, bf16[2,400,800]{2,1,0:T(8,128)(2,1)S(1)}, u32[]{:S(2)}, u32[]{:S(2)}) collective-permute-start(bf16[2,400,800]{2,1,0:T(8,128)(2,1)S(1)} %pad_maximum_fusion.9.refs_0_), channel_id=1, source_target_pairs={{0,4},{1,5},{2,6},{3,7},{4,0},{5,1},{6,2},{7,3},{8,12},{9,13},{10,... | collective-permute-start | bytes 3840008 | tf_op jit(solution)/shard_map/ppermute | solution.py:413
  433.8 52.6 %collective-permute-start.62 = (bf16[2,416,768]{2,1,0:T(8,128)(2,1)S(1)}, bf16[2,416,768]{2,1,0:T(8,128)(2,1)}, u32[]{:S(2)}, u32[]{:S(2)}) collective-permute-start(bf16[2,416,768]{2,1,0:T(8,128)(2,1)S(1)} %pad_maximum_fusion.4.refs_0_), channel_id=1, source_target_pairs={{0,4},{1,5},{2,6},{3,7},{4,0},{5,1},{6,2},{7,3},{8,12},{9,13},{10,... | collective-permute-start | bytes 3833864 | tf_op jit(solution)/shard_map/ppermute | solution.py:413
  436.4 61.6 %collective-permute-start.64 = (bf16[2,416,768]{2,1,0:T(8,128)(2,1)S(1)}, bf16[2,416,768]{2,1,0:T(8,128)(2,1)}, u32[]{:S(2)}, u32[]{:S(2)}) collective-permute-start(bf16[2,416,768]{2,1,0:T(8,128)(2,1)S(1)} %pad_maximum_fusion.4.refs_0_), channel_id=1, source_target_pairs={{0,8},{1,9},{2,10},{3,11},{4,12},{5,13},{6,14},{7,15},{8,0},{9,1},... | collective-permute-start | bytes 3833864 | tf_op jit(solution)/shard_map/ppermute | solution.py:413
  436.5 50.0 %collective-permute-start.60 = (bf16[1,56,1600]{2,1,0:T(8,128)(2,1)S(1)}, bf16[1,56,1600]{2,1,0:T(8,128)(2,1)S(1)}, u32[]{:S(2)}, u32[]{:S(2)}) collective-permute-start(bf16[1,56,1600]{2,1,0:T(8,128)(2,1)S(1)} %add_convert_fusion.16), channel_id=1, source_target_pairs={{0,16},{1,17},{2,18},{3,19},{4,20},{5,21},{6,22},{7,23},{8,24},{9,... | collective-permute-start | bytes 537608 | tf_op jit(solution)/shard_map/ppermute | solution.py:413
  465.4 35.9 %collective-permute-start.59 = (bf16[128,1600]{0,1:T(8,128)(2,1)}, bf16[128,1600]{0,1:T(8,128)(2,1)}, u32[]{:S(2)}, u32[]{:S(2)}) collective-permute-start(bf16[128,1600]{0,1:T(8,128)(2,1)} %get-tuple-element.190), channel_id=1, source_target_pairs={{0,10},{1,11},{2,8},{3,9},{4,14},{5,15},{6,12},{7,13},{8,2},{9,3},... | collective-permute-start | bytes 1228808 | tf_op jit(solution)/shard_map/ppermute | solution.py:413
  498.0 45.9 %collective-permute-start.70 = (bf16[2,400,800]{2,1,0:T(8,128)(2,1)}, bf16[2,400,800]{2,1,0:T(8,128)(2,1)S(1)}, u32[]{:S(2)}, u32[]{:S(2)}) collective-permute-start(bf16[2,400,800]{2,1,0:T(8,128)(2,1)} %collective-permute-done.58.refs_1_), channel_id=1, source_target_pairs={{0,4},{1,5},{2,6},{3,7},{4,0},{5,1},{6,2},{7,3},{8,12},{9,13},{10,... | collective-permute-start | bytes 3840008 | tf_op jit(solution)/shard_map/ppermute | solution.py:413
  501.4 49.6 %collective-permute-start.68 = (bf16[2,416,768]{2,1,0:T(8,128)(2,1)}, bf16[2,416,768]{2,1,0:T(8,128)(2,1)S(1)}, u32[]{:S(2)}, u32[]{:S(2)}) collective-permute-start(bf16[2,416,768]{2,1,0:T(8,128)(2,1)} %collective-permute-done.62.refs_1_), channel_id=1, source_target_pairs={{0,8},{1,9},{2,10},{3,11},{4,12},{5,13},{6,14},{7,15},{8,0},{9,1},... | collective-permute-start | bytes 3833864 | tf_op jit(solution)/shard_map/ppermute | solution.py:413
  504.6 37.0 %collective-permute-start.69 = (bf16[4,56,1600]{2,1,0:T(8,128)(2,1)S(1)}, bf16[4,56,1600]{2,1,0:T(8,128)(2,1)S(1)}, u32[]{:S(2)}, u32[]{:S(2)}) collective-permute-start(bf16[4,56,1600]{2,1,0:T(8,128)(2,1)S(1)} %pad_maximum_fusion.15.refs_0_), channel_id=1, source_target_pairs={{0,4},{1,5},{2,6},{3,7},{4,0},{5,1},{6,2},{7,3},{8,12},{9,13},{10,... | collective-permute-start | bytes 2150408 | tf_op jit(solution)/shard_map/ppermute | solution.py:413
  (112 other events, 1495.0 us)

commit v4 on v3

--- a/solution.py
+++ b/solution.py
@@ -54,7 +54,7 @@
 
 
 UNROLLED = 1024
-BUMP = 2
+BUMP = 1
 SPLIT = ("down", "up", "qkv")
 TURNS = "mdmudmpudupmgduqpugqdqpuopqpopuqpg"
 
@@ -365,8 +365,15 @@
             r += 1
 
 
-def lay_kernel(plan, numbers, *refs):
-    blocks, out_ref, held = refs[:-2], refs[-2], refs[-1]
+def lay_kernel(plan, more, numbers, *refs):
+    refs, held = refs[:-1], refs[-1]
+    if more:
+        refs, sum_ref = refs[:-1], refs[-1]
+        last = slice(held.shape[1] - more, held.shape[1])
+        sum_ref[...] = sum(
+            ref[k, last, :].astype(F32) for ref in refs[:-1] for k in range(ref.shape[0])
+        )
+    blocks, out_ref = refs[:-1], refs[-1]
     r = 0
     for ref in blocks:
         for k in range(ref.shape[0]):
@@ -376,14 +383,16 @@
         out_ref[rows, cols] = held[b, from_rows, from_cols].astype(F32)
 
 
-def lay(blocks, numbers, plan, shape):
+def lay(blocks, numbers, plan, shape, more=0):
     steps = [
         (b, slice(r, r + h), slice(q, q + v), slice(tr, tr + h), slice(tq, tq + v))
         for b, (r, q), (h, v), (tr, tq) in plan
     ]
     scratch = [pltpu.VMEM((len(numbers),) + blocks[0].shape[1:], BF16)]
-    kernel = functools.partial(lay_kernel, steps)
-    return rearrange(kernel, [shaped(shape, F32)], numbers, blocks, scratch)[0]
+    kernel = functools.partial(lay_kernel, steps, more)
+    outs = [shaped(shape, F32)] + ([shaped((more, blocks[0].shape[2]), F32)] if more else [])
+    found = rearrange(kernel, outs, numbers, blocks, scratch)
+    return found if more else found[0]
 
 
 def by_rows(value):
@@ -588,7 +597,8 @@
         ]
     )
     entries = small.shape[0]
-    more = -(-(-(-entries // (3 * heads.wide))) // 16) * 16
+    take = share if 3 * heads.wide >= share else share // 2
+    more = -(-max(-(-entries // (3 * heads.wide)), entries // take) // 16) * 16
     small = jnp.pad(small, [(0, more * 3 * heads.wide - entries)]).reshape(more, 3 * heads.wide)
     seen = {0: own}
     for bit in reversed(links.bits[1:]):
@@ -724,7 +734,7 @@
         return (yield from links.gather(found, bits["up"], "up" in SPLIT))
 
     def output_chain():
-        hidden = kept["hidden"]
+        hidden = traffic.now(kept["hidden"])
         near_part = dot(hidden[:near], wdown).astype(BF16)
         far_part = dot(hidden[near:], wdown).astype(BF16)
         return (yield from links.sum_plane(lambda: near_part, far_part))
@@ -757,7 +767,7 @@
             jnp.zeros((m * 2, per), F32),
             jnp.sum(kept["grad_pre"].astype(F32), axis=0)[None],
             (w * 2 + half, 0),
-        ).reshape(m, hid // m)
+        ).reshape(m, hid // m // share, share)
         vectors = [
             kept["d_gain1"],
             jnp.sum(grad_a2 * normed2, axis=0),
@@ -768,9 +778,12 @@
             jnp.sum(grad_proj.astype(F32), axis=0),
             jnp.sum(grad_out32, axis=0),
         ]
-        vectors = jnp.concatenate([v.reshape(m, share) for v in vectors] + [d_up_bias], axis=1)
-        vectors = jnp.pad(vectors, [(0, 0), (0, more * 3 * heads.wide - entries)])
-        vectors = vectors.astype(BF16).reshape(m * more, 3 * heads.wide)
+        vectors = jnp.stack([v.reshape(m, share) for v in vectors], axis=1)
+        vectors = jnp.concatenate([vectors, d_up_bias], axis=1).astype(BF16)
+        vectors = vectors.reshape(m, entries // take, take)
+        beside = (more - entries // take, 3 * heads.wide - take)
+        vectors = jnp.pad(vectors, [(0, 0), (0, beside[0]), (0, beside[1])])
+        vectors = vectors.reshape(m * more, 3 * heads.wide)
         found = by_rows(over_rows(a1, grad_qkv).astype(BF16))
         pieces = [
             jnp.concatenate(
@@ -847,24 +860,21 @@
         for t in range(3)
         for p in range(-(-width // 128))
     ]
-    d_qkv_weight = lay(d_qkv, owners("qkv"), plan, (share, 3 * width))
-    vectors = sum(jnp.sum(part[:, share:].astype(F32), axis=0) for part in d_qkv)
-    vectors = vectors.reshape(-1)[:entries]
-    eight = vectors[: 8 * share].reshape(8, share)
-
+    d_qkv_weight, vectors = lay(d_qkv, owners("qkv"), plan, (share, 3 * width), more)
+    vectors = vectors[: entries // take, :take].reshape(entries // share, share)
     return (
         output.astype(BF16)[None],
         d_tokens.astype(BF16)[None],
-        eight[0:2],
-        eight[2:4],
+        vectors[0:2],
+        vectors[2:4],
         d_qkv_weight,
-        eight[4:6],
+        vectors[4:6],
         d_proj_weight,
-        eight[6],
+        vectors[6],
         d_up_weight,
-        vectors[8 * share :],
+        vectors[8 : 8 + hid // width].reshape(-1),
         d_down_weight,
-        eight[7],
+        vectors[7],
     )
 
 

time: 571 us -> 560 us (0.981)
  waiting for transfers between devices: 229 us -> 238 us
    ppermute x72 -> x71, waiting for transfers between devices: 226 us -> 234 us  [swap(): return lax.ppermute(value, AXES, pairs)]
    ppermute x72 -> x71, starting transfers between devices: 68.7 us -> 67.6 us  [swap(): return lax.ppermute(value, AXES, pairs)]
    unnamed x165 -> x153, local copies, waits for them, and re-layouts: 24.4 us -> 23.6 us
  transfers between devices with their start and end apart: 74 -> 73, of which waited for: 28 -> 27; matrix products, arithmetic and copies ran while one was open for 29% -> 27% of each run, Pallas kernels for 9% -> 9%
where the time goes in v4:
time: 560 us; the launch traced here: 553 us
  waiting for transfers between devices  238 us (42%)
  starting transfers between devices  76.8 us (14%)
  matrix products  62.2 us (11%)
  other arithmetic  61.5 us (11%)
  local copies, waits for them, and re-layouts  57.2 us (10%)
  Pallas kernels  55.3 us (10%)
    ppermute x71, waiting for transfers between devices, swap(): return lax.ppermute(value, AXES, pairs)  234 us
    ppermute x71, starting transfers between devices, swap(): return lax.ppermute(value, AXES, pairs)  67.6 us
    pallas_call x9, Pallas kernels, rearrange(): pl.pallas_call(kernel, out_shape=tuple((jax.ShapeDtypeStruct(o.shape, o.d...  34.2 us
    dot_general x6, matrix products, by_transpose(): lax.dot_general(left, right, (((1,), (1,)), ((), ())), preferred_element_...  25.4 us
    unnamed x153, local copies, waits for them, and re-layouts  23.6 us
    convert_element_type x14, other arithmetic, add_low(): return (left.astype(F32) + right.astype(F32)).astype(BF16)  21.7 us
    dot_general x7, matrix products, dot(): return jnp.dot(left, right, preferred_element_type=F32)  21.2 us
    dot_general x4, matrix products, over_rows(): lax.dot_general(left, right, (((0,), (0,)), ((), ())), preferred_element_...  15.6 us
  transfers between devices with their start and end apart: 73, of which 27 were waited for; matrix products, arithmetic and copies ran while one was open for 27% of the time, Pallas kernels for 9%

profile of v4, /device:TPU:0, one launch (start us, length us, event | category | flops | bytes accessed | tf_op | source)
XLA Modules:
  0.0 553.2 jit_solution(2458895291288466926)
XLA Ops:
  17.1 7.6 %collective-permute-done = bf16[128,1600]{0,1:T(8,128)(2,1)S(1)} collective-permute-done((bf16[128,1600]{0,1:T(8,128)(2,1)}, bf16[128,1600]{0,1:T(8,128)(2,1)S(1)}, u32[]{:S(2)}, u32[]{:S(2)}) %collective-permute-start) | collective-permute-done | bytes 409632 | tf_op jit(solution)/shard_map/ppermute | solution.py:422
  28.4 6.6 %collective-permute-done.1 = bf16[128,1600]{0,1:T(8,128)(2,1)} collective-permute-done((bf16[128,1600]{0,1:T(8,128)(2,1)S(1)}, bf16[128,1600]{0,1:T(8,128)(2,1)}, u32[]{:S(2)}, u32[]{:S(2)}) %collective-permute-start.1) | collective-permute-done | bytes 409632 | tf_op jit(solution)/shard_map/ppermute | solution.py:422
  35.8 5.0 shard_map.242
  42.4 13.8 %collective-permute-done.3 = bf16[128,1600]{0,1:T(8,128)(2,1)} collective-permute-done((bf16[128,1600]{0,1:T(8,128)(2,1)}, bf16[128,1600]{0,1:T(8,128)(2,1)}, u32[]{:S(2)}, u32[]{:S(2)}) %collective-permute-start.3) | collective-permute-done | bytes 409632 | tf_op jit(solution)/shard_map/ppermute | solution.py:422
  68.5 5.5 add_convert_fusion.3.qkv_ref
  74.1 6.7 %shard_map.240 = (bf16[8,128,256]{2,1,0:T(8,128)(2,1)S(1)}, f32[1024,128]{1,0:T(8,128)S(1)}) custom-call(s32[16]{0:T(128)S(1)} %select_reduce_fusion.place_ref, s32[16]{0:T(128)S(1)} %copy-done.14, bf16[1024,768]{1,0:T(8,128)(2,1)S(1)} %add_convert_fusion.3.qkv_ref), custom_call_target="tpu_custom_call" | custom-call | flops 1073741824 | bytes 2621440 | tf_op jit(solution)/shard_map/pallas_call | solution.py:200
  94.1 5.3 shard_map.241
  105.4 5.0 fusion.85
  112.1 5.4 collective-permute-done.24
  125.9 8.8 %collective-permute-done.16 = bf16[128,1600]{0,1:T(8,128)(2,1)S(1)} collective-permute-done((bf16[128,1600]{0,1:T(8,128)(2,1)S(1)}, bf16[128,1600]{0,1:T(8,128)(2,1)S(1)}, u32[]{:S(2)}, u32[]{:S(2)}) %collective-permute-start.16) | collective-permute-done | bytes 409632 | tf_op jit(solution)/shard_map/ppermute | solution.py:422
  147.6 5.1 convert_reduce_fusion.2
  162.5 6.0 %convolution_convert_fusion.1 = bf16[1600,800]{1,0:T(8,128)(2,1)S(1)} fusion(bf16[1024,1600]{0,1:T(8,128)(2,1)} %copy-done.48, bf16[1024,800]{0,1:T(8,128)(2,1)} %copy-done.56), kind=kOutput, calls=%fused_computation.18 | convolution fusion | flops 2622720000 | bytes 7475200 | tf_op jit(solution)/shard_map/dot_general | solution.py:45
  181.0 12.7 %collective-permute-done.34 = bf16[2,200,1600]{2,1,0:T(8,128)(2,1)} collective-permute-done((bf16[2,200,1600]{2,1,0:T(8,128)(2,1)}, bf16[2,200,1600]{2,1,0:T(8,128)(2,1)}, u32[]{:S(2)}, u32[]{:S(2)}) %collective-permute-start.34) | collective-permute-done | bytes 1280032 | tf_op jit(solution)/shard_map/ppermute | solution.py:422
  210.6 4.7 all-to-all-start.1
  223.1 5.2 collective-permute-done.32
  251.1 10.7 %shard_map.246 = bf16[1024,768]{1,0:T(8,128)(2,1)S(1)} custom-call(s32[16]{0:T(128)S(1)} %select_reduce_fusion.place_ref, s32[16]{0:T(128)S(1)} %copy-done.14, bf16[1024,768]{1,0:T(8,128)(2,1)S(1)} %copy-done.16, f32[1024,128]{1,0:T(8,128)S(1)} %copy-done.18, bf16[8,128,256]{2,1,0:T(8,128)(2,1)S(1)} %all-to-all-done.1.grad_ref), custom_call_target="tpu_custom_call" | custom-call | flops 2684354560 | bytes 4194304 | tf_op jit(solution)/shard_map/pallas_call | solution.py:220
  265.3 9.2 %fusion.16 = (bf16[1600]{0:T(1024)(128)(2,1)S(1)}, bf16[512,1600]{0,1:T(8,128)(2,1)}, f32[512,1600]{0,1:T(8,128)}) fusion(f32[1024,1600]{0,1:T(8,128)} %fusion.2, f32[512,1600]{0,1:T(8,128)} %fusion.46, bf16[1600,768]{1,0:T(8,128)(2,1)S(1)} %shard_map.239, bf16[1024,768]{1,0:T(8,128)(2,1)} %copy-done.1), kind=kOutput, calls=%fused_computation.29 | convolution fusion | flops 1262385664 | bytes 17992832 | tf_op jit(solution)/shard_map/dot_general | solution.py:49
  275.0 4.6 convolution_convert_fusion.3
  295.2 16.9 %collective-permute-done.45 = bf16[512,1600]{0,1:T(8,128)(2,1)} collective-permute-done((bf16[512,1600]{0,1:T(8,128)(2,1)}, bf16[512,1600]{0,1:T(8,128)(2,1)}, u32[]{:S(2)}, u32[]{:S(2)}) %collective-permute-start.45) | collective-permute-done | bytes 1638432 | tf_op jit(solution)/shard_map/ppermute | solution.py:422
  312.1 13.8 %collective-permute-done.43 = bf16[1,400,800]{2,1,0:T(8,128)(2,1)S(1)} collective-permute-done((bf16[1,400,800]{2,1,0:T(8,128)(2,1)S(1)}, bf16[1,400,800]{2,1,0:T(8,128)(2,1)S(1)}, u32[]{:S(2)}, u32[]{:S(2)}) %collective-permute-start.43) | collective-permute-done | bytes 640032 | tf_op jit(solution)/shard_map/ppermute | solution.py:422
  341.3 6.4 %collective-permute-done.50 = bf16[416,768]{1,0:T(8,128)(2,1)} collective-permute-done((bf16[416,768]{1,0:T(8,128)(2,1)}, bf16[416,768]{1,0:T(8,128)(2,1)}, u32[]{:S(2)}, u32[]{:S(2)}) %collective-permute-start.50) | collective-permute-done | bytes 639008 | tf_op jit(solution)/shard_map/ppermute | solution.py:422
  349.2 4.9 collective-permute-done.47
  358.9 10.6 %collective-permute-done.46 = bf16[1,400,800]{2,1,0:T(8,128)(2,1)} collective-permute-done((bf16[1,400,800]{2,1,0:T(8,128)(2,1)}, bf16[1,400,800]{2,1,0:T(8,128)(2,1)}, u32[]{:S(2)}, u32[]{:S(2)}) %collective-permute-start.46) | collective-permute-done | bytes 640032 | tf_op jit(solution)/shard_map/ppermute | solution.py:422
  371.2 4.9 collective-permute-done.51
  386.9 38.3 %collective-permute-done.56 = bf16[1,416,768]{2,1,0:T(8,128)(2,1)S(1)} collective-permute-done((bf16[1,416,768]{2,1,0:T(8,128)(2,1)S(1)}, bf16[1,416,768]{2,1,0:T(8,128)(2,1)S(1)}, u32[]{:S(2)}, u32[]{:S(2)}) %collective-permute-start.56) | collective-permute-done | bytes 639008 | tf_op jit(solution)/shard_map/ppermute | solution.py:422
  433.3 26.2 %collective-permute-done.60.refs_2_ = bf16[2,400,800]{2,1,0:T(8,128)(2,1)S(1)} collective-permute-done((bf16[2,400,800]{2,1,0:T(8,128)(2,1)S(1)}, bf16[2,400,800]{2,1,0:T(8,128)(2,1)S(1)}, u32[]{:S(2)}, u32[]{:S(2)}) %collective-permute-start.60) | collective-permute-done | bytes 1280032 | tf_op jit(solution)/shard_map/ppermute | solution.py:422
  464.3 16.7 %collective-permute-done.61.refs_1_ = bf16[2,416,768]{2,1,0:T(8,128)(2,1)} collective-permute-done((bf16[2,416,768]{2,1,0:T(8,128)(2,1)S(1)}, bf16[2,416,768]{2,1,0:T(8,128)(2,1)}, u32[]{:S(2)}, u32[]{:S(2)}) %collective-permute-start.61) | collective-permute-done | bytes 1277984 | tf_op jit(solution)/shard_map/ppermute | solution.py:422
  499.3 9.9 %collective-permute-done.64 = bf16[128,1600]{0,1:T(8,128)(2,1)S(1)} collective-permute-done((bf16[128,1600]{0,1:T(8,128)(2,1)}, bf16[128,1600]{0,1:T(8,128)(2,1)S(1)}, u32[]{:S(2)}, u32[]{:S(2)}) %collective-permute-start.64) | collective-permute-done | bytes 409632 | tf_op jit(solution)/shard_map/ppermute | solution.py:422
  511.9 7.4 %shard_map.250 = f32[1600,1600]{1,0:T(8,128)} custom-call(s32[8]{0:T(128)S(1)} %stack.245.numbers, bf16[2,200,1600]{2,1,0:T(8,128)(2,1)} %pad_maximum_fusion.10.refs_0_, bf16[2,200,1600]{2,1,0:T(8,128)(2,1)} %collective-permute-done.49.refs_1_, bf16[2,200,1600]{2,1,0:T(8,128)(2,1)} %collective-permute-done.70.refs_2_, bf16[2,200,1600]{2,1,0:T(8,128)(2,1)S(1)} %copy-done.10), custom_call_target="tpu_custom_call" | custom-call | bytes 15360000 | tf_op jit(solution)/shard_map/pallas_call | solution.py:238
  519.3 15.7 %collective-permute-done.66 = bf16[1,128,1600]{1,2,0:T(8,128)(2,1)S(1)} collective-permute-done((bf16[1,128,1600]{1,2,0:T(8,128)(2,1)S(1)}, bf16[1,128,1600]{1,2,0:T(8,128)(2,1)S(1)}, u32[]{:S(2)}, u32[]{:S(2)}) %collective-permute-start.66) | collective-permute-done | bytes 409632 | tf_op jit(solution)/shard_map/ppermute | solution.py:422
  538.9 6.3 %shard_map.249 = f32[400,6400]{1,0:T(8,128)} custom-call(s32[8]{0:T(128)S(1)} %stack.245.numbers, bf16[2,400,800]{2,1,0:T(8,128)(2,1)S(1)} %pad_maximum_fusion.8.refs_0_, bf16[2,400,800]{2,1,0:T(8,128)(2,1)S(1)} %copy-done.6, bf16[2,400,800]{2,1,0:T(8,128)(2,1)S(1)} %copy-done.8, bf16[2,400,800]{2,1,0:T(8,128)(2,1)S(1)} %collective-permute-done.69.refs_3_), custom_call_target="tpu_custom_call" | custom-call | bytes 15360000 | tf_op jit(solution)/shard_map/pallas_call | solution.py:238
  545.2 6.0 %shard_map.247 = (f32[400,4800]{1,0:T(8,128)}, f32[16,768]{1,0:T(8,128)S(1)}) custom-call(s32[8]{0:T(128)S(1)} %stack.244.numbers, bf16[2,416,768]{2,1,0:T(8,128)(2,1)S(1)} %pad_maximum_fusion.12.refs_0_, bf16[2,416,768]{2,1,0:T(8,128)(2,1)} %collective-permute-done.61.refs_1_, bf16[2,416,768]{2,1,0:T(8,128)(2,1)} %collective-permute-done.63.refs_2_, ...), custom_call_target="tpu_custom_call" | custom-call | bytes 12840960 | tf_op jit(solution)/shard_map/pallas_call | solution.py:238
  (448 shorter events, 239.1 us)
Async XLA Ops:
  16.5 45.6 %collective-permute-start.13 = (bf16[400,1600]{1,0:T(8,128)(2,1)}, bf16[400,1600]{1,0:T(8,128)(2,1)}, u32[]{:S(2)}, u32[]{:S(2)}) collective-permute-start(bf16[400,1600]{1,0:T(8,128)(2,1)} %param.21), channel_id=1, source_target_pairs={{0,2},{1,3},{2,0},{3,1},{4,6},{5,7},{6,4},{7,5},{8,10},{9,11},{10,... | collective-permute-start | bytes 3840008 | tf_op jit(solution)/shard_map/ppermute | solution.py:422
  26.5 30.9 %collective-permute-start.5 = (bf16[256,1600]{0,1:T(8,128)(2,1)}, bf16[256,1600]{0,1:T(8,128)(2,1)}, u32[]{:S(2)}, u32[]{:S(2)}) collective-permute-start(bf16[256,1600]{0,1:T(8,128)(2,1)} %pad_maximum_fusion.13), channel_id=1, source_target_pairs={{0,4},{1,5},{2,6},{3,7},{4,0},{5,1},{6,2},{7,3},{8,12},{9,13},{10,... | collective-permute-start | bytes 2457608 | tf_op jit(solution)/shard_map/ppermute | solution.py:422
  65.6 34.5 %collective-permute-start.15 = (bf16[2,400,800]{2,1,0:T(8,128)(2,1)}, bf16[2,400,800]{2,1,0:T(8,128)(2,1)}, u32[]{:S(2)}, u32[]{:S(2)}) collective-permute-start(bf16[2,400,800]{2,1,0:T(8,128)(2,1)} %get-tuple-element.124), channel_id=1, source_target_pairs={{0,2},{1,3},{2,0},{3,1},{4,6},{5,7},{6,4},{7,5},{8,10},{9,11},{10,... | collective-permute-start | bytes 3840008 | tf_op jit(solution)/shard_map/ppermute | solution.py:422
  90.1 31.5 %collective-permute-start.25 = (bf16[128,1600]{0,1:T(8,128)(2,1)}, bf16[128,1600]{0,1:T(8,128)(2,1)}, u32[]{:S(2)}, u32[]{:S(2)}) collective-permute-start(bf16[128,1600]{0,1:T(8,128)(2,1)} %bitcast.164), channel_id=1, source_target_pairs={{0,8},{1,9},{2,10},{3,11},{4,12},{5,13},{6,14},{7,15},{8,0},{9,1},... | collective-permute-start | bytes 1228808 | tf_op jit(solution)/shard_map/ppermute | solution.py:422
  92.1 31.9 %collective-permute-start.26 = (bf16[128,1600]{0,1:T(8,128)(2,1)}, bf16[128,1600]{0,1:T(8,128)(2,1)}, u32[]{:S(2)}, u32[]{:S(2)}) collective-permute-start(bf16[128,1600]{0,1:T(8,128)(2,1)} %bitcast.165), channel_id=1, source_target_pairs={{0,10},{1,11},{2,8},{3,9},{4,14},{5,15},{6,12},{7,13},{8,2},{9,3},... | collective-permute-start | bytes 1228808 | tf_op jit(solution)/shard_map/ppermute | solution.py:422
  161.9 31.8 %collective-permute-start.34 = (bf16[2,200,1600]{2,1,0:T(8,128)(2,1)}, bf16[2,200,1600]{2,1,0:T(8,128)(2,1)}, u32[]{:S(2)}, u32[]{:S(2)}) collective-permute-start(bf16[2,200,1600]{2,1,0:T(8,128)(2,1)} %pad_maximum_fusion.9), channel_id=1, source_target_pairs={{0,4},{1,5},{2,6},{3,7},{4,0},{5,1},{6,2},{7,3},{8,12},{9,13},{10,... | collective-permute-start | bytes 3840008 | tf_op jit(solution)/shard_map/ppermute | solution.py:422
  179.5 48.7 %collective-permute-start.32 = (bf16[2,400,800]{2,1,0:T(8,128)(2,1)}, bf16[2,400,800]{2,1,0:T(8,128)(2,1)}, u32[]{:S(2)}, u32[]{:S(2)}) collective-permute-start(bf16[2,400,800]{2,1,0:T(8,128)(2,1)} %pad_maximum_fusion.5), channel_id=1, source_target_pairs={{0,2},{1,3},{2,0},{3,1},{4,6},{5,7},{6,4},{7,5},{8,10},{9,11},{10,... | collective-permute-start | bytes 3840008 | tf_op jit(solution)/shard_map/ppermute | solution.py:422
  196.3 38.6 %collective-permute-start.38 = (bf16[1,200,1600]{2,1,0:T(8,128)(2,1)}, bf16[1,200,1600]{2,1,0:T(8,128)(2,1)}, u32[]{:S(2)}, u32[]{:S(2)}) collective-permute-start(bf16[1,200,1600]{2,1,0:T(8,128)(2,1)} %slice.302), channel_id=1, source_target_pairs={{0,16},{1,17},{2,18},{3,19},{4,20},{5,21},{6,22},{7,23},{8,24},{9,... | collective-permute-start | bytes 1920008 | tf_op jit(solution)/shard_map/ppermute | solution.py:422
  210.6 38.1 %all-to-all-start.1 = ((bf16[8,128,256]{2,1,0:T(8,128)(2,1)}), bf16[8,128,256]{2,1,0:T(8,128)(2,1)S(1)}, u32[]{:S(2)}, u32[]{:S(2)}) async-start(bf16[8,128,256]{2,1,0:T(8,128)(2,1)} %shard_map.245), calls=%async_computation.1 | async-start | bytes 1048576 | tf_op jit(solution)/shard_map/all_to_all | solution.py:531
  237.0 42.6 %collective-permute-start.40 = (bf16[1,200,1600]{2,1,0:T(8,128)(2,1)}, bf16[1,200,1600]{2,1,0:T(8,128)(2,1)}, u32[]{:S(2)}, u32[]{:S(2)}) collective-permute-start(bf16[1,200,1600]{2,1,0:T(8,128)(2,1)} %add_convert_fusion.10), channel_id=1, source_target_pairs={{0,16},{1,17},{2,18},{3,19},{4,20},{5,21},{6,22},{7,23},{8,24},{9,... | collective-permute-start | bytes 1920008 | tf_op jit(solution)/shard_map/ppermute | solution.py:422
  242.6 46.0 %collective-permute-start.39 = (bf16[2,400,800]{2,1,0:T(8,128)(2,1)}, bf16[2,400,800]{2,1,0:T(8,128)(2,1)}, u32[]{:S(2)}, u32[]{:S(2)}) collective-permute-start(bf16[2,400,800]{2,1,0:T(8,128)(2,1)} %pad_maximum_fusion.7), channel_id=1, source_target_pairs={{0,4},{1,5},{2,6},{3,7},{4,0},{5,1},{6,2},{7,3},{8,12},{9,13},{10,... | collective-permute-start | bytes 3840008 | tf_op jit(solution)/shard_map/ppermute | solution.py:422
  247.2 43.8 %collective-permute-start.44 = (bf16[400,1600]{1,0:T(8,128)(2,1)}, bf16[400,1600]{1,0:T(8,128)(2,1)}, u32[]{:S(2)}, u32[]{:S(2)}) collective-permute-start(bf16[400,1600]{1,0:T(8,128)(2,1)} %fusion.18), channel_id=1, source_target_pairs={{0,2},{1,3},{2,0},{3,1},{4,6},{5,7},{6,4},{7,5},{8,10},{9,11},{10,... | collective-permute-start | bytes 3840008 | tf_op jit(solution)/shard_map/ppermute | solution.py:422
  274.5 37.7 %collective-permute-start.45 = (bf16[512,1600]{0,1:T(8,128)(2,1)}, bf16[512,1600]{0,1:T(8,128)(2,1)}, u32[]{:S(2)}, u32[]{:S(2)}) collective-permute-start(bf16[512,1600]{0,1:T(8,128)(2,1)} %get-tuple-element.159), channel_id=1, source_target_pairs={{0,4},{1,5},{2,6},{3,7},{4,0},{5,1},{6,2},{7,3},{8,12},{9,13},{10,... | collective-permute-start | bytes 4915208 | tf_op jit(solution)/shard_map/ppermute | solution.py:422
  282.1 49.3 %collective-permute-start.49 = (bf16[2,200,1600]{2,1,0:T(8,128)(2,1)}, bf16[2,200,1600]{2,1,0:T(8,128)(2,1)}, u32[]{:S(2)}, u32[]{:S(2)}) collective-permute-start(bf16[2,200,1600]{2,1,0:T(8,128)(2,1)} %pad_maximum_fusion.10.refs_0_), channel_id=1, source_target_pairs={{0,8},{1,9},{2,10},{3,11},{4,12},{5,13},{6,14},{7,15},{8,0},{9,1},... | collective-permute-start | bytes 3840008 | tf_op jit(solution)/shard_map/ppermute | solution.py:422
  290.9 35.0 %collective-permute-start.43 = (bf16[1,400,800]{2,1,0:T(8,128)(2,1)S(1)}, bf16[1,400,800]{2,1,0:T(8,128)(2,1)S(1)}, u32[]{:S(2)}, u32[]{:S(2)}) collective-permute-start(bf16[1,400,800]{2,1,0:T(8,128)(2,1)S(1)} %slice.306), channel_id=1, source_target_pairs={{0,16},{1,17},{2,18},{3,19},{4,20},{5,21},{6,22},{7,23},{8,24},{9,... | collective-permute-start | bytes 1920008 | tf_op jit(solution)/shard_map/ppermute | solution.py:422
  291.0 40.4 %collective-permute-start.48 = (bf16[2,416,768]{2,1,0:T(8,128)(2,1)}, bf16[2,416,768]{2,1,0:T(8,128)(2,1)}, u32[]{:S(2)}, u32[]{:S(2)}) collective-permute-start(bf16[2,416,768]{2,1,0:T(8,128)(2,1)} %pad_maximum_fusion.11), channel_id=1, source_target_pairs={{0,1},{1,0},{2,3},{3,2},{4,5},{5,4},{6,7},{7,6},{8,9},{9,8},{10,11... | collective-permute-start | bytes 3833864 | tf_op jit(solution)/shard_map/ppermute | solution.py:422
  336.2 33.3 %collective-permute-start.46 = (bf16[1,400,800]{2,1,0:T(8,128)(2,1)}, bf16[1,400,800]{2,1,0:T(8,128)(2,1)}, u32[]{:S(2)}, u32[]{:S(2)}) collective-permute-start(bf16[1,400,800]{2,1,0:T(8,128)(2,1)} %add_convert_fusion.9), channel_id=1, source_target_pairs={{0,16},{1,17},{2,18},{3,19},{4,20},{5,21},{6,22},{7,23},{8,24},{9,... | collective-permute-start | bytes 1920008 | tf_op jit(solution)/shard_map/ppermute | solution.py:422
  340.8 35.3 %collective-permute-start.51 = (bf16[2,128,1600]{1,2,0:T(8,128)(2,1)}, bf16[2,128,1600]{1,2,0:T(8,128)(2,1)}, u32[]{:S(2)}, u32[]{:S(2)}) collective-permute-start(bf16[2,128,1600]{1,2,0:T(8,128)(2,1)} %copy.67), channel_id=1, source_target_pairs={{0,8},{1,9},{2,10},{3,11},{4,12},{5,13},{6,14},{7,15},{8,0},{9,1},... | collective-permute-start | bytes 2457608 | tf_op jit(solution)/shard_map/ppermute | solution.py:422
  340.8 39.0 %collective-permute-start.52 = (bf16[2,200,1600]{2,1,0:T(8,128)(2,1)}, bf16[2,200,1600]{2,1,0:T(8,128)(2,1)S(1)}, u32[]{:S(2)}, u32[]{:S(2)}) collective-permute-start(bf16[2,200,1600]{2,1,0:T(8,128)(2,1)} %collective-permute-done.49.refs_1_), channel_id=1, source_target_pairs={{0,4},{1,5},{2,6},{3,7},{4,0},{5,1},{6,2},{7,3},{8,12},{9,13},{10,... | collective-permute-start | bytes 3840008 | tf_op jit(solution)/shard_map/ppermute | solution.py:422
  371.2 58.5 %collective-permute-start.57 = (bf16[2,400,800]{2,1,0:T(8,128)(2,1)S(1)}, bf16[2,400,800]{2,1,0:T(8,128)(2,1)S(1)}, u32[]{:S(2)}, u32[]{:S(2)}) collective-permute-start(bf16[2,400,800]{2,1,0:T(8,128)(2,1)S(1)} %pad_maximum_fusion.8.refs_0_), channel_id=1, source_target_pairs={{0,8},{1,9},{2,10},{3,11},{4,12},{5,13},{6,14},{7,15},{8,0},{9,1},... | collective-permute-start | bytes 3840008 | tf_op jit(solution)/shard_map/ppermute | solution.py:422
  379.9 50.3 %collective-permute-start.53 = (bf16[512,1600]{0,1:T(8,128)(2,1)S(1)}, bf16[512,1600]{0,1:T(8,128)(2,1)S(1)}, u32[]{:S(2)}, u32[]{:S(2)}) collective-permute-start(bf16[512,1600]{0,1:T(8,128)(2,1)S(1)} %convolution_convert_fusion.5), channel_id=1, source_target_pairs={{0,1},{1,0},{2,3},{3,2},{4,5},{5,4},{6,7},{7,6},{8,9},{9,8},{10,11... | collective-permute-start | bytes 4915208 | tf_op jit(solution)/shard_map/ppermute | solution.py:422
  380.0 110.6 %collective-permute-start.70 = (bf16[2,200,1600]{2,1,0:T(8,128)(2,1)}, bf16[2,200,1600]{2,1,0:T(8,128)(2,1)}, u32[]{:S(2)}, u32[]{:S(2)}) collective-permute-start(bf16[2,200,1600]{2,1,0:T(8,128)(2,1)} %pad_maximum_fusion.10.refs_0_), channel_id=1, source_target_pairs={{0,4},{1,5},{2,6},{3,7},{4,0},{5,1},{6,2},{7,3},{8,12},{9,13},{10,... | collective-permute-start | bytes 3840008 | tf_op jit(solution)/shard_map/ppermute | solution.py:422
  381.3 43.9 %collective-permute-start.56 = (bf16[1,416,768]{2,1,0:T(8,128)(2,1)S(1)}, bf16[1,416,768]{2,1,0:T(8,128)(2,1)S(1)}, u32[]{:S(2)}, u32[]{:S(2)}) collective-permute-start(bf16[1,416,768]{2,1,0:T(8,128)(2,1)S(1)} %fusion.48), channel_id=1, source_target_pairs={{0,16},{1,17},{2,18},{3,19},{4,20},{5,21},{6,22},{7,23},{8,24},{9,... | collective-permute-start | bytes 1916936 | tf_op jit(solution)/shard_map/ppermute | solution.py:422
  384.8 44.8 %collective-permute-start.55 = (bf16[1,56,1600]{2,1,0:T(8,128)(2,1)S(1)}, bf16[1,56,1600]{2,1,0:T(8,128)(2,1)S(1)}, u32[]{:S(2)}, u32[]{:S(2)}) collective-permute-start(bf16[1,56,1600]{2,1,0:T(8,128)(2,1)S(1)} %slice.316), channel_id=1, source_target_pairs={{0,16},{1,17},{2,18},{3,19},{4,20},{5,21},{6,22},{7,23},{8,24},{9,... | collective-permute-start | bytes 537608 | tf_op jit(solution)/shard_map/ppermute | solution.py:422
  425.2 34.3 %collective-permute-start.60 = (bf16[2,400,800]{2,1,0:T(8,128)(2,1)S(1)}, bf16[2,400,800]{2,1,0:T(8,128)(2,1)S(1)}, u32[]{:S(2)}, u32[]{:S(2)}) collective-permute-start(bf16[2,400,800]{2,1,0:T(8,128)(2,1)S(1)} %pad_maximum_fusion.8.refs_0_), channel_id=1, source_target_pairs={{0,4},{1,5},{2,6},{3,7},{4,0},{5,1},{6,2},{7,3},{8,12},{9,13},{10,... | collective-permute-start | bytes 3840008 | tf_op jit(solution)/shard_map/ppermute | solution.py:422
  429.6 51.4 %collective-permute-start.61 = (bf16[2,416,768]{2,1,0:T(8,128)(2,1)S(1)}, bf16[2,416,768]{2,1,0:T(8,128)(2,1)}, u32[]{:S(2)}, u32[]{:S(2)}) collective-permute-start(bf16[2,416,768]{2,1,0:T(8,128)(2,1)S(1)} %pad_maximum_fusion.12.refs_0_), channel_id=1, source_target_pairs={{0,4},{1,5},{2,6},{3,7},{4,0},{5,1},{6,2},{7,3},{8,12},{9,13},{10,... | collective-permute-start | bytes 3833864 | tf_op jit(solution)/shard_map/ppermute | solution.py:422
  429.6 62.6 %collective-permute-start.63 = (bf16[2,416,768]{2,1,0:T(8,128)(2,1)S(1)}, bf16[2,416,768]{2,1,0:T(8,128)(2,1)}, u32[]{:S(2)}, u32[]{:S(2)}) collective-permute-start(bf16[2,416,768]{2,1,0:T(8,128)(2,1)S(1)} %pad_maximum_fusion.12.refs_0_), channel_id=1, source_target_pairs={{0,8},{1,9},{2,10},{3,11},{4,12},{5,13},{6,14},{7,15},{8,0},{9,1},... | collective-permute-start | bytes 3833864 | tf_op jit(solution)/shard_map/ppermute | solution.py:422
  430.2 50.8 %collective-permute-start.59 = (bf16[1,56,1600]{2,1,0:T(8,128)(2,1)S(1)}, bf16[1,56,1600]{2,1,0:T(8,128)(2,1)S(1)}, u32[]{:S(2)}, u32[]{:S(2)}) collective-permute-start(bf16[1,56,1600]{2,1,0:T(8,128)(2,1)S(1)} %add_convert_fusion.16), channel_id=1, source_target_pairs={{0,16},{1,17},{2,18},{3,19},{4,20},{5,21},{6,22},{7,23},{8,24},{9,... | collective-permute-start | bytes 537608 | tf_op jit(solution)/shard_map/ppermute | solution.py:422
  460.6 31.9 %collective-permute-start.58 = (bf16[128,1600]{0,1:T(8,128)(2,1)}, bf16[128,1600]{0,1:T(8,128)(2,1)}, u32[]{:S(2)}, u32[]{:S(2)}) collective-permute-start(bf16[128,1600]{0,1:T(8,128)(2,1)} %get-tuple-element.194), channel_id=1, source_target_pairs={{0,10},{1,11},{2,8},{3,9},{4,14},{5,15},{6,12},{7,13},{8,2},{9,3},... | collective-permute-start | bytes 1228808 | tf_op jit(solution)/shard_map/ppermute | solution.py:422
  492.2 46.7 %collective-permute-start.69 = (bf16[2,400,800]{2,1,0:T(8,128)(2,1)}, bf16[2,400,800]{2,1,0:T(8,128)(2,1)S(1)}, u32[]{:S(2)}, u32[]{:S(2)}) collective-permute-start(bf16[2,400,800]{2,1,0:T(8,128)(2,1)} %copy-done.5), channel_id=1, source_target_pairs={{0,4},{1,5},{2,6},{3,7},{4,0},{5,1},{6,2},{7,3},{8,12},{9,13},{10,... | collective-permute-start | bytes 3840008 | tf_op jit(solution)/shard_map/ppermute | solution.py:422
  492.5 52.7 %collective-permute-start.67 = (bf16[2,416,768]{2,1,0:T(8,128)(2,1)}, bf16[2,416,768]{2,1,0:T(8,128)(2,1)S(1)}, u32[]{:S(2)}, u32[]{:S(2)}) collective-permute-start(bf16[2,416,768]{2,1,0:T(8,128)(2,1)} %collective-permute-done.61.refs_1_), channel_id=1, source_target_pairs={{0,8},{1,9},{2,10},{3,11},{4,12},{5,13},{6,14},{7,15},{8,0},{9,1},... | collective-permute-start | bytes 3833864 | tf_op jit(solution)/shard_map/ppermute | solution.py:422
  495.6 40.9 %collective-permute-start.68 = (bf16[4,56,1600]{2,1,0:T(8,128)(2,1)S(1)}, bf16[4,56,1600]{2,1,0:T(8,128)(2,1)S(1)}, u32[]{:S(2)}, u32[]{:S(2)}) collective-permute-start(bf16[4,56,1600]{2,1,0:T(8,128)(2,1)S(1)} %pad_maximum_fusion.15.refs_0_), channel_id=1, source_target_pairs={{0,4},{1,5},{2,6},{3,7},{4,0},{5,1},{6,2},{7,3},{8,12},{9,13},{10,... | collective-permute-start | bytes 2150408 | tf_op jit(solution)/shard_map/ppermute | solution.py:422
  (105 other events, 1505.3 us)

commit v5 on v4

--- a/solution.py
+++ b/solution.py
@@ -56,7 +56,7 @@
 UNROLLED = 1024
 BUMP = 1
 SPLIT = ("down", "up", "qkv")
-TURNS = "mdmudmpudupmgduqpugqdqpuopqpopuqpg"
+TURNS = "mdmudmpudupmgduqpugqdqpuopqpgupoqp"
 
 
 def for_tiles(one, length, tile, key_axis):

time: 560 us -> 539 us (0.963)
  waiting for transfers between devices: 238 us -> 223 us
    ppermute x71, waiting for transfers between devices: 234 us -> 220 us  [swap(): return lax.ppermute(value, AXES, pairs)]
    unnamed x153 -> x151, local copies, waits for them, and re-layouts: 23.6 us -> 21.1 us
  transfers between devices with their start and end apart: 73 -> 73, of which waited for: 27 -> 31; matrix products, arithmetic and copies ran while one was open for 27% -> 28% of each run, Pallas kernels for 9% -> 9%
where the time goes in v5:
time: 539 us; the launch traced here: 532 us
  waiting for transfers between devices  223 us (41%)
  starting transfers between devices  72.9 us (14%)
  matrix products  64.9 us (12%)
  other arithmetic  61.7 us (11%)
  local copies, waits for them, and re-layouts  53.6 us (10%)
  Pallas kernels  53.6 us (10%)
    ppermute x71, waiting for transfers between devices, swap(): return lax.ppermute(value, AXES, pairs)  220 us
    ppermute x71, starting transfers between devices, swap(): return lax.ppermute(value, AXES, pairs)  63.7 us
    pallas_call x9, Pallas kernels, rearrange(): pl.pallas_call(kernel, out_shape=tuple((jax.ShapeDtypeStruct(o.shape, o.d...  32.3 us
    dot_general x6, matrix products, by_transpose(): lax.dot_general(left, right, (((1,), (1,)), ((), ())), preferred_element_...  28 us
    convert_element_type x14, other arithmetic, add_low(): return (left.astype(F32) + right.astype(F32)).astype(BF16)  21.9 us
    dot_general x7, matrix products, dot(): return jnp.dot(left, right, preferred_element_type=F32)  21.3 us
    unnamed x151, local copies, waits for them, and re-layouts  21.1 us
    dot_general x4, matrix products, over_rows(): lax.dot_general(left, right, (((0,), (0,)), ((), ())), preferred_element_...  15.6 us
  transfers between devices with their start and end apart: 73, of which 31 were waited for; matrix products, arithmetic and copies ran while one was open for 28% of the time, Pallas kernels for 9%

profile of v5, /device:TPU:0, one launch (start us, length us, event | category | flops | bytes accessed | tf_op | source)
XLA Modules:
  0.0 531.9 jit_solution(9598378998371190991)
XLA Ops:
  17.1 7.6 %collective-permute-done = bf16[128,1600]{0,1:T(8,128)(2,1)S(1)} collective-permute-done((bf16[128,1600]{0,1:T(8,128)(2,1)}, bf16[128,1600]{0,1:T(8,128)(2,1)S(1)}, u32[]{:S(2)}, u32[]{:S(2)}) %collective-permute-start) | collective-permute-done | bytes 409632 | tf_op jit(solution)/shard_map/ppermute | solution.py:422
  28.5 6.6 %collective-permute-done.1 = bf16[128,1600]{0,1:T(8,128)(2,1)} collective-permute-done((bf16[128,1600]{0,1:T(8,128)(2,1)S(1)}, bf16[128,1600]{0,1:T(8,128)(2,1)}, u32[]{:S(2)}, u32[]{:S(2)}) %collective-permute-start.1) | collective-permute-done | bytes 409632 | tf_op jit(solution)/shard_map/ppermute | solution.py:422
  35.8 4.6 shard_map.242
  44.0 12.2 %collective-permute-done.3 = bf16[128,1600]{0,1:T(8,128)(2,1)} collective-permute-done((bf16[128,1600]{0,1:T(8,128)(2,1)}, bf16[128,1600]{0,1:T(8,128)(2,1)}, u32[]{:S(2)}, u32[]{:S(2)}) %collective-permute-start.3) | collective-permute-done | bytes 409632 | tf_op jit(solution)/shard_map/ppermute | solution.py:422
  68.6 5.6 %add_convert_fusion.3.qkv_ref = bf16[1024,768]{1,0:T(8,128)(2,1)S(1)} fusion(bf16[1600,768]{1,0:T(8,128)(2,1)S(1)} %shard_map.239, f32[768]{0:T(1024)S(1)} %pad_maximum_fusion.17, bf16[1024,1600]{0,1:T(8,128)(2,1)} %copy-done.15, f32[1600]{0:T(1024)S(1)} %add.349, f32[1600]{0:T(1024)S(1)} %mul.277, f32[1024]{0:T(1024)S(1)} %add_rsqrt_fusion.1, ...), kind=kOutput, calls=%fused_computation.37 | convolution fusion | flops 2527985664 | bytes 7331328 | tf_op jit(solution)/shard_map/dot_general | solution.py:41
  74.2 6.8 %shard_map.240 = (bf16[8,128,256]{2,1,0:T(8,128)(2,1)S(1)}, f32[1024,128]{1,0:T(8,128)S(1)}) custom-call(s32[16]{0:T(128)S(1)} %select_reduce_fusion.place_ref, s32[16]{0:T(128)S(1)} %copy-done.10, bf16[1024,768]{1,0:T(8,128)(2,1)S(1)} %add_convert_fusion.3.qkv_ref), custom_call_target="tpu_custom_call" | custom-call | flops 1073741824 | bytes 2621440 | tf_op jit(solution)/shard_map/pallas_call | solution.py:200
  82.6 4.5 all-to-all-start
  92.5 5.3 %shard_map.241 = bf16[1600,1600]{1,0:T(8,128)(2,1)} custom-call(s32[4]{0:T(128)S(1)} %pad_add_fusion.numbers, bf16[2,400,1600]{2,1,0:T(8,128)(2,1)} %pad_maximum_fusion.1.refs_0_, bf16[2,400,1600]{2,1,0:T(8,128)(2,1)} %collective-permute-done.14.refs_1_), custom_call_target="tpu_custom_call" | custom-call | bytes 10240000 | tf_op jit(solution)/shard_map/pallas_call | solution.py:238
  104.5 5.0 fusion.85
  111.2 6.5 %collective-permute-done.24 = bf16[128,1600]{0,1:T(8,128)(2,1)} collective-permute-done((bf16[128,1600]{0,1:T(8,128)(2,1)}, bf16[128,1600]{0,1:T(8,128)(2,1)}, u32[]{:S(2)}, u32[]{:S(2)}) %collective-permute-start.24) | collective-permute-done | bytes 409632 | tf_op jit(solution)/shard_map/ppermute | solution.py:422
  126.0 8.8 %collective-permute-done.16 = bf16[128,1600]{0,1:T(8,128)(2,1)S(1)} collective-permute-done((bf16[128,1600]{0,1:T(8,128)(2,1)S(1)}, bf16[128,1600]{0,1:T(8,128)(2,1)S(1)}, u32[]{:S(2)}, u32[]{:S(2)}) %collective-permute-start.16) | collective-permute-done | bytes 409632 | tf_op jit(solution)/shard_map/ppermute | solution.py:422
  147.5 7.6 %convert_reduce_fusion.2 = (bf16[800]{0:T(1024)(128)(2,1)S(1)}, bf16[1024,800]{0,1:T(8,128)(2,1)S(1)}) fusion(bf16[1024,1600]{0,1:T(8,128)(2,1)S(1)} %copy-done.52, bf16[1600,1600]{1,0:T(8,128)(2,1)} %param.25, s32[]{:T(128)S(6)} %select_n.120, f32[1024,800]{0,1:T(8,128)S(1)} %get-tuple-element.293, f32[800]{0:T(1024)S(1)} %fusion.70), kind=kOutput, calls=%fused_computation.33 | convolution fusion | flops 2643557632 | bytes 10859204 | tf_op jit(solution)/shard_map/dot_general | solution.py:49
  165.0 6.0 %convolution_convert_fusion.1 = bf16[1600,800]{1,0:T(8,128)(2,1)S(1)} fusion(bf16[1024,1600]{0,1:T(8,128)(2,1)} %copy-done.50, bf16[1024,800]{0,1:T(8,128)(2,1)} %copy-done.57), kind=kOutput, calls=%fused_computation.18 | convolution fusion | flops 2622720000 | bytes 7475200 | tf_op jit(solution)/shard_map/dot_general | solution.py:45
  183.5 12.5 %collective-permute-done.34 = bf16[2,200,1600]{2,1,0:T(8,128)(2,1)} collective-permute-done((bf16[2,200,1600]{2,1,0:T(8,128)(2,1)}, bf16[2,200,1600]{2,1,0:T(8,128)(2,1)}, u32[]{:S(2)}, u32[]{:S(2)}) %collective-permute-start.34) | collective-permute-done | bytes 1280032 | tf_op jit(solution)/shard_map/ppermute | solution.py:422
  212.8 4.6 all-to-all-start.1
  225.3 5.2 collective-permute-done.32
  253.1 10.7 %shard_map.246 = bf16[1024,768]{1,0:T(8,128)(2,1)S(1)} custom-call(s32[16]{0:T(128)S(1)} %select_reduce_fusion.place_ref, s32[16]{0:T(128)S(1)} %copy-done.10, bf16[1024,768]{1,0:T(8,128)(2,1)S(1)} %copy-done.12, f32[1024,128]{1,0:T(8,128)S(1)} %copy-done.14, bf16[8,128,256]{2,1,0:T(8,128)(2,1)S(1)} %all-to-all-done.1.grad_ref), custom_call_target="tpu_custom_call" | custom-call | flops 2684354560 | bytes 4194304 | tf_op jit(solution)/shard_map/pallas_call | solution.py:220
  267.4 9.3 %fusion.16 = (bf16[1600]{0:T(1024)(128)(2,1)S(1)}, bf16[512,1600]{0,1:T(8,128)(2,1)}, f32[512,1600]{0,1:T(8,128)}) fusion(f32[1024,1600]{0,1:T(8,128)} %fusion.2, f32[512,1600]{0,1:T(8,128)} %fusion.46, bf16[1600,768]{1,0:T(8,128)(2,1)S(1)} %shard_map.239, bf16[1024,768]{1,0:T(8,128)(2,1)} %copy-done.1), kind=kOutput, calls=%fused_computation.29 | convolution fusion | flops 1262385664 | bytes 17992832 | tf_op jit(solution)/shard_map/dot_general | solution.py:49
  299.3 16.4 %collective-permute-done.45 = bf16[512,1600]{0,1:T(8,128)(2,1)} collective-permute-done((bf16[512,1600]{0,1:T(8,128)(2,1)}, bf16[512,1600]{0,1:T(8,128)(2,1)}, u32[]{:S(2)}, u32[]{:S(2)}) %collective-permute-start.45) | collective-permute-done | bytes 1638432 | tf_op jit(solution)/shard_map/ppermute | solution.py:422
  315.7 12.4 %collective-permute-done.43 = bf16[1,400,800]{2,1,0:T(8,128)(2,1)S(1)} collective-permute-done((bf16[1,400,800]{2,1,0:T(8,128)(2,1)S(1)}, bf16[1,400,800]{2,1,0:T(8,128)(2,1)S(1)}, u32[]{:S(2)}, u32[]{:S(2)}) %collective-permute-start.43) | collective-permute-done | bytes 640032 | tf_op jit(solution)/shard_map/ppermute | solution.py:422
  355.3 4.9 collective-permute-done.47
  362.3 12.8 %collective-permute-done.46 = bf16[1,400,800]{2,1,0:T(8,128)(2,1)} collective-permute-done((bf16[1,400,800]{2,1,0:T(8,128)(2,1)}, bf16[1,400,800]{2,1,0:T(8,128)(2,1)}, u32[]{:S(2)}, u32[]{:S(2)}) %collective-permute-start.46) | collective-permute-done | bytes 640032 | tf_op jit(solution)/shard_map/ppermute | solution.py:422
  376.6 5.8 %collective-permute-done.51 = bf16[2,128,1600]{1,2,0:T(8,128)(2,1)} collective-permute-done((bf16[2,128,1600]{1,2,0:T(8,128)(2,1)}, bf16[2,128,1600]{1,2,0:T(8,128)(2,1)}, u32[]{:S(2)}, u32[]{:S(2)}) %collective-permute-start.51) | collective-permute-done | bytes 819232 | tf_op jit(solution)/shard_map/ppermute | solution.py:422
  388.6 13.4 %collective-permute-done.54 = bf16[2,56,1600]{2,1,0:T(8,128)(2,1)S(1)} collective-permute-done((bf16[2,56,1600]{2,1,0:T(8,128)(2,1)S(1)}, bf16[2,56,1600]{2,1,0:T(8,128)(2,1)S(1)}, u32[]{:S(2)}, u32[]{:S(2)}) %collective-permute-start.54) | collective-permute-done | bytes 358432 | tf_op jit(solution)/shard_map/ppermute | solution.py:422
  405.0 27.0 %collective-permute-done.57.refs_1_ = bf16[2,400,800]{2,1,0:T(8,128)(2,1)S(1)} collective-permute-done((bf16[2,400,800]{2,1,0:T(8,128)(2,1)S(1)}, bf16[2,400,800]{2,1,0:T(8,128)(2,1)S(1)}, u32[]{:S(2)}, u32[]{:S(2)}) %collective-permute-start.57) | collective-permute-done | bytes 1280032 | tf_op jit(solution)/shard_map/ppermute | solution.py:422
  437.2 27.4 %collective-permute-done.58 = bf16[1,56,1600]{2,1,0:T(8,128)(2,1)S(1)} collective-permute-done((bf16[1,56,1600]{2,1,0:T(8,128)(2,1)S(1)}, bf16[1,56,1600]{2,1,0:T(8,128)(2,1)S(1)}, u32[]{:S(2)}, u32[]{:S(2)}) %collective-permute-start.58) | collective-permute-done | bytes 179232 | tf_op jit(solution)/shard_map/ppermute | solution.py:422
  483.7 5.9 %collective-permute-done.67 = bf16[128,1600]{0,1:T(8,128)(2,1)S(1)} collective-permute-done((bf16[128,1600]{0,1:T(8,128)(2,1)S(1)}, bf16[128,1600]{0,1:T(8,128)(2,1)S(1)}, u32[]{:S(2)}, u32[]{:S(2)}) %collective-permute-start.67) | collective-permute-done | bytes 409632 | tf_op jit(solution)/shard_map/ppermute | solution.py:422
  489.7 9.7 %collective-permute-done.66 = bf16[128,1600]{0,1:T(8,128)(2,1)S(1)} collective-permute-done((bf16[128,1600]{0,1:T(8,128)(2,1)S(1)}, bf16[128,1600]{0,1:T(8,128)(2,1)S(1)}, u32[]{:S(2)}, u32[]{:S(2)}) %collective-permute-start.66) | collective-permute-done | bytes 409632 | tf_op jit(solution)/shard_map/ppermute | solution.py:422
  500.1 6.3 %shard_map.249 = f32[400,6400]{1,0:T(8,128)} custom-call(s32[8]{0:T(128)S(1)} %stack.245.numbers, bf16[2,400,800]{2,1,0:T(8,128)(2,1)S(1)} %pad_maximum_fusion.8.refs_0_, bf16[2,400,800]{2,1,0:T(8,128)(2,1)S(1)} %collective-permute-done.57.refs_1_, bf16[2,400,800]{2,1,0:T(8,128)(2,1)S(1)} %collective-permute-done.59.refs_2_, ...), custom_call_target="tpu_custom_call" | custom-call | bytes 15360000 | tf_op jit(solution)/shard_map/pallas_call | solution.py:238
  506.4 7.1 %shard_map.250 = f32[1600,1600]{1,0:T(8,128)} custom-call(s32[8]{0:T(128)S(1)} %stack.245.numbers, bf16[2,200,1600]{2,1,0:T(8,128)(2,1)} %pad_maximum_fusion.10.refs_0_, bf16[2,200,1600]{2,1,0:T(8,128)(2,1)} %collective-permute-done.49.refs_1_, bf16[2,200,1600]{2,1,0:T(8,128)(2,1)S(1)} %copy-done.6, bf16[2,200,1600]{2,1,0:T(8,128)(2,1)S(1)} %collective-permute-done.52.refs_3_), custom_call_target="tpu_custom_call" | custom-call | bytes 15360000 | tf_op jit(solution)/shard_map/pallas_call | solution.py:238
  517.9 7.0 %collective-permute-done.68.refs_3_ = bf16[2,416,768]{2,1,0:T(8,128)(2,1)S(1)} collective-permute-done((bf16[2,416,768]{2,1,0:T(8,128)(2,1)S(1)}, bf16[2,416,768]{2,1,0:T(8,128)(2,1)S(1)}, u32[]{:S(2)}, u32[]{:S(2)}) %collective-permute-start.68) | collective-permute-done | bytes 1277984 | tf_op jit(solution)/shard_map/ppermute | solution.py:422
  525.0 4.8 shard_map.247
  (445 shorter events, 239.1 us)
Async XLA Ops:
  16.5 45.7 %collective-permute-start.13 = (bf16[400,1600]{1,0:T(8,128)(2,1)}, bf16[400,1600]{1,0:T(8,128)(2,1)}, u32[]{:S(2)}, u32[]{:S(2)}) collective-permute-start(bf16[400,1600]{1,0:T(8,128)(2,1)} %param.21), channel_id=1, source_target_pairs={{0,2},{1,3},{2,0},{3,1},{4,6},{5,7},{6,4},{7,5},{8,10},{9,11},{10,... | collective-permute-start | bytes 3840008 | tf_op jit(solution)/shard_map/ppermute | solution.py:422
  65.6 34.5 %collective-permute-start.15 = (bf16[2,400,800]{2,1,0:T(8,128)(2,1)}, bf16[2,400,800]{2,1,0:T(8,128)(2,1)}, u32[]{:S(2)}, u32[]{:S(2)}) collective-permute-start(bf16[2,400,800]{2,1,0:T(8,128)(2,1)} %get-tuple-element.124), channel_id=1, source_target_pairs={{0,2},{1,3},{2,0},{3,1},{4,6},{5,7},{6,4},{7,5},{8,10},{9,11},{10,... | collective-permute-start | bytes 3840008 | tf_op jit(solution)/shard_map/ppermute | solution.py:422
  89.1 32.5 %collective-permute-start.25 = (bf16[128,1600]{0,1:T(8,128)(2,1)}, bf16[128,1600]{0,1:T(8,128)(2,1)}, u32[]{:S(2)}, u32[]{:S(2)}) collective-permute-start(bf16[128,1600]{0,1:T(8,128)(2,1)} %bitcast.164), channel_id=1, source_target_pairs={{0,8},{1,9},{2,10},{3,11},{4,12},{5,13},{6,14},{7,15},{8,0},{9,1},... | collective-permute-start | bytes 1228808 | tf_op jit(solution)/shard_map/ppermute | solution.py:422
  91.2 32.9 %collective-permute-start.26 = (bf16[128,1600]{0,1:T(8,128)(2,1)}, bf16[128,1600]{0,1:T(8,128)(2,1)}, u32[]{:S(2)}, u32[]{:S(2)}) collective-permute-start(bf16[128,1600]{0,1:T(8,128)(2,1)} %bitcast.165), channel_id=1, source_target_pairs={{0,10},{1,11},{2,8},{3,9},{4,14},{5,15},{6,12},{7,13},{8,2},{9,3},... | collective-permute-start | bytes 1228808 | tf_op jit(solution)/shard_map/ppermute | solution.py:422
  164.1 31.8 %collective-permute-start.34 = (bf16[2,200,1600]{2,1,0:T(8,128)(2,1)}, bf16[2,200,1600]{2,1,0:T(8,128)(2,1)}, u32[]{:S(2)}, u32[]{:S(2)}) collective-permute-start(bf16[2,200,1600]{2,1,0:T(8,128)(2,1)} %pad_maximum_fusion.9), channel_id=1, source_target_pairs={{0,4},{1,5},{2,6},{3,7},{4,0},{5,1},{6,2},{7,3},{8,12},{9,13},{10,... | collective-permute-start | bytes 3840008 | tf_op jit(solution)/shard_map/ppermute | solution.py:422
  182.0 48.5 %collective-permute-start.32 = (bf16[2,400,800]{2,1,0:T(8,128)(2,1)}, bf16[2,400,800]{2,1,0:T(8,128)(2,1)}, u32[]{:S(2)}, u32[]{:S(2)}) collective-permute-start(bf16[2,400,800]{2,1,0:T(8,128)(2,1)} %pad_maximum_fusion.5), channel_id=1, source_target_pairs={{0,2},{1,3},{2,0},{3,1},{4,6},{5,7},{6,4},{7,5},{8,10},{9,11},{10,... | collective-permute-start | bytes 3840008 | tf_op jit(solution)/shard_map/ppermute | solution.py:422
  198.6 38.5 %collective-permute-start.38 = (bf16[1,200,1600]{2,1,0:T(8,128)(2,1)}, bf16[1,200,1600]{2,1,0:T(8,128)(2,1)}, u32[]{:S(2)}, u32[]{:S(2)}) collective-permute-start(bf16[1,200,1600]{2,1,0:T(8,128)(2,1)} %slice.302), channel_id=1, source_target_pairs={{0,16},{1,17},{2,18},{3,19},{4,20},{5,21},{6,22},{7,23},{8,24},{9,... | collective-permute-start | bytes 1920008 | tf_op jit(solution)/shard_map/ppermute | solution.py:422
  212.8 37.8 %all-to-all-start.1 = ((bf16[8,128,256]{2,1,0:T(8,128)(2,1)}), bf16[8,128,256]{2,1,0:T(8,128)(2,1)S(1)}, u32[]{:S(2)}, u32[]{:S(2)}) async-start(bf16[8,128,256]{2,1,0:T(8,128)(2,1)} %shard_map.245), calls=%async_computation.1 | async-start | bytes 1048576 | tf_op jit(solution)/shard_map/all_to_all | solution.py:531
  239.2 42.5 %collective-permute-start.40 = (bf16[1,200,1600]{2,1,0:T(8,128)(2,1)}, bf16[1,200,1600]{2,1,0:T(8,128)(2,1)}, u32[]{:S(2)}, u32[]{:S(2)}) collective-permute-start(bf16[1,200,1600]{2,1,0:T(8,128)(2,1)} %add_convert_fusion.10), channel_id=1, source_target_pairs={{0,16},{1,17},{2,18},{3,19},{4,20},{5,21},{6,22},{7,23},{8,24},{9,... | collective-permute-start | bytes 1920008 | tf_op jit(solution)/shard_map/ppermute | solution.py:422
  244.6 47.0 %collective-permute-start.39 = (bf16[2,400,800]{2,1,0:T(8,128)(2,1)}, bf16[2,400,800]{2,1,0:T(8,128)(2,1)}, u32[]{:S(2)}, u32[]{:S(2)}) collective-permute-start(bf16[2,400,800]{2,1,0:T(8,128)(2,1)} %pad_maximum_fusion.7), channel_id=1, source_target_pairs={{0,4},{1,5},{2,6},{3,7},{4,0},{5,1},{6,2},{7,3},{8,12},{9,13},{10,... | collective-permute-start | bytes 3840008 | tf_op jit(solution)/shard_map/ppermute | solution.py:422
  249.2 45.2 %collective-permute-start.44 = (bf16[400,1600]{1,0:T(8,128)(2,1)}, bf16[400,1600]{1,0:T(8,128)(2,1)}, u32[]{:S(2)}, u32[]{:S(2)}) collective-permute-start(bf16[400,1600]{1,0:T(8,128)(2,1)} %fusion.18), channel_id=1, source_target_pairs={{0,2},{1,3},{2,0},{3,1},{4,6},{5,7},{6,4},{7,5},{8,10},{9,11},{10,... | collective-permute-start | bytes 3840008 | tf_op jit(solution)/shard_map/ppermute | solution.py:422
  276.7 39.0 %collective-permute-start.45 = (bf16[512,1600]{0,1:T(8,128)(2,1)}, bf16[512,1600]{0,1:T(8,128)(2,1)}, u32[]{:S(2)}, u32[]{:S(2)}) collective-permute-start(bf16[512,1600]{0,1:T(8,128)(2,1)} %get-tuple-element.159), channel_id=1, source_target_pairs={{0,4},{1,5},{2,6},{3,7},{4,0},{5,1},{6,2},{7,3},{8,12},{9,13},{10,... | collective-permute-start | bytes 4915208 | tf_op jit(solution)/shard_map/ppermute | solution.py:422
  284.2 50.1 %collective-permute-start.49 = (bf16[2,200,1600]{2,1,0:T(8,128)(2,1)}, bf16[2,200,1600]{2,1,0:T(8,128)(2,1)}, u32[]{:S(2)}, u32[]{:S(2)}) collective-permute-start(bf16[2,200,1600]{2,1,0:T(8,128)(2,1)} %pad_maximum_fusion.10.refs_0_), channel_id=1, source_target_pairs={{0,8},{1,9},{2,10},{3,11},{4,12},{5,13},{6,14},{7,15},{8,0},{9,1},... | collective-permute-start | bytes 3840008 | tf_op jit(solution)/shard_map/ppermute | solution.py:422
  287.1 62.5 %collective-permute-start.70 = (bf16[2,200,1600]{2,1,0:T(8,128)(2,1)}, bf16[2,200,1600]{2,1,0:T(8,128)(2,1)S(1)}, u32[]{:S(2)}, u32[]{:S(2)}) collective-permute-start(bf16[2,200,1600]{2,1,0:T(8,128)(2,1)} %pad_maximum_fusion.10.refs_0_), channel_id=1, source_target_pairs={{0,4},{1,5},{2,6},{3,7},{4,0},{5,1},{6,2},{7,3},{8,12},{9,13},{10,... | collective-permute-start | bytes 3840008 | tf_op jit(solution)/shard_map/ppermute | solution.py:422
  293.9 34.2 %collective-permute-start.43 = (bf16[1,400,800]{2,1,0:T(8,128)(2,1)S(1)}, bf16[1,400,800]{2,1,0:T(8,128)(2,1)S(1)}, u32[]{:S(2)}, u32[]{:S(2)}) collective-permute-start(bf16[1,400,800]{2,1,0:T(8,128)(2,1)S(1)} %slice.306), channel_id=1, source_target_pairs={{0,16},{1,17},{2,18},{3,19},{4,20},{5,21},{6,22},{7,23},{8,24},{9,... | collective-permute-start | bytes 1920008 | tf_op jit(solution)/shard_map/ppermute | solution.py:422
  294.4 39.9 %collective-permute-start.48 = (bf16[2,416,768]{2,1,0:T(8,128)(2,1)}, bf16[2,416,768]{2,1,0:T(8,128)(2,1)}, u32[]{:S(2)}, u32[]{:S(2)}) collective-permute-start(bf16[2,416,768]{2,1,0:T(8,128)(2,1)} %pad_maximum_fusion.11), channel_id=1, source_target_pairs={{0,1},{1,0},{2,3},{3,2},{4,5},{5,4},{6,7},{7,6},{8,9},{9,8},{10,11... | collective-permute-start | bytes 3833864 | tf_op jit(solution)/shard_map/ppermute | solution.py:422
  339.5 35.6 %collective-permute-start.46 = (bf16[1,400,800]{2,1,0:T(8,128)(2,1)}, bf16[1,400,800]{2,1,0:T(8,128)(2,1)}, u32[]{:S(2)}, u32[]{:S(2)}) collective-permute-start(bf16[1,400,800]{2,1,0:T(8,128)(2,1)} %add_convert_fusion.9), channel_id=1, source_target_pairs={{0,16},{1,17},{2,18},{3,19},{4,20},{5,21},{6,22},{7,23},{8,24},{9,... | collective-permute-start | bytes 1920008 | tf_op jit(solution)/shard_map/ppermute | solution.py:422
  344.1 38.3 %collective-permute-start.51 = (bf16[2,128,1600]{1,2,0:T(8,128)(2,1)}, bf16[2,128,1600]{1,2,0:T(8,128)(2,1)}, u32[]{:S(2)}, u32[]{:S(2)}) collective-permute-start(bf16[2,128,1600]{1,2,0:T(8,128)(2,1)} %copy.67), channel_id=1, source_target_pairs={{0,8},{1,9},{2,10},{3,11},{4,12},{5,13},{6,14},{7,15},{8,0},{9,1},... | collective-permute-start | bytes 2457608 | tf_op jit(solution)/shard_map/ppermute | solution.py:422
  349.6 39.0 %collective-permute-start.52 = (bf16[2,200,1600]{2,1,0:T(8,128)(2,1)}, bf16[2,200,1600]{2,1,0:T(8,128)(2,1)S(1)}, u32[]{:S(2)}, u32[]{:S(2)}) collective-permute-start(bf16[2,200,1600]{2,1,0:T(8,128)(2,1)} %collective-permute-done.49.refs_1_), channel_id=1, source_target_pairs={{0,4},{1,5},{2,6},{3,7},{4,0},{5,1},{6,2},{7,3},{8,12},{9,13},{10,... | collective-permute-start | bytes 3840008 | tf_op jit(solution)/shard_map/ppermute | solution.py:422
  351.9 52.5 %collective-permute-start.56 = (bf16[1,416,768]{2,1,0:T(8,128)(2,1)S(1)}, bf16[1,416,768]{2,1,0:T(8,128)(2,1)S(1)}, u32[]{:S(2)}, u32[]{:S(2)}) collective-permute-start(bf16[1,416,768]{2,1,0:T(8,128)(2,1)S(1)} %fusion.48), channel_id=1, source_target_pairs={{0,16},{1,17},{2,18},{3,19},{4,20},{5,21},{6,22},{7,23},{8,24},{9,... | collective-permute-start | bytes 1916936 | tf_op jit(solution)/shard_map/ppermute | solution.py:422
  361.8 40.2 %collective-permute-start.54 = (bf16[2,56,1600]{2,1,0:T(8,128)(2,1)S(1)}, bf16[2,56,1600]{2,1,0:T(8,128)(2,1)S(1)}, u32[]{:S(2)}, u32[]{:S(2)}) collective-permute-start(bf16[2,56,1600]{2,1,0:T(8,128)(2,1)S(1)} %slice.313), channel_id=1, source_target_pairs={{0,8},{1,9},{2,10},{3,11},{4,12},{5,13},{6,14},{7,15},{8,0},{9,1},... | collective-permute-start | bytes 1075208 | tf_op jit(solution)/shard_map/ppermute | solution.py:422
  376.6 55.5 %collective-permute-start.57 = (bf16[2,400,800]{2,1,0:T(8,128)(2,1)S(1)}, bf16[2,400,800]{2,1,0:T(8,128)(2,1)S(1)}, u32[]{:S(2)}, u32[]{:S(2)}) collective-permute-start(bf16[2,400,800]{2,1,0:T(8,128)(2,1)S(1)} %pad_maximum_fusion.8.refs_0_), channel_id=1, source_target_pairs={{0,8},{1,9},{2,10},{3,11},{4,12},{5,13},{6,14},{7,15},{8,0},{9,1},... | collective-permute-start | bytes 3840008 | tf_op jit(solution)/shard_map/ppermute | solution.py:422
  382.4 53.9 %collective-permute-start.59 = (bf16[2,400,800]{2,1,0:T(8,128)(2,1)S(1)}, bf16[2,400,800]{2,1,0:T(8,128)(2,1)S(1)}, u32[]{:S(2)}, u32[]{:S(2)}) collective-permute-start(bf16[2,400,800]{2,1,0:T(8,128)(2,1)S(1)} %pad_maximum_fusion.8.refs_0_), channel_id=1, source_target_pairs={{0,4},{1,5},{2,6},{3,7},{4,0},{5,1},{6,2},{7,3},{8,12},{9,13},{10,... | collective-permute-start | bytes 3840008 | tf_op jit(solution)/shard_map/ppermute | solution.py:422
  388.6 47.9 %collective-permute-start.53 = (bf16[512,1600]{0,1:T(8,128)(2,1)S(1)}, bf16[512,1600]{0,1:T(8,128)(2,1)S(1)}, u32[]{:S(2)}, u32[]{:S(2)}) collective-permute-start(bf16[512,1600]{0,1:T(8,128)(2,1)S(1)} %convolution_convert_fusion.5), channel_id=1, source_target_pairs={{0,1},{1,0},{2,3},{3,2},{4,5},{5,4},{6,7},{7,6},{8,9},{9,8},{10,11... | collective-permute-start | bytes 4915208 | tf_op jit(solution)/shard_map/ppermute | solution.py:422
  404.5 64.2 %collective-permute-start.60 = (bf16[2,416,768]{2,1,0:T(8,128)(2,1)S(1)}, bf16[2,416,768]{2,1,0:T(8,128)(2,1)S(1)}, u32[]{:S(2)}, u32[]{:S(2)}) collective-permute-start(bf16[2,416,768]{2,1,0:T(8,128)(2,1)S(1)} %pad_maximum_fusion.12.refs_0_), channel_id=1, source_target_pairs={{0,4},{1,5},{2,6},{3,7},{4,0},{5,1},{6,2},{7,3},{8,12},{9,13},{10,... | collective-permute-start | bytes 3833864 | tf_op jit(solution)/shard_map/ppermute | solution.py:422
  432.0 41.8 %collective-permute-start.63 = (bf16[2,416,768]{2,1,0:T(8,128)(2,1)S(1)}, bf16[2,416,768]{2,1,0:T(8,128)(2,1)S(1)}, u32[]{:S(2)}, u32[]{:S(2)}) collective-permute-start(bf16[2,416,768]{2,1,0:T(8,128)(2,1)S(1)} %pad_maximum_fusion.12.refs_0_), channel_id=1, source_target_pairs={{0,8},{1,9},{2,10},{3,11},{4,12},{5,13},{6,14},{7,15},{8,0},{9,1},... | collective-permute-start | bytes 3833864 | tf_op jit(solution)/shard_map/ppermute | solution.py:422
  432.1 32.5 %collective-permute-start.58 = (bf16[1,56,1600]{2,1,0:T(8,128)(2,1)S(1)}, bf16[1,56,1600]{2,1,0:T(8,128)(2,1)S(1)}, u32[]{:S(2)}, u32[]{:S(2)}) collective-permute-start(bf16[1,56,1600]{2,1,0:T(8,128)(2,1)S(1)} %add_convert_fusion.16), channel_id=1, source_target_pairs={{0,16},{1,17},{2,18},{3,19},{4,20},{5,21},{6,22},{7,23},{8,24},{9,... | collective-permute-start | bytes 537608 | tf_op jit(solution)/shard_map/ppermute | solution.py:422
  436.3 37.5 %collective-permute-start.64 = (bf16[1,128,1600]{1,2,0:T(8,128)(2,1)S(1)}, bf16[1,128,1600]{1,2,0:T(8,128)(2,1)S(1)}, u32[]{:S(2)}, u32[]{:S(2)}) collective-permute-start(bf16[1,128,1600]{1,2,0:T(8,128)(2,1)S(1)} %slice.318), channel_id=1, source_target_pairs={{0,16},{1,17},{2,18},{3,19},{4,20},{5,21},{6,22},{7,23},{8,24},{9,... | collective-permute-start | bytes 1228808 | tf_op jit(solution)/shard_map/ppermute | solution.py:422
  436.6 39.5 %collective-permute-start.65 = (bf16[2,400,800]{2,1,0:T(8,128)(2,1)S(1)}, bf16[2,400,800]{2,1,0:T(8,128)(2,1)S(1)}, u32[]{:S(2)}, u32[]{:S(2)}) collective-permute-start(bf16[2,400,800]{2,1,0:T(8,128)(2,1)S(1)} %collective-permute-done.57.refs_1_), channel_id=1, source_target_pairs={{0,4},{1,5},{2,6},{3,7},{4,0},{5,1},{6,2},{7,3},{8,12},{9,13},{10,... | collective-permute-start | bytes 3840008 | tf_op jit(solution)/shard_map/ppermute | solution.py:422
  468.7 31.5 %collective-permute-start.61 = (bf16[128,1600]{0,1:T(8,128)(2,1)S(1)}, bf16[128,1600]{0,1:T(8,128)(2,1)S(1)}, u32[]{:S(2)}, u32[]{:S(2)}) collective-permute-start(bf16[128,1600]{0,1:T(8,128)(2,1)S(1)} %get-tuple-element.200), channel_id=1, source_target_pairs={{0,10},{1,11},{2,8},{3,9},{4,14},{5,15},{6,12},{7,13},{8,2},{9,3},... | collective-permute-start | bytes 1228808 | tf_op jit(solution)/shard_map/ppermute | solution.py:422
  476.1 48.9 %collective-permute-start.68 = (bf16[2,416,768]{2,1,0:T(8,128)(2,1)S(1)}, bf16[2,416,768]{2,1,0:T(8,128)(2,1)S(1)}, u32[]{:S(2)}, u32[]{:S(2)}) collective-permute-start(bf16[2,416,768]{2,1,0:T(8,128)(2,1)S(1)} %collective-permute-done.60.refs_1_), channel_id=1, source_target_pairs={{0,8},{1,9},{2,10},{3,11},{4,12},{5,13},{6,14},{7,15},{8,0},{9,1},... | collective-permute-start | bytes 3833864 | tf_op jit(solution)/shard_map/ppermute | solution.py:422
  481.9 33.7 %collective-permute-start.69 = (bf16[4,56,1600]{2,1,0:T(8,128)(2,1)S(1)}, bf16[4,56,1600]{2,1,0:T(8,128)(2,1)S(1)}, u32[]{:S(2)}, u32[]{:S(2)}) collective-permute-start(bf16[4,56,1600]{2,1,0:T(8,128)(2,1)S(1)} %pad_maximum_fusion.15.refs_0_), channel_id=1, source_target_pairs={{0,4},{1,5},{2,6},{3,7},{4,0},{5,1},{6,2},{7,3},{8,12},{9,13},{10,... | collective-permute-start | bytes 2150408 | tf_op jit(solution)/shard_map/ppermute | solution.py:422
  (104 other events, 1271.1 us)

commit v6 on v5

--- a/solution.py
+++ b/solution.py
@@ -56,7 +56,7 @@
 UNROLLED = 1024
 BUMP = 1
 SPLIT = ("down", "up", "qkv")
-TURNS = "mdmudmpudupmgduqpugqdqpuopqpgupoqp"
+TURNS = "mdmudmpudupmgduqpugqdqpuopqpgupqop"
 
 
 def for_tiles(one, length, tile, key_axis):

time: 539 us -> 565 us (1.048)
  waiting for transfers between devices: 223 us -> 244 us
    ppermute x71, waiting for transfers between devices: 220 us -> 241 us  [swap(): return lax.ppermute(value, AXES, pairs)]
    unnamed x151 -> x165, local copies, waits for them, and re-layouts: 21.1 us -> 23.6 us
  transfers between devices with their start and end apart: 73 -> 73, of which waited for: 31 -> 29; matrix products, arithmetic and copies ran while one was open for 28% -> 27% of each run, Pallas kernels for 9% -> 9%
where the time goes in v6:
time: 565 us; the launch traced here: 558 us
  waiting for transfers between devices  244 us (43%)
  starting transfers between devices  73.3 us (13%)
  other arithmetic  63.9 us (11%)
  matrix products  62.3 us (11%)
  Pallas kernels  56.6 us (10%)
  local copies, waits for them, and re-layouts  54.7 us (10%)
    ppermute x71, waiting for transfers between devices, swap(): return lax.ppermute(value, AXES, pairs)  241 us
    ppermute x71, starting transfers between devices, swap(): return lax.ppermute(value, AXES, pairs)  64.1 us
    pallas_call x9, Pallas kernels, rearrange(): pl.pallas_call(kernel, out_shape=tuple((jax.ShapeDtypeStruct(o.shape, o.d...  35.4 us
    dot_general x6, matrix products, by_transpose(): lax.dot_general(left, right, (((1,), (1,)), ((), ())), preferred_element_...  25.6 us
    unnamed x165, local copies, waits for them, and re-layouts  23.6 us
    dot_general x7, matrix products, dot(): return jnp.dot(left, right, preferred_element_type=F32)  21.2 us
    convert_element_type x14, other arithmetic, add_low(): return (left.astype(F32) + right.astype(F32)).astype(BF16)  21.1 us
    dot_general x4, matrix products, over_rows(): lax.dot_general(left, right, (((0,), (0,)), ((), ())), preferred_element_...  15.6 us
  transfers between devices with their start and end apart: 73, of which 29 were waited for; matrix products, arithmetic and copies ran while one was open for 27% of the time, Pallas kernels for 9%

profile of v6, /device:TPU:0, one launch (start us, length us, event | category | flops | bytes accessed | tf_op | source)
XLA Modules:
  0.0 557.7 jit_solution(15510919433250374819)
XLA Ops:
  17.1 7.6 %collective-permute-done = bf16[128,1600]{0,1:T(8,128)(2,1)S(1)} collective-permute-done((bf16[128,1600]{0,1:T(8,128)(2,1)}, bf16[128,1600]{0,1:T(8,128)(2,1)S(1)}, u32[]{:S(2)}, u32[]{:S(2)}) %collective-permute-start) | collective-permute-done | bytes 409632 | tf_op jit(solution)/shard_map/ppermute | solution.py:422
  28.4 6.6 %collective-permute-done.1 = bf16[128,1600]{0,1:T(8,128)(2,1)} collective-permute-done((bf16[128,1600]{0,1:T(8,128)(2,1)S(1)}, bf16[128,1600]{0,1:T(8,128)(2,1)}, u32[]{:S(2)}, u32[]{:S(2)}) %collective-permute-start.1) | collective-permute-done | bytes 409632 | tf_op jit(solution)/shard_map/ppermute | solution.py:422
  35.8 4.6 shard_map.242
  42.0 14.2 %collective-permute-done.3 = bf16[128,1600]{0,1:T(8,128)(2,1)} collective-permute-done((bf16[128,1600]{0,1:T(8,128)(2,1)}, bf16[128,1600]{0,1:T(8,128)(2,1)}, u32[]{:S(2)}, u32[]{:S(2)}) %collective-permute-start.3) | collective-permute-done | bytes 409632 | tf_op jit(solution)/shard_map/ppermute | solution.py:422
  68.4 5.5 add_convert_fusion.3.qkv_ref
  73.9 6.7 %shard_map.240 = (bf16[8,128,256]{2,1,0:T(8,128)(2,1)S(1)}, f32[1024,128]{1,0:T(8,128)S(1)}) custom-call(s32[16]{0:T(128)S(1)} %select_reduce_fusion.place_ref, s32[16]{0:T(128)S(1)} %copy-done.16, bf16[1024,768]{1,0:T(8,128)(2,1)S(1)} %add_convert_fusion.3.qkv_ref), custom_call_target="tpu_custom_call" | custom-call | flops 1073741824 | bytes 2621440 | tf_op jit(solution)/shard_map/pallas_call | solution.py:200
  83.4 4.6 all-to-all-start
  93.4 5.3 shard_map.241
  105.3 5.0 fusion.85
  112.0 5.4 collective-permute-done.24
  125.8 8.8 %collective-permute-done.16 = bf16[128,1600]{0,1:T(8,128)(2,1)S(1)} collective-permute-done((bf16[128,1600]{0,1:T(8,128)(2,1)S(1)}, bf16[128,1600]{0,1:T(8,128)(2,1)S(1)}, u32[]{:S(2)}, u32[]{:S(2)}) %collective-permute-start.16) | collective-permute-done | bytes 409632 | tf_op jit(solution)/shard_map/ppermute | solution.py:422
  147.5 5.3 convert_reduce_fusion.2
  162.3 6.0 %convolution_convert_fusion.1 = bf16[1600,800]{1,0:T(8,128)(2,1)S(1)} fusion(bf16[1024,1600]{0,1:T(8,128)(2,1)} %copy-done.55, bf16[1024,800]{0,1:T(8,128)(2,1)} %copy-done.62), kind=kOutput, calls=%fused_computation.18 | convolution fusion | flops 2622720000 | bytes 7475200 | tf_op jit(solution)/shard_map/dot_general | solution.py:45
  180.9 12.9 %collective-permute-done.34 = bf16[2,200,1600]{2,1,0:T(8,128)(2,1)} collective-permute-done((bf16[2,200,1600]{2,1,0:T(8,128)(2,1)}, bf16[2,200,1600]{2,1,0:T(8,128)(2,1)}, u32[]{:S(2)}, u32[]{:S(2)}) %collective-permute-start.34) | collective-permute-done | bytes 1280032 | tf_op jit(solution)/shard_map/ppermute | solution.py:422
  210.6 4.7 all-to-all-start.1
  223.2 4.9 collective-permute-done.32
  251.0 10.7 %shard_map.246 = bf16[1024,768]{1,0:T(8,128)(2,1)S(1)} custom-call(s32[16]{0:T(128)S(1)} %select_reduce_fusion.place_ref, s32[16]{0:T(128)S(1)} %copy-done.16, bf16[1024,768]{1,0:T(8,128)(2,1)S(1)} %copy-done.18, f32[1024,128]{1,0:T(8,128)S(1)} %copy-done.20, bf16[8,128,256]{2,1,0:T(8,128)(2,1)S(1)} %all-to-all-done.1.grad_ref), custom_call_target="tpu_custom_call" | custom-call | flops 2684354560 | bytes 4194304 | tf_op jit(solution)/shard_map/pallas_call | solution.py:220
  265.2 9.1 %fusion.16 = (bf16[1600]{0:T(1024)(128)(2,1)S(1)}, bf16[512,1600]{0,1:T(8,128)(2,1)}, f32[512,1600]{0,1:T(8,128)}) fusion(f32[1024,1600]{0,1:T(8,128)} %fusion.2, f32[512,1600]{0,1:T(8,128)} %fusion.46, bf16[1600,768]{1,0:T(8,128)(2,1)S(1)} %shard_map.239, bf16[1024,768]{1,0:T(8,128)(2,1)} %copy-done.1), kind=kOutput, calls=%fused_computation.29 | convolution fusion | flops 1262385664 | bytes 17992832 | tf_op jit(solution)/shard_map/dot_general | solution.py:49
  296.3 15.7 %collective-permute-done.45 = bf16[512,1600]{0,1:T(8,128)(2,1)} collective-permute-done((bf16[512,1600]{0,1:T(8,128)(2,1)}, bf16[512,1600]{0,1:T(8,128)(2,1)}, u32[]{:S(2)}, u32[]{:S(2)}) %collective-permute-start.45) | collective-permute-done | bytes 1638432 | tf_op jit(solution)/shard_map/ppermute | solution.py:422
  312.0 13.7 %collective-permute-done.43 = bf16[1,400,800]{2,1,0:T(8,128)(2,1)S(1)} collective-permute-done((bf16[1,400,800]{2,1,0:T(8,128)(2,1)S(1)}, bf16[1,400,800]{2,1,0:T(8,128)(2,1)S(1)}, u32[]{:S(2)}, u32[]{:S(2)}) %collective-permute-start.43) | collective-permute-done | bytes 640032 | tf_op jit(solution)/shard_map/ppermute | solution.py:422
  358.4 13.6 %collective-permute-done.46 = bf16[1,400,800]{2,1,0:T(8,128)(2,1)} collective-permute-done((bf16[1,400,800]{2,1,0:T(8,128)(2,1)}, bf16[1,400,800]{2,1,0:T(8,128)(2,1)}, u32[]{:S(2)}, u32[]{:S(2)}) %collective-permute-start.46) | collective-permute-done | bytes 640032 | tf_op jit(solution)/shard_map/ppermute | solution.py:422
  373.4 6.7 %collective-permute-done.51 = bf16[2,128,1600]{1,2,0:T(8,128)(2,1)} collective-permute-done((bf16[2,128,1600]{1,2,0:T(8,128)(2,1)}, bf16[2,128,1600]{1,2,0:T(8,128)(2,1)}, u32[]{:S(2)}, u32[]{:S(2)}) %collective-permute-start.51) | collective-permute-done | bytes 819232 | tf_op jit(solution)/shard_map/ppermute | solution.py:422
  384.4 15.6 %collective-permute-done.55 = bf16[2,56,1600]{2,1,0:T(8,128)(2,1)S(1)} collective-permute-done((bf16[2,56,1600]{2,1,0:T(8,128)(2,1)S(1)}, bf16[2,56,1600]{2,1,0:T(8,128)(2,1)S(1)}, u32[]{:S(2)}, u32[]{:S(2)}) %collective-permute-start.55) | collective-permute-done | bytes 358432 | tf_op jit(solution)/shard_map/ppermute | solution.py:422
  402.9 26.5 %collective-permute-done.58.refs_1_ = bf16[2,400,800]{2,1,0:T(8,128)(2,1)} collective-permute-done((bf16[2,400,800]{2,1,0:T(8,128)(2,1)S(1)}, bf16[2,400,800]{2,1,0:T(8,128)(2,1)}, u32[]{:S(2)}, u32[]{:S(2)}) %collective-permute-start.58) | collective-permute-done | bytes 1280032 | tf_op jit(solution)/shard_map/ppermute | solution.py:422
  434.7 12.6 %collective-permute-done.59 = bf16[1,56,1600]{2,1,0:T(8,128)(2,1)S(1)} collective-permute-done((bf16[1,56,1600]{2,1,0:T(8,128)(2,1)S(1)}, bf16[1,56,1600]{2,1,0:T(8,128)(2,1)S(1)}, u32[]{:S(2)}, u32[]{:S(2)}) %collective-permute-start.59) | collective-permute-done | bytes 179232 | tf_op jit(solution)/shard_map/ppermute | solution.py:422
  450.4 5.0 collective-permute-done.63
  456.6 13.8 %collective-permute-done.70.refs_2_ = bf16[2,200,1600]{2,1,0:T(8,128)(2,1)S(1)} collective-permute-done((bf16[2,200,1600]{2,1,0:T(8,128)(2,1)}, bf16[2,200,1600]{2,1,0:T(8,128)(2,1)S(1)}, u32[]{:S(2)}, u32[]{:S(2)}) %collective-permute-start.70) | collective-permute-done | bytes 1280032 | tf_op jit(solution)/shard_map/ppermute | solution.py:422
  478.5 18.6 %collective-permute-done.64.refs_3_ = bf16[2,400,800]{2,1,0:T(8,128)(2,1)} collective-permute-done((bf16[2,400,800]{2,1,0:T(8,128)(2,1)}, bf16[2,400,800]{2,1,0:T(8,128)(2,1)}, u32[]{:S(2)}, u32[]{:S(2)}) %collective-permute-start.64) | collective-permute-done | bytes 1280032 | tf_op jit(solution)/shard_map/ppermute | solution.py:422
  501.7 23.5 %collective-permute-done.65 = bf16[128,1600]{0,1:T(8,128)(2,1)} collective-permute-done((bf16[128,1600]{0,1:T(8,128)(2,1)}, bf16[128,1600]{0,1:T(8,128)(2,1)}, u32[]{:S(2)}, u32[]{:S(2)}) %collective-permute-start.65) | collective-permute-done | bytes 409632 | tf_op jit(solution)/shard_map/ppermute | solution.py:422
  526.8 6.0 %shard_map.247 = (f32[400,4800]{1,0:T(8,128)}, f32[16,768]{1,0:T(8,128)S(1)}) custom-call(s32[8]{0:T(128)S(1)} %stack.244.numbers, bf16[2,416,768]{2,1,0:T(8,128)(2,1)S(1)} %pad_maximum_fusion.12.refs_0_, bf16[2,416,768]{2,1,0:T(8,128)(2,1)} %collective-permute-done.56.refs_1_, bf16[2,416,768]{2,1,0:T(8,128)(2,1)S(1)} %copy-done.12, ...), custom_call_target="tpu_custom_call" | custom-call | bytes 12840960 | tf_op jit(solution)/shard_map/pallas_call | solution.py:238
  536.2 7.7 %shard_map.249 = f32[400,6400]{1,0:T(8,128)} custom-call(s32[8]{0:T(128)S(1)} %stack.245.numbers, bf16[2,400,800]{2,1,0:T(8,128)(2,1)S(1)} %pad_maximum_fusion.8.refs_0_, bf16[2,400,800]{2,1,0:T(8,128)(2,1)} %collective-permute-done.58.refs_1_, bf16[2,400,800]{2,1,0:T(8,128)(2,1)S(1)} %copy-done.6, bf16[2,400,800]{2,1,0:T(8,128)(2,1)} %collective-permute-done.64.refs_3_), custom_call_target="tpu_custom_call" | custom-call | bytes 15360000 | tf_op jit(solution)/shard_map/pallas_call | solution.py:238
  543.9 7.0 %shard_map.250 = f32[1600,1600]{1,0:T(8,128)} custom-call(s32[8]{0:T(128)S(1)} %stack.245.numbers, bf16[2,200,1600]{2,1,0:T(8,128)(2,1)} %pad_maximum_fusion.10.refs_0_, bf16[2,200,1600]{2,1,0:T(8,128)(2,1)} %collective-permute-done.49.refs_1_, bf16[2,200,1600]{2,1,0:T(8,128)(2,1)S(1)} %copy-done.10, bf16[2,200,1600]{2,1,0:T(8,128)(2,1)S(1)} %copy-done.8), custom_call_target="tpu_custom_call" | custom-call | bytes 15360000 | tf_op jit(solution)/shard_map/pallas_call | solution.py:238
  (460 shorter events, 241.1 us)
Async XLA Ops:
  16.5 45.5 %collective-permute-start.13 = (bf16[400,1600]{1,0:T(8,128)(2,1)}, bf16[400,1600]{1,0:T(8,128)(2,1)}, u32[]{:S(2)}, u32[]{:S(2)}) collective-permute-start(bf16[400,1600]{1,0:T(8,128)(2,1)} %param.21), channel_id=1, source_target_pairs={{0,2},{1,3},{2,0},{3,1},{4,6},{5,7},{6,4},{7,5},{8,10},{9,11},{10,... | collective-permute-start | bytes 3840008 | tf_op jit(solution)/shard_map/ppermute | solution.py:422
  65.5 34.5 %collective-permute-start.15 = (bf16[2,400,800]{2,1,0:T(8,128)(2,1)}, bf16[2,400,800]{2,1,0:T(8,128)(2,1)}, u32[]{:S(2)}, u32[]{:S(2)}) collective-permute-start(bf16[2,400,800]{2,1,0:T(8,128)(2,1)} %get-tuple-element.124), channel_id=1, source_target_pairs={{0,2},{1,3},{2,0},{3,1},{4,6},{5,7},{6,4},{7,5},{8,10},{9,11},{10,... | collective-permute-start | bytes 3840008 | tf_op jit(solution)/shard_map/ppermute | solution.py:422
  92.0 31.9 %collective-permute-start.26 = (bf16[128,1600]{0,1:T(8,128)(2,1)}, bf16[128,1600]{0,1:T(8,128)(2,1)}, u32[]{:S(2)}, u32[]{:S(2)}) collective-permute-start(bf16[128,1600]{0,1:T(8,128)(2,1)} %bitcast.165), channel_id=1, source_target_pairs={{0,10},{1,11},{2,8},{3,9},{4,14},{5,15},{6,12},{7,13},{8,2},{9,3},... | collective-permute-start | bytes 1228808 | tf_op jit(solution)/shard_map/ppermute | solution.py:422
  162.0 31.8 %collective-permute-start.34 = (bf16[2,200,1600]{2,1,0:T(8,128)(2,1)}, bf16[2,200,1600]{2,1,0:T(8,128)(2,1)}, u32[]{:S(2)}, u32[]{:S(2)}) collective-permute-start(bf16[2,200,1600]{2,1,0:T(8,128)(2,1)} %pad_maximum_fusion.9), channel_id=1, source_target_pairs={{0,4},{1,5},{2,6},{3,7},{4,0},{5,1},{6,2},{7,3},{8,12},{9,13},{10,... | collective-permute-start | bytes 3840008 | tf_op jit(solution)/shard_map/ppermute | solution.py:422
  179.4 48.7 %collective-permute-start.32 = (bf16[2,400,800]{2,1,0:T(8,128)(2,1)}, bf16[2,400,800]{2,1,0:T(8,128)(2,1)}, u32[]{:S(2)}, u32[]{:S(2)}) collective-permute-start(bf16[2,400,800]{2,1,0:T(8,128)(2,1)} %pad_maximum_fusion.5), channel_id=1, source_target_pairs={{0,2},{1,3},{2,0},{3,1},{4,6},{5,7},{6,4},{7,5},{8,10},{9,11},{10,... | collective-permute-start | bytes 3840008 | tf_op jit(solution)/shard_map/ppermute | solution.py:422
  196.3 38.4 %collective-permute-start.38 = (bf16[1,200,1600]{2,1,0:T(8,128)(2,1)}, bf16[1,200,1600]{2,1,0:T(8,128)(2,1)}, u32[]{:S(2)}, u32[]{:S(2)}) collective-permute-start(bf16[1,200,1600]{2,1,0:T(8,128)(2,1)} %slice.302), channel_id=1, source_target_pairs={{0,16},{1,17},{2,18},{3,19},{4,20},{5,21},{6,22},{7,23},{8,24},{9,... | collective-permute-start | bytes 1920008 | tf_op jit(solution)/shard_map/ppermute | solution.py:422
  210.6 37.9 %all-to-all-start.1 = ((bf16[8,128,256]{2,1,0:T(8,128)(2,1)}), bf16[8,128,256]{2,1,0:T(8,128)(2,1)S(1)}, u32[]{:S(2)}, u32[]{:S(2)}) async-start(bf16[8,128,256]{2,1,0:T(8,128)(2,1)} %shard_map.245), calls=%async_computation.1 | async-start | bytes 1048576 | tf_op jit(solution)/shard_map/all_to_all | solution.py:531
  236.9 42.5 %collective-permute-start.40 = (bf16[1,200,1600]{2,1,0:T(8,128)(2,1)}, bf16[1,200,1600]{2,1,0:T(8,128)(2,1)}, u32[]{:S(2)}, u32[]{:S(2)}) collective-permute-start(bf16[1,200,1600]{2,1,0:T(8,128)(2,1)} %add_convert_fusion.10), channel_id=1, source_target_pairs={{0,16},{1,17},{2,18},{3,19},{4,20},{5,21},{6,22},{7,23},{8,24},{9,... | collective-permute-start | bytes 1920008 | tf_op jit(solution)/shard_map/ppermute | solution.py:422
  242.5 46.4 %collective-permute-start.39 = (bf16[2,400,800]{2,1,0:T(8,128)(2,1)}, bf16[2,400,800]{2,1,0:T(8,128)(2,1)}, u32[]{:S(2)}, u32[]{:S(2)}) collective-permute-start(bf16[2,400,800]{2,1,0:T(8,128)(2,1)} %pad_maximum_fusion.7), channel_id=1, source_target_pairs={{0,4},{1,5},{2,6},{3,7},{4,0},{5,1},{6,2},{7,3},{8,12},{9,13},{10,... | collective-permute-start | bytes 3840008 | tf_op jit(solution)/shard_map/ppermute | solution.py:422
  247.1 44.2 %collective-permute-start.44 = (bf16[400,1600]{1,0:T(8,128)(2,1)}, bf16[400,1600]{1,0:T(8,128)(2,1)}, u32[]{:S(2)}, u32[]{:S(2)}) collective-permute-start(bf16[400,1600]{1,0:T(8,128)(2,1)} %fusion.18), channel_id=1, source_target_pairs={{0,2},{1,3},{2,0},{3,1},{4,6},{5,7},{6,4},{7,5},{8,10},{9,11},{10,... | collective-permute-start | bytes 3840008 | tf_op jit(solution)/shard_map/ppermute | solution.py:422
  274.4 37.7 %collective-permute-start.45 = (bf16[512,1600]{0,1:T(8,128)(2,1)}, bf16[512,1600]{0,1:T(8,128)(2,1)}, u32[]{:S(2)}, u32[]{:S(2)}) collective-permute-start(bf16[512,1600]{0,1:T(8,128)(2,1)} %get-tuple-element.159), channel_id=1, source_target_pairs={{0,4},{1,5},{2,6},{3,7},{4,0},{5,1},{6,2},{7,3},{8,12},{9,13},{10,... | collective-permute-start | bytes 4915208 | tf_op jit(solution)/shard_map/ppermute | solution.py:422
  281.9 49.5 %collective-permute-start.49 = (bf16[2,200,1600]{2,1,0:T(8,128)(2,1)}, bf16[2,200,1600]{2,1,0:T(8,128)(2,1)}, u32[]{:S(2)}, u32[]{:S(2)}) collective-permute-start(bf16[2,200,1600]{2,1,0:T(8,128)(2,1)} %pad_maximum_fusion.10.refs_0_), channel_id=1, source_target_pairs={{0,8},{1,9},{2,10},{3,11},{4,12},{5,13},{6,14},{7,15},{8,0},{9,1},... | collective-permute-start | bytes 3840008 | tf_op jit(solution)/shard_map/ppermute | solution.py:422
  291.2 34.5 %collective-permute-start.43 = (bf16[1,400,800]{2,1,0:T(8,128)(2,1)S(1)}, bf16[1,400,800]{2,1,0:T(8,128)(2,1)S(1)}, u32[]{:S(2)}, u32[]{:S(2)}) collective-permute-start(bf16[1,400,800]{2,1,0:T(8,128)(2,1)S(1)} %slice.306), channel_id=1, source_target_pairs={{0,16},{1,17},{2,18},{3,19},{4,20},{5,21},{6,22},{7,23},{8,24},{9,... | collective-permute-start | bytes 1920008 | tf_op jit(solution)/shard_map/ppermute | solution.py:422
  291.3 40.1 %collective-permute-start.48 = (bf16[2,416,768]{2,1,0:T(8,128)(2,1)}, bf16[2,416,768]{2,1,0:T(8,128)(2,1)}, u32[]{:S(2)}, u32[]{:S(2)}) collective-permute-start(bf16[2,416,768]{2,1,0:T(8,128)(2,1)} %pad_maximum_fusion.11), channel_id=1, source_target_pairs={{0,1},{1,0},{2,3},{3,2},{4,5},{5,4},{6,7},{7,6},{8,9},{9,8},{10,11... | collective-permute-start | bytes 3833864 | tf_op jit(solution)/shard_map/ppermute | solution.py:422
  336.4 35.6 %collective-permute-start.46 = (bf16[1,400,800]{2,1,0:T(8,128)(2,1)}, bf16[1,400,800]{2,1,0:T(8,128)(2,1)}, u32[]{:S(2)}, u32[]{:S(2)}) collective-permute-start(bf16[1,400,800]{2,1,0:T(8,128)(2,1)} %add_convert_fusion.9), channel_id=1, source_target_pairs={{0,16},{1,17},{2,18},{3,19},{4,20},{5,21},{6,22},{7,23},{8,24},{9,... | collective-permute-start | bytes 1920008 | tf_op jit(solution)/shard_map/ppermute | solution.py:422
  341.1 39.1 %collective-permute-start.51 = (bf16[2,128,1600]{1,2,0:T(8,128)(2,1)}, bf16[2,128,1600]{1,2,0:T(8,128)(2,1)}, u32[]{:S(2)}, u32[]{:S(2)}) collective-permute-start(bf16[2,128,1600]{1,2,0:T(8,128)(2,1)} %copy.67), channel_id=1, source_target_pairs={{0,8},{1,9},{2,10},{3,11},{4,12},{5,13},{6,14},{7,15},{8,0},{9,1},... | collective-permute-start | bytes 2457608 | tf_op jit(solution)/shard_map/ppermute | solution.py:422
  343.7 40.6 %collective-permute-start.52 = (bf16[2,200,1600]{2,1,0:T(8,128)(2,1)}, bf16[2,200,1600]{2,1,0:T(8,128)(2,1)S(1)}, u32[]{:S(2)}, u32[]{:S(2)}) collective-permute-start(bf16[2,200,1600]{2,1,0:T(8,128)(2,1)} %collective-permute-done.49.refs_1_), channel_id=1, source_target_pairs={{0,4},{1,5},{2,6},{3,7},{4,0},{5,1},{6,2},{7,3},{8,12},{9,13},{10,... | collective-permute-start | bytes 3840008 | tf_op jit(solution)/shard_map/ppermute | solution.py:422
  349.2 51.1 %collective-permute-start.54 = (bf16[1,416,768]{2,1,0:T(8,128)(2,1)S(1)}, bf16[1,416,768]{2,1,0:T(8,128)(2,1)S(1)}, u32[]{:S(2)}, u32[]{:S(2)}) collective-permute-start(bf16[1,416,768]{2,1,0:T(8,128)(2,1)S(1)} %fusion.48), channel_id=1, source_target_pairs={{0,16},{1,17},{2,18},{3,19},{4,20},{5,21},{6,22},{7,23},{8,24},{9,... | collective-permute-start | bytes 1916936 | tf_op jit(solution)/shard_map/ppermute | solution.py:422
  355.9 44.1 %collective-permute-start.55 = (bf16[2,56,1600]{2,1,0:T(8,128)(2,1)S(1)}, bf16[2,56,1600]{2,1,0:T(8,128)(2,1)S(1)}, u32[]{:S(2)}, u32[]{:S(2)}) collective-permute-start(bf16[2,56,1600]{2,1,0:T(8,128)(2,1)S(1)} %slice.313), channel_id=1, source_target_pairs={{0,8},{1,9},{2,10},{3,11},{4,12},{5,13},{6,14},{7,15},{8,0},{9,1},... | collective-permute-start | bytes 1075208 | tf_op jit(solution)/shard_map/ppermute | solution.py:422
  373.3 56.1 %collective-permute-start.58 = (bf16[2,400,800]{2,1,0:T(8,128)(2,1)S(1)}, bf16[2,400,800]{2,1,0:T(8,128)(2,1)}, u32[]{:S(2)}, u32[]{:S(2)}) collective-permute-start(bf16[2,400,800]{2,1,0:T(8,128)(2,1)S(1)} %pad_maximum_fusion.8.refs_0_), channel_id=1, source_target_pairs={{0,8},{1,9},{2,10},{3,11},{4,12},{5,13},{6,14},{7,15},{8,0},{9,1},... | collective-permute-start | bytes 3840008 | tf_op jit(solution)/shard_map/ppermute | solution.py:422
  380.1 52.3 %collective-permute-start.60 = (bf16[2,400,800]{2,1,0:T(8,128)(2,1)S(1)}, bf16[2,400,800]{2,1,0:T(8,128)(2,1)S(1)}, u32[]{:S(2)}, u32[]{:S(2)}) collective-permute-start(bf16[2,400,800]{2,1,0:T(8,128)(2,1)S(1)} %pad_maximum_fusion.8.refs_0_), channel_id=1, source_target_pairs={{0,4},{1,5},{2,6},{3,7},{4,0},{5,1},{6,2},{7,3},{8,12},{9,13},{10,... | collective-permute-start | bytes 3840008 | tf_op jit(solution)/shard_map/ppermute | solution.py:422
  384.3 49.9 %collective-permute-start.53 = (bf16[512,1600]{0,1:T(8,128)(2,1)S(1)}, bf16[512,1600]{0,1:T(8,128)(2,1)S(1)}, u32[]{:S(2)}, u32[]{:S(2)}) collective-permute-start(bf16[512,1600]{0,1:T(8,128)(2,1)S(1)} %convolution_convert_fusion.5), channel_id=1, source_target_pairs={{0,1},{1,0},{2,3},{3,2},{4,5},{5,4},{6,7},{7,6},{8,9},{9,8},{10,11... | collective-permute-start | bytes 4915208 | tf_op jit(solution)/shard_map/ppermute | solution.py:422
  400.4 49.5 %collective-permute-start.56 = (bf16[2,416,768]{2,1,0:T(8,128)(2,1)S(1)}, bf16[2,416,768]{2,1,0:T(8,128)(2,1)}, u32[]{:S(2)}, u32[]{:S(2)}) collective-permute-start(bf16[2,416,768]{2,1,0:T(8,128)(2,1)S(1)} %pad_maximum_fusion.12.refs_0_), channel_id=1, source_target_pairs={{0,4},{1,5},{2,6},{3,7},{4,0},{5,1},{6,2},{7,3},{8,12},{9,13},{10,... | collective-permute-start | bytes 3833864 | tf_op jit(solution)/shard_map/ppermute | solution.py:422
  429.4 41.0 %collective-permute-start.70 = (bf16[2,200,1600]{2,1,0:T(8,128)(2,1)}, bf16[2,200,1600]{2,1,0:T(8,128)(2,1)S(1)}, u32[]{:S(2)}, u32[]{:S(2)}) collective-permute-start(bf16[2,200,1600]{2,1,0:T(8,128)(2,1)} %pad_maximum_fusion.10.refs_0_), channel_id=1, source_target_pairs={{0,4},{1,5},{2,6},{3,7},{4,0},{5,1},{6,2},{7,3},{8,12},{9,13},{10,... | collective-permute-start | bytes 3840008 | tf_op jit(solution)/shard_map/ppermute | solution.py:422
  434.2 43.2 %collective-permute-start.67 = (bf16[2,416,768]{2,1,0:T(8,128)(2,1)S(1)}, bf16[2,416,768]{2,1,0:T(8,128)(2,1)S(1)}, u32[]{:S(2)}, u32[]{:S(2)}) collective-permute-start(bf16[2,416,768]{2,1,0:T(8,128)(2,1)S(1)} %pad_maximum_fusion.12.refs_0_), channel_id=1, source_target_pairs={{0,8},{1,9},{2,10},{3,11},{4,12},{5,13},{6,14},{7,15},{8,0},{9,1},... | collective-permute-start | bytes 3833864 | tf_op jit(solution)/shard_map/ppermute | solution.py:422
  447.3 49.9 %collective-permute-start.64 = (bf16[2,400,800]{2,1,0:T(8,128)(2,1)}, bf16[2,400,800]{2,1,0:T(8,128)(2,1)}, u32[]{:S(2)}, u32[]{:S(2)}) collective-permute-start(bf16[2,400,800]{2,1,0:T(8,128)(2,1)} %collective-permute-done.58.refs_1_), channel_id=1, source_target_pairs={{0,4},{1,5},{2,6},{3,7},{4,0},{5,1},{6,2},{7,3},{8,12},{9,13},{10,... | collective-permute-start | bytes 3840008 | tf_op jit(solution)/shard_map/ppermute | solution.py:422
  449.9 48.7 %collective-permute-start.62 = (bf16[2,56,1600]{2,1,0:T(8,128)(2,1)}, bf16[2,56,1600]{2,1,0:T(8,128)(2,1)}, u32[]{:S(2)}, u32[]{:S(2)}) collective-permute-start(bf16[2,56,1600]{2,1,0:T(8,128)(2,1)} %pad_maximum_fusion.16), channel_id=1, source_target_pairs={{0,8},{1,9},{2,10},{3,11},{4,12},{5,13},{6,14},{7,15},{8,0},{9,1},... | collective-permute-start | bytes 1075208 | tf_op jit(solution)/shard_map/ppermute | solution.py:422
  455.4 71.4 %collective-permute-start.68 = (bf16[2,416,768]{2,1,0:T(8,128)(2,1)}, bf16[2,416,768]{2,1,0:T(8,128)(2,1)}, u32[]{:S(2)}, u32[]{:S(2)}) collective-permute-start(bf16[2,416,768]{2,1,0:T(8,128)(2,1)} %collective-permute-done.56.refs_1_), channel_id=1, source_target_pairs={{0,8},{1,9},{2,10},{3,11},{4,12},{5,13},{6,14},{7,15},{8,0},{9,1},... | collective-permute-start | bytes 3833864 | tf_op jit(solution)/shard_map/ppermute | solution.py:422
  471.5 53.8 %collective-permute-start.61 = (bf16[128,1600]{0,1:T(8,128)(2,1)}, bf16[128,1600]{0,1:T(8,128)(2,1)}, u32[]{:S(2)}, u32[]{:S(2)}) collective-permute-start(bf16[128,1600]{0,1:T(8,128)(2,1)} %get-tuple-element.202), channel_id=1, source_target_pairs={{0,10},{1,11},{2,8},{3,9},{4,14},{5,15},{6,12},{7,13},{8,2},{9,3},... | collective-permute-start | bytes 1228808 | tf_op jit(solution)/shard_map/ppermute | solution.py:422
  478.5 46.8 %collective-permute-start.65 = (bf16[128,1600]{0,1:T(8,128)(2,1)}, bf16[128,1600]{0,1:T(8,128)(2,1)}, u32[]{:S(2)}, u32[]{:S(2)}) collective-permute-start(bf16[128,1600]{0,1:T(8,128)(2,1)} %get-tuple-element.203), channel_id=1, source_target_pairs={{0,8},{1,9},{2,10},{3,11},{4,12},{5,13},{6,14},{7,15},{8,0},{9,1},... | collective-permute-start | bytes 1228808 | tf_op jit(solution)/shard_map/ppermute | solution.py:422
  497.2 55.0 %collective-permute-start.66 = (bf16[128,1600]{0,1:T(8,128)(2,1)}, bf16[128,1600]{0,1:T(8,128)(2,1)}, u32[]{:S(2)}, u32[]{:S(2)}) collective-permute-start(bf16[128,1600]{0,1:T(8,128)(2,1)} %get-tuple-element.204), channel_id=1, source_target_pairs={{0,2},{1,3},{2,0},{3,1},{4,6},{5,7},{6,4},{7,5},{8,10},{9,11},{10,... | collective-permute-start | bytes 1228808 | tf_op jit(solution)/shard_map/ppermute | solution.py:422
  499.9 54.7 %collective-permute-start.69 = (bf16[4,56,1600]{2,1,0:T(8,128)(2,1)S(1)}, bf16[4,56,1600]{2,1,0:T(8,128)(2,1)}, u32[]{:S(2)}, u32[]{:S(2)}) collective-permute-start(bf16[4,56,1600]{2,1,0:T(8,128)(2,1)S(1)} %pad_maximum_fusion.15.refs_0_), channel_id=1, source_target_pairs={{0,4},{1,5},{2,6},{3,7},{4,0},{5,1},{6,2},{7,3},{8,12},{9,13},{10,... | collective-permute-start | bytes 2150408 | tf_op jit(solution)/shard_map/ppermute | solution.py:422
  (111 other events, 1451.2 us)
